TPU v7x, 256 devices: a whole 4x4x8 slice. The times are simulated.
256 devices in a mesh: sens: 32 (over x_lo, z, core), hour: 8 (over x_hi, y).
Axes of the slice: x: 4 (x_hi: 2, x_lo: 2; x = x_hi * 2 + x_lo), y: 4, z: 8, core: 2. Of those that a mesh axis runs over, the one named last changes fastest.
Arguments:
- windows: bfloat16 [8, 256, 3, 4096], P('hour', 'sens'), may hold values from -6 to 6
- pair_first: int32 [2048], P('sens'), may hold values from 0 to 7
- pair_second: int32 [2048], P('sens'), may hold values from 0 to 23
- owners: int32 [2048, 1], P('sens'), may hold values from 0 to 31; in each aligned block of 64 rows (0 to 63, 64 to 127, ...) at most 4 rows name the same one
Outputs:
- stacks: float32 [4096, 9216], P('sens', 'hour')
Inputs may be any that keep to these rules, and one draw needn't show every extreme that they name: `owners`: within the 64 pairs of one block no owner appears more than 4 times, and some owner appears exactly 4 times.
All inputs are finite; a program needn't handle non-finite values.
Results may differ from a plain program's by a relative error of at most 0.004.
Values may be sent and summed in bfloat16 or wider, within the bound.
No kernel may reach another device: no remote copies, remote signals or barrier semaphores. Data moves between devices by JAX's collectives and lax.ppermute only.
A program may use at most 128 MiB of HBM per device.

v0:
```python
import jax
import jax.numpy as jnp
from jax import lax
from jax.sharding import PartitionSpec as P

SAMPLES = 4096
PADDED = 8192
NB = 2048
LAGS = 1024
COMPS = 3


def from_behind(value, axis, steps):
    count = lax.axis_size(axis)
    pairs = [(source, (source + steps) % count) for source in range(count)]
    return lax.ppermute(value, axis, pairs)


def build_tables():
    times = jnp.arange(SAMPLES, dtype=jnp.int32)
    bins = jnp.arange(NB, dtype=jnp.int32) + 1
    phase = times[:, None] * bins[None, :] % PADDED
    angle = phase.astype(jnp.float32) * (2.0 * jnp.pi / PADDED)
    fwd = jnp.concatenate([jnp.cos(angle), -jnp.sin(angle)], axis=1).astype(jnp.bfloat16)
    shifts = jnp.arange(LAGS, dtype=jnp.int32) - LAGS // 2
    phase_back = bins[:, None] * shifts[None, :] % PADDED
    angle_back = phase_back.astype(jnp.float32) * (2.0 * jnp.pi / PADDED)
    inv = jnp.concatenate([jnp.cos(angle_back), -jnp.sin(angle_back)], axis=0).astype(jnp.bfloat16)
    return (fwd, inv)


def whiten(rows, fwd):
    spec = jnp.dot(rows, fwd, preferred_element_type=jnp.float32)
    real_part = spec[:, :NB]
    imag_part = spec[:, NB:]
    power = real_part * real_part + imag_part * imag_part
    level = jnp.mean(power, axis=1, keepdims=True)
    scale = 1.0 / jnp.sqrt(power + 0.1 * level + 1e-06)
    return jnp.concatenate([real_part * scale, imag_part * scale], axis=1).astype(jnp.bfloat16)


def shards(windows, pair_first, pair_second, owners):
    hours_here = windows.shape[0]
    sensors_here = windows.shape[1]
    pairs_here = pair_first.shape[0]
    width = COMPS * COMPS * LAGS
    fwd, inv = build_tables()
    white = whiten(windows.reshape(hours_here * sensors_here * COMPS, SAMPLES), fwd)
    white = white.reshape(hours_here, sensors_here, COMPS, 2 * NB)
    nearer = from_behind(white, "sens", -1)
    farther = from_behind(nearer, "sens", -1)
    candidates = jnp.concatenate([white, nearer, farther], axis=1)
    first_spec = jnp.take(white, pair_first, axis=1)
    second_spec = jnp.take(candidates, pair_second, axis=1)
    ar = first_spec[..., :NB].astype(jnp.float32)
    ai = first_spec[..., NB:].astype(jnp.float32)
    br = second_spec[..., :NB].astype(jnp.float32)
    bi = second_spec[..., NB:].astype(jnp.float32)
    real_part = (
        ar[:, :, :, None, :] * br[:, :, None, :, :] + ai[:, :, :, None, :] * bi[:, :, None, :, :]
    )
    imag_part = (
        ar[:, :, :, None, :] * bi[:, :, None, :, :] - ai[:, :, :, None, :] * br[:, :, None, :, :]
    )
    cross = jnp.concatenate([real_part, imag_part], axis=-1).astype(jnp.bfloat16)
    lagged = jnp.dot(
        cross.reshape(hours_here * pairs_here * COMPS * COMPS, 2 * NB),
        inv,
        preferred_element_type=jnp.float32,
    )
    summed = jnp.sum(lagged.reshape(hours_here, pairs_here, width), axis=0)
    owner_count = lax.axis_size("sens")
    capacity = max(2, 2 * pairs_here // owner_count)
    owner = owners[:, 0]
    same = owner[:, None] == owner[None, :]
    order = jnp.arange(pairs_here, dtype=jnp.int32)
    earlier = order[None, :] < order[:, None]
    slot = jnp.sum((same & earlier).astype(jnp.int32), axis=1)
    target = owner * capacity + slot
    outgoing = jnp.zeros((owner_count * capacity, width), jnp.float32).at[target].set(summed)
    received = lax.all_to_all(outgoing, "sens", split_axis=0, concat_axis=0, tiled=True)
    stacked = lax.psum_scatter(received, "hour", scatter_dimension=1, tiled=True)
    all_hours = hours_here * lax.axis_size("hour")
    return stacked / jnp.sqrt(jnp.float32(NB * all_hours))


def solution(mesh):
    placed = (P("hour", "sens", None, None), P("sens"), P("sens"), P("sens", None))
    return jax.shard_map(
        shards, mesh=mesh, in_specs=placed, out_specs=P("sens", "hour"), check_vma=False
    )
```

profile of v0, /device:TPU:1, one launch (start us, length us, event | category | flops | bytes accessed | tf_op | source)
XLA Modules:
  0.0 471.8 jit_solution(7177942356168153208)
XLA Ops:
  6.5 136.1 %cosine_convert_fusion = (bf16[4096,2048]{1,0:T(8,128)(2,1)}, bf16[4096,2048]{1,0:T(8,128)(2,1)}) fusion(s32[2048]{0:T(1024)S(1)} %iota_add_fusion), kind=kLoop, calls=%fused_computation.14 | loop fusion | flops 142606336 | bytes 33562624 | tf_op jit(solution)/shard_map/convert.14
  142.7 0.2 copy.6
  142.8 0.2 reshape.132
  143.0 12.1 %fusion.20 = f32[24,4096]{1,0:T(8,128)S(1)} fusion(bf16[24,4096]{1,0:T(8,128)(2,1)S(1)} %reshape.132, bf16[4096,2048]{1,0:T(8,128)(2,1)} %get-tuple-element.16, bf16[4096,2048]{1,0:T(8,128)(2,1)} %get-tuple-element.15), kind=kOutput, calls=%fused_computation.37 | convolution fusion | flops 872415232 | bytes 34144256 | tf_op jit(solution)/shard_map/dot_general | solution.py:33
  155.1 0.1 fusion.33
  155.3 0.1 multiply_convert_fusion
  155.4 0.1 concatenate.34
  155.5 0.1 concatenate.35
  155.6 0.1 constant_dynamic-update-slice_fusion
  155.7 3.5 collective-permute-start
  159.2 35.9 %cosine_convert_fusion.1 = (bf16[2048,1024]{1,0:T(8,128)(2,1)}, bf16[2048,1024]{1,0:T(8,128)(2,1)}) fusion(s32[1024]{0:T(1024)S(1)} %iota_add_fusion.1, s32[2048]{0:T(1024)S(1)} %iota_add_fusion), kind=kLoop, calls=%fused_computation.31 | loop fusion | flops 35651584 | bytes 8400896 | tf_op jit(solution)/shard_map/convert.4
  195.1 0.2 convert_reduce_fusion
  195.3 2.4 gather_fusion
  197.7 2.4 bitcast_select_fusion.1
  200.1 4.5 collective-permute-start.1
  204.6 1.3 collective-permute-done.1
  205.9 0.5 maximum_bitcast_fusion
  206.5 2.4 gather_fusion.1
  208.8 1.1 bitcast_select_fusion
  209.9 3.2 fusion.27
  213.1 5.2 %add_convert_fusion = (bf16[64,3,3,2048]{3,2,1,0:T(4,128)(2,1)}, bf16[64,3,3,2048]{3,2,1,0:T(4,128)(2,1)S(1)}) fusion(f32[64,3,2048]{2,1,0:T(4,128)S(1)} %get-tuple-element.10, f32[64,3,2048]{2,1,0:T(4,128)S(1)} %get-tuple-element.17, f32[64,3,2048]{2,1,0:T(4,128)S(1)} %get-tuple-element.9, f32[64,3,2048]{2,1,0:T(4,128)S(1)} %get-tuple-element.18), kind=kLoop, calls=%fused_computation.33 | loop fusion | flops 9437184 | bytes 11010048 | tf_op jit(solution)/shard_map/convert.9
  218.3 6.7 %add.113 = bf16[576,2048]{1,0:T(8,128)(2,1)} reshape(bf16[64,3,3,2048]{3,2,1,0:T(4,128)(2,1)} %get-tuple-element.5) | data formatting | bytes 4718592 | tf_op jit(solution)/shard_map/add | solution.py:60
  225.0 4.2 sub.17
  229.2 9.8 %fusion.13 = f32[576,1024]{1,0:T(8,128)S(1)} fusion(bf16[2048,1024]{1,0:T(8,128)(2,1)} %get-tuple-element.14, bf16[2048,1024]{1,0:T(8,128)(2,1)} %get-tuple-element.13, bf16[576,2048]{1,0:T(8,128)(2,1)} %sub.17, bf16[576,2048]{1,0:T(8,128)(2,1)} %add.113), kind=kOutput, calls=%fused_computation.26 | convolution fusion | flops 4858052608 | bytes 15466496 | tf_op jit(solution)/shard_map/dot_general | solution.py:66
  239.1 2.2 reshape.161
  241.2 5.4 %scatter_custom_fusion = f32[128,9216]{1,0:T(8,128)} fusion(s32[64]{0:T(128)S(1)} %fusion.30, f32[64,9216]{1,0:T(8,128)} %reshape.161, f32[]{:T(128)} %constant.41.clone.1), kind=kCustom, calls=%fused_computation.38 | custom fusion | bytes 4719104 | tf_op jit(solution)/shard_map/scatter | solution.py:80
  246.6 5.6 %all_to_all.8 = f32[32,4,9216]{2,1,0:T(4,128)} reshape(f32[128,9216]{1,0:T(8,128)} %scatter_custom_fusion) | data formatting | bytes 9437184 | tf_op jit(solution)/shard_map/all_to_all | solution.py:81
  252.2 115.1 %all_to_all.12 = f32[32,4,9216]{2,1,0:T(4,128)} all-to-all(f32[32,4,9216]{2,1,0:T(4,128)} %all_to_all.8), channel_id=1, replica_groups=mesh['sens'=32,'hour'=8] {'sens'}, dimensions={0} | all-to-all | bytes 9437184 | tf_op jit(solution)/shard_map/all_to_all | solution.py:81
  367.3 5.7 %all_to_all.10 = f32[128,9216]{1,0:T(8,128)} reshape(f32[32,4,9216]{2,1,0:T(4,128)} %all_to_all.12) | data formatting | bytes 9437184 | tf_op jit(solution)/shard_map/all_to_all | solution.py:81
  373.0 0.0 reduce-scatter.2.cloned.1.call-update
  373.1 89.9 %reduce-scatter.2.cloned.1.call-done = f32[128,1152]{1,0:T(8,128)} async-done(((f32[128,9216]{1,0:T(8,128)}), f32[128,1152]{1,0:T(8,128)}) %reduce-scatter.2.cloned.1.call-update) | async-done | bytes 589840 | tf_op jit(solution)/shard_map/reduce_scatter | solution.py:82
  463.0 1.9 broadcast_multiply_fusion
  (21 shorter events, 0.1 us)
Async XLA Ops:
  6.5 456.5 %reduce-scatter.2.cloned.1.call-start = ((), (), s32[]{:S(2)}) async-start(), calls=%async_computation.2 | async-start | bytes 5308416 | tf_op jit(solution)/shard_map/reduce_scatter | solution.py:82
  6.5 136.1 %copy-start = (bf16[1,8,3,4096]{3,1,2,0:T(8,128)(2,1)S(1)}, bf16[1,8,3,4096]{3,1,2,0:T(8,128)(2,1)}, u32[]{:S(2)}) copy-start(bf16[1,8,3,4096]{3,1,2,0:T(8,128)(2,1)} %param.4) | copy-start | bytes 589828
  143.0 16.1 %copy-start.1 = (s32[64]{0:T(128)S(1)}, s32[64]{0:T(128)}, u32[]{:S(2)}) copy-start(s32[64]{0:T(128)} %param.5) | copy-start | bytes 772
  143.0 16.2 %copy-start.3 = (s32[64]{0:T(128)S(1)}, s32[64]{0:T(128)}, u32[]{:S(2)}) copy-start(s32[64]{0:T(128)} %param.6) | copy-start | bytes 772
  155.1 40.0 %copy-start.2 = (s32[64,1]{0,1:T(1,128)S(1)}, s32[64,1]{0,1:T(1,128)}, u32[]{:S(2)}) copy-start(s32[64,1]{0,1:T(1,128)} %param.7) | copy-start | bytes 772
  155.7 44.4 %collective-permute-start = (bf16[1,8,3,4096]{3,2,1,0:T(4,128)(2,1)S(1)}, bf16[1,8,3,4096]{3,2,1,0:T(4,128)(2,1)S(1)}, u32[]{:S(2)}, u32[]{:S(2)}) collective-permute-start(bf16[1,8,3,4096]{3,2,1,0:T(4,128)(2,1)S(1)} %constant_dynamic-update-slice_fusion), channel_id=1, source_target_pairs={{0,248},{8,0},{16,8},{24,16},{32,24},{40,32},{48,40},{56,48},{64,5... | collective-permute-start | bytes 589832 | tf_op jit(solution)/shard_map/ppermute | solution.py:16
  200.1 5.8 %collective-permute-start.1 = (bf16[1,8,3,4096]{3,2,1,0:T(4,128)(2,1)S(1)}, bf16[1,8,3,4096]{3,2,1,0:T(4,128)(2,1)S(1)}, u32[]{:S(2)}, u32[]{:S(2)}) collective-permute-start(bf16[1,8,3,4096]{3,2,1,0:T(4,128)(2,1)S(1)} %collective-permute-done), channel_id=1, source_target_pairs={{0,248},{8,0},{16,8},{24,16},{32,24},{40,32},{48,40},{56,48},{64,5... | collective-permute-start | bytes 589832 | tf_op jit(solution)/shard_map/ppermute | solution.py:16
Sparse Core Ops, SparseCore 0:
  373.2 89.7 reduce-scatter.1
where the time goes:
time: 472 us
  other arithmetic  187 us (40%)
  blocking collectives  115 us (24%)
  waiting for transfers between devices  91.3 us (19%)
  local copies, waits for them, and re-layouts  35.1 us (7%)
  matrix products  21.9 us (5%)
  between operations  13.6 us (3%)
  starting transfers between devices  7.99 us (2%)
    another operation x4, other arithmetic  177 us
    all_to_all x1, blocking collectives, shards(): lax.all_to_all(outgoing, 'sens', split_axis=0, concat_axis=0, tiled=True)  115 us
    reduce_scatter x1, waiting for transfers between devices, shards(): lax.psum_scatter(received, 'hour', scatter_dimension=1, tiled=True)  89.9 us
    dot_general x1, matrix products, whiten(): spec = jnp.dot(rows, fwd, preferred_element_type=jnp.float32)  12.1 us
    all_to_all x2, local copies, waits for them, and re-layouts, shards(): lax.all_to_all(outgoing, 'sens', split_axis=0, concat_axis=0, tiled=True)  11.3 us
    dot_general x1, matrix products, shards(): jnp.dot(cross.reshape(hours_here * pairs_here * COMPS * COMPS, 2 * NB), i...  9.83 us
  transfers between devices with their start and end apart: 3, of which 2 were waited for; matrix products, arithmetic and copies ran while one was open for 9% of the time, Pallas kernels for 0%

commit v1 on v0

v1 whole, which is shorter than its diff:
```python
import jax
import jax.numpy as jnp
import ml_dtypes
import numpy as np
from jax import lax
from jax.experimental import pallas as pl
from jax.experimental.pallas import tpu as pltpu
from jax.sharding import PartitionSpec as P

SAMPLES = 4096
PADDED = 8192
NB = 2048
LAGS = 1024
COMPS = 3
SENSORS = 8
PAIRS = 64
CAP = 4
CHUNKS = 8
SPAN = SAMPLES // CHUNKS
RES = 2 * CHUNKS
BINS = NB // RES
ROWS = COMPS * SENSORS
SLAB = 32
MIB = 1 << 20


def tables():
    k = np.arange(1, RES + 1)
    t2 = np.arange(SPAN)
    q = np.arange(BINS)
    angle = 2 * np.pi * ((k[:, None] * t2[None, :]) % PADDED) / PADDED
    twiddle = np.stack([np.cos(angle), -np.sin(angle)]).astype(np.float32)
    period = PADDED // RES
    angle = 2 * np.pi * ((t2[:, None] * q[None, :]) % period) / period
    cos, sin = np.cos(angle), np.sin(angle)
    exact = np.block([[cos, -sin], [sin, cos]])
    high = exact.astype(ml_dtypes.bfloat16)
    common = np.stack([high, (exact - high.astype(np.float64)).astype(ml_dtypes.bfloat16)])
    bins = (k[:, None] + RES * q[None, :]).reshape(-1)
    shifts = np.arange(LAGS) - LAGS // 2
    angle = 2 * np.pi * ((bins[:, None] * shifts[None, :]) % PADDED) / PADDED
    inverse = np.concatenate([np.cos(angle), -np.sin(angle)]).astype(ml_dtypes.bfloat16)
    return twiddle, common, inverse


def forward(rows, twiddle_ref, common_ref, parts_ref, store):
    chunks = [rows[:, SPAN * i : SPAN * (i + 1)].astype(jnp.float32) for i in range(CHUNKS)]

    def combine(weights):
        total = None
        for weight, chunk in zip(weights, chunks):
            weight = float(weight)
            if abs(weight) < 1e-9:
                continue
            term = chunk if abs(weight - 1) < 1e-9 else -chunk if abs(weight + 1) < 1e-9 else chunk * weight
            total = term if total is None else total + term
        return total

    for k in range(0, CHUNKS + 1):
        angle = 2 * np.pi * ((k * np.arange(CHUNKS)) % RES) / RES
        real_part = combine(np.cos(angle))
        imag_part = combine(-np.sin(angle))
        both = ((RES, 1.0),) if k == 0 else ((CHUNKS, 1.0),) if k == CHUNKS else ((k, 1.0), (RES - k, -1.0))
        for residue, sign in both:
            tr = twiddle_ref[0, residue - 1 : residue, :]
            ti = twiddle_ref[1, residue - 1 : residue, :]
            if imag_part is None:
                yr, yi = real_part * tr, real_part * ti
            elif sign > 0:
                yr, yi = real_part * tr - imag_part * ti, real_part * ti + imag_part * tr
            else:
                yr, yi = real_part * tr + imag_part * ti, real_part * ti - imag_part * tr
            at = pl.ds((residue - 1) * ROWS, ROWS)
            parts_ref[at, :SPAN] = yr
            parts_ref[at, SPAN:] = yi
    both = parts_ref[...]
    high = both.astype(jnp.bfloat16)
    low = (both - high.astype(jnp.float32)).astype(jnp.bfloat16)
    spec = jnp.dot(high, common_ref[0], preferred_element_type=jnp.float32)
    spec = spec + jnp.dot(low, common_ref[0], preferred_element_type=jnp.float32)
    spec = spec + jnp.dot(high, common_ref[1], preferred_element_type=jnp.float32)
    real_part, imag_part = spec[:, :BINS], spec[:, BINS:]
    power = real_part * real_part + imag_part * imag_part
    total = power[:ROWS]
    for k in range(1, RES):
        total = total + power[k * ROWS : (k + 1) * ROWS]
    level = jnp.sum(total, axis=1, keepdims=True) * (1.0 / NB)
    floor = 0.1 * level + 1e-06
    for k in range(RES):
        at = slice(k * ROWS, (k + 1) * ROWS)
        scale = lax.rsqrt(power[at] + floor)
        store(k, jnp.concatenate([real_part[at] * scale, imag_part[at] * scale], axis=1))


def padded(value):
    return jnp.concatenate([value, jnp.zeros((SLAB - ROWS, value.shape[1]), value.dtype)], axis=0).astype(jnp.bfloat16)


def whiten_kernel(rows_ref, twiddle_ref, common_ref, white_ref, parts_ref):
    def store(k, value):
        white_ref[k] = padded(value)

    forward(rows_ref[...], twiddle_ref, common_ref, parts_ref, store)


def pairs_kernel(white_ref, nearer_ref, farther_ref, pick_ref, twiddle_ref, common_ref, inverse_ref, out_ref,
                 parts_ref, all_ref, cross_ref, table_ref, sem):
    load = pltpu.make_async_copy(inverse_ref, table_ref, sem)
    load.start()
    for block, rows_ref in ((1, nearer_ref), (2, farther_ref)):
        def store(k, value, block=block):
            all_ref[k, pl.ds(block * SLAB, SLAB), :] = padded(value)

        forward(rows_ref[...], twiddle_ref, common_ref, parts_ref, store)
    for k in range(RES):
        all_ref[k, pl.ds(0, SLAB), :] = white_ref[k]
        all_ref[k, pl.ds(3 * SLAB, SLAB), :] = jnp.zeros((SLAB, 2 * BINS), jnp.bfloat16)

    def cross(k, carry):
        picked = jnp.dot(pick_ref[...], all_ref[k], preferred_element_type=jnp.float32)
        at_re = pl.ds(pl.multiple_of(k * BINS, BINS), BINS)
        at_im = pl.ds(pl.multiple_of(NB + k * BINS, BINS), BINS)
        for c in range(COMPS):
            first = picked[c * PAIRS : (c + 1) * PAIRS]
            ar, ai = first[:, :BINS], first[:, BINS:]
            for e in range(COMPS):
                second = picked[(COMPS + e) * PAIRS : (COMPS + e + 1) * PAIRS]
                br, bi = second[:, :BINS], second[:, BINS:]
                at = pl.ds((c * COMPS + e) * PAIRS, PAIRS)
                cross_ref[at, at_re] = (ar * br + ai * bi).astype(jnp.bfloat16)
                cross_ref[at, at_im] = (ar * bi - ai * br).astype(jnp.bfloat16)
        return carry

    lax.fori_loop(0, RES, cross, 0)
    load.wait()
    width = 256
    tiles = COMPS * COMPS * LAGS // 128 // out_ref.shape[0]
    for n in range(LAGS // width):
        lagged = jnp.dot(cross_ref[...], table_ref[:, n * width : (n + 1) * width], preferred_element_type=jnp.float32)
        lagged = lagged.astype(jnp.bfloat16)
        for i in range(COMPS * COMPS):
            for half in range(width // 128):
                flat = i * (LAGS // 128) + n * (width // 128) + half
                out_ref[flat // tiles, :, (flat % tiles) * 128 : (flat % tiles + 1) * 128] = lagged[
                    i * PAIRS : (i + 1) * PAIRS, half * 128 : (half + 1) * 128]


def collect_kernel(parts_ref, place_ref, out_ref):
    total = parts_ref[0].astype(jnp.float32)
    for h in range(1, parts_ref.shape[0]):
        total = total + parts_ref[h].astype(jnp.float32)
    total = (total * (1.0 / 128.0)).astype(jnp.bfloat16)
    out_ref[...] = jnp.dot(place_ref[...], total, preferred_element_type=jnp.float32).astype(jnp.bfloat16)


def from_behind(value, axis, steps):
    count = lax.axis_size(axis)
    return lax.ppermute(value, axis, [(source, (source + steps) % count) for source in range(count)])


def shards(windows, pair_first, pair_second, owners):
    twiddle, common, inverse = (jnp.asarray(t) for t in tables())
    hours = lax.axis_size("hour")
    share = COMPS * COMPS * LAGS // hours
    bf16 = jnp.bfloat16
    rows = windows[0].transpose(1, 0, 2).reshape(ROWS, SAMPLES)
    nearer = from_behind(rows, "sens", -1)
    farther = from_behind(rows, "sens", -2)

    comps = jnp.arange(COMPS, dtype=jnp.int32)[:, None] * SENSORS
    pick_first = (comps + pair_first[None, :]).reshape(-1)
    pick_second = (comps + (pair_second // SENSORS * SLAB + pair_second % SENSORS)[None, :]).reshape(-1)
    picks = jnp.concatenate([pick_first, pick_second])
    pick = (picks[:, None] == jnp.arange(4 * SLAB, dtype=jnp.int32)[None, :]).astype(bf16)

    owner = owners[:, 0]
    order = jnp.arange(PAIRS, dtype=jnp.int32)
    same = (owner[:, None] == owner[None, :]) & (order[None, :] < order[:, None])
    target = owner * CAP + jnp.sum(same.astype(jnp.int32), axis=1)
    slots = lax.axis_size("sens") * CAP
    place = (jnp.arange(slots, dtype=jnp.int32)[:, None] == target[None, :]).astype(bf16)

    vmem = pl.BlockSpec(memory_space=pltpu.VMEM)
    white = pl.pallas_call(
        whiten_kernel,
        out_shape=jax.ShapeDtypeStruct((RES, SLAB, 2 * BINS), bf16),
        in_specs=[vmem] * 3,
        out_specs=vmem,
        scratch_shapes=[pltpu.VMEM((RES * ROWS, 2 * SPAN), jnp.float32)],
        compiler_params=pltpu.CompilerParams(vmem_limit_bytes=32 * MIB),
        cost_estimate=pl.CostEstimate(flops=3 * 10**8, bytes_accessed=10**6, transcendentals=0),
        name="whiten",
    )(rows, twiddle, common)
    partial = pl.pallas_call(
        pairs_kernel,
        out_shape=jax.ShapeDtypeStruct((hours, PAIRS, share), bf16),
        in_specs=[vmem] * 6 + [pl.BlockSpec(memory_space=pl.ANY)],
        out_specs=vmem,
        scratch_shapes=[
            pltpu.VMEM((RES * ROWS, 2 * SPAN), jnp.float32),
            pltpu.VMEM((RES, 4 * SLAB, 2 * BINS), bf16),
            pltpu.VMEM((COMPS * COMPS * PAIRS, 2 * NB), bf16),
            pltpu.VMEM((2 * NB, LAGS), bf16),
            pltpu.SemaphoreType.DMA,
        ],
        compiler_params=pltpu.CompilerParams(vmem_limit_bytes=48 * MIB),
        cost_estimate=pl.CostEstimate(flops=6 * 10**9, bytes_accessed=10**7, transcendentals=0),
        name="pairs",
    )(white, nearer, farther, pick, twiddle, common, inverse)
    received = lax.all_to_all(partial, "hour", split_axis=0, concat_axis=0, tiled=True)
    outgoing = pl.pallas_call(
        collect_kernel,
        out_shape=jax.ShapeDtypeStruct((slots, share), bf16),
        in_specs=[vmem] * 2,
        out_specs=vmem,
        compiler_params=pltpu.CompilerParams(vmem_limit_bytes=32 * MIB),
        cost_estimate=pl.CostEstimate(flops=2 * 10**7, bytes_accessed=2 * 10**6, transcendentals=0),
        name="collect",
    )(received, place)
    stacked = lax.all_to_all(outgoing, "sens", split_axis=0, concat_axis=0, tiled=True)
    return stacked.astype(jnp.float32)


def solution(mesh):
    placed = (P("hour", "sens", None, None), P("sens"), P("sens"), P("sens", None))
    return jax.shard_map(
        shards, mesh=mesh, in_specs=placed, out_specs=P("sens", "hour"), check_vma=False
    )
```

time: 472 us -> 69.7 us (0.15)
  other arithmetic: 187 us -> 1.79 us
  blocking collectives: 115 us -> 20 us
  waiting for transfers between devices: 91.3 us -> 14.6 us
  local copies, waits for them, and re-layouts: 35.1 us -> 4.1 us
  matrix products: 21.9 us -> 0 us
  Pallas kernels: 0 us -> 14.4 us
  between operations: 13.6 us -> 0.1 us
  starting transfers between devices: 7.99 us -> 14.4 us
    another operation x4 -> x0, other arithmetic: 177 us -> none
    all_to_all x1, blocking collectives: 115 us -> 20 us  [shards(): lax.all_to_all(outgoing, 'sens', split_axis=0, concat_axis=0, tiled=True)]
    reduce_scatter x1 -> x0, waiting for transfers between devices: 89.9 us -> none  [shards(): lax.psum_scatter(received, 'hour', scatter_dimension=1, tiled=True)]
    dot_general x2 -> x0, matrix products: 21.9 us -> none  [the longest x1 12.1 us: whiten(): spec = jnp.dot(rows, fwd, preferred_element_type=jnp.float32)]
    all_to_all x0 -> x1, waiting for transfers between devices: none -> 14.6 us  [shards(): lax.all_to_all(partial, 'hour', split_axis=0, concat_axis=0, tiled=True)]
    pallas_call x0 -> x3, Pallas kernels: none -> 14.4 us  [the longest x1 12.9 us: shards(): pl.pallas_call(pairs_kernel, out_shape=jax.ShapeDtypeStruct((hours, PAIRS...]
    all_to_all x2 -> x1, local copies, waits for them, and re-layouts: 11.3 us -> 0.08 us  [shards(): lax.all_to_all(outgoing, 'sens', split_axis=0, concat_axis=0, tiled=True)]
    add x1 -> x2, local copies, waits for them, and re-layouts: 6.72 us -> 0.16 us  [the longest x1 0.08 us: shards(): pick_first = (comps + pair_first[None, :]).reshape(-1)]
  transfers between devices with their start and end apart: 3 -> 3, of which waited for: 2 -> 1; matrix products, arithmetic and copies ran while one was open for 9% -> 3% of each run, Pallas kernels for 0% -> 2%
where the time goes in v1:
time: 69.7 us; the launch traced here: 69.4 us
  blocking collectives  20 us (29%)
  waiting for transfers between devices  14.6 us (21%)
  starting transfers between devices  14.4 us (21%)
  Pallas kernels  14.4 us (21%)
  local copies, waits for them, and re-layouts  4.1 us (6%)
  other arithmetic  1.79 us (3%)
    all_to_all x1, blocking collectives, shards(): lax.all_to_all(outgoing, 'sens', split_axis=0, concat_axis=0, tiled=True)  20 us
    all_to_all x1, waiting for transfers between devices, shards(): lax.all_to_all(partial, 'hour', split_axis=0, concat_axis=0, tiled=True)  14.6 us
    pallas_call x1, Pallas kernels, shards(): pl.pallas_call(pairs_kernel, out_shape=jax.ShapeDtypeStruct((hours, PAIRS...  12.9 us
    ppermute x2, starting transfers between devices, from_behind(): lax.ppermute(value, axis, [(source, (source + steps) % count) for source...  8.01 us
    all_to_all x1, starting transfers between devices, shards(): lax.all_to_all(partial, 'hour', split_axis=0, concat_axis=0, tiled=True)  6.38 us
    unnamed x12, local copies, waits for them, and re-layouts  3 us
  transfers between devices with their start and end apart: 3, of which 1 were waited for; matrix products, arithmetic and copies ran while one was open for 3% of the time, Pallas kernels for 2%

profile of v1, /device:TPU:1, one launch (start us, length us, event | category | flops | bytes accessed | tf_op | source)
XLA Modules:
  0.0 69.4 jit_solution(2082979052399695184)
XLA Ops:
  0.0 3.2 %collective-permute-start = (bf16[24,4096]{1,0:T(8,128)(2,1)}, bf16[24,4096]{1,0:T(8,128)(2,1)S(1)}, u32[]{:S(2)}, u32[]{:S(2)}) collective-permute-start(bf16[24,4096]{1,0:T(8,128)(2,1)} %bitcast.7), channel_id=1, source_target_pairs={{0,248},{8,0},{16,8},{24,16},{32,24},{40,32},{48,40},{56,48},{64,5... | collective-permute-start | bytes 589832 | tf_op jit(solution)/shard_map/ppermute | solution.py:158
  3.2 4.8 %collective-permute-start.1 = (bf16[24,4096]{1,0:T(8,128)(2,1)}, bf16[24,4096]{1,0:T(8,128)(2,1)S(1)}, u32[]{:S(2)}, u32[]{:S(2)}) collective-permute-start(bf16[24,4096]{1,0:T(8,128)(2,1)} %bitcast.8), channel_id=1, source_target_pairs={{0,240},{8,248},{16,0},{24,8},{32,16},{40,24},{48,32},{56,40},{64,... | collective-permute-start | bytes 589832 | tf_op jit(solution)/shard_map/ppermute | solution.py:158
  8.0 0.7 fusion.3
  8.7 0.7 %broadcast_add_fusion.1 = (s32[3,64]{1,0:T(4,128)S(1)}, s32[3,64]{1,0:T(4,128)S(1)}) fusion(s32[64]{0:T(128)} %param.8, s32[3]{0:T(128)S(1)} %iota_multiply_fusion, s32[64]{0:T(128)S(1)} %fusion.3), kind=kLoop, calls=%fused_computation.14 | loop fusion | flops 384 | bytes 2060 | tf_op jit(solution)/shard_map/add | solution.py:171
  9.4 0.1 add.54
  9.5 0.1 add.59
  9.6 0.0 copy-start
  9.6 1.2 %copy-done = bf16[2,1024,256]{2,1,0:T(8,128)(2,1)S(1)} copy-done((bf16[2,1024,256]{2,1,0:T(8,128)(2,1)S(1)}, bf16[2,1024,256]{2,1,0:T(8,128)(2,1)}, u32[]{:S(2)}) %copy-start) | copy-done | bytes 1048600
  10.8 0.0 copy-start.2
  10.8 0.9 %copy-done.2 = bf16[1,8,3,4096]{3,1,2,0:T(8,128)(2,1)S(1)} copy-done((bf16[1,8,3,4096]{3,1,2,0:T(8,128)(2,1)S(1)}, bf16[1,8,3,4096]{3,1,2,0:T(8,128)(2,1)}, u32[]{:S(2)}) %copy-start.2) | copy-done | bytes 196632
  11.7 0.0 copy-start.3
  11.7 0.8 %copy-done.3 = f32[2,16,512]{2,1,0:T(8,128)S(1)} copy-done((f32[2,16,512]{2,1,0:T(8,128)S(1)}, f32[2,16,512]{2,1,0:T(8,128)}, u32[]{:S(2)}) %copy-start.3) | copy-done | bytes 65560
  12.6 0.0 copy-start.1
  12.6 0.0 copy-start.4
  12.6 1.2 %whiten.1.white_ref = bf16[16,32,256]{2,1,0:T(8,128)(2,1)S(1)} custom-call(bf16[24,4096]{1,0:T(8,128)(2,1)S(1)} %bitcast.9, f32[2,16,512]{2,1,0:T(8,128)S(1)} %copy-done.3, bf16[2,1024,256]{2,1,0:T(8,128)(2,1)S(1)} %copy-done), custom_call_target="tpu_custom_call" | custom-call | flops 300000000 | bytes 1000000 | tf_op jit(solution)/shard_map/whiten/pallas_call | solution.py:184
  13.8 0.1 pad_add_fusion
  13.8 0.1 fusion.pick_ref
  14.0 0.0 collective-permute-done.nearer_ref
  14.0 0.0 collective-permute-done.1.farther_ref
  14.0 0.0 copy-done.1
  14.0 0.0 copy-done.4
  14.0 12.9 %pairs.1 = bf16[8,64,1152]{2,1,0:T(8,128)(2,1)} custom-call(bf16[16,32,256]{2,1,0:T(8,128)(2,1)S(1)} %whiten.1.white_ref, bf16[24,4096]{1,0:T(8,128)(2,1)S(1)} %collective-permute-done.nearer_ref, bf16[24,4096]{1,0:T(8,128)(2,1)S(1)} %collective-permute-done.1.farther_ref, bf16[384,128]{1,0:T(8,128)(2,1)S(1)} %fusion.pick_ref, f32[2,16,512]{2,1,0:T(8,128)S(1)} %copy-done.4, ...), custom_call_target="tpu_custom_call" | custom-call | flops 6000000000 | bytes 10000000 | tf_op jit(solution)/shard_map/pairs/pallas_call | solution.py:194
  26.9 0.0 copy-start.5
  26.9 6.4 %all-to-all-start = ((bf16[8,64,1152]{2,1,0:T(8,128)(2,1)}), bf16[8,64,1152]{2,1,0:T(8,128)(2,1)S(1)}, u32[]{:S(2)}, u32[]{:S(2)}) async-start(bf16[8,64,1152]{2,1,0:T(8,128)(2,1)} %pairs.1), calls=%async_computation | async-start | bytes 2359296 | tf_op jit(solution)/shard_map/all_to_all | solution.py:210
  33.3 0.0 copy-done.5
  33.3 0.2 convert_reduce_fusion
  33.5 14.6 %all-to-all-done.parts_ref = bf16[8,64,1152]{2,1,0:T(8,128)(2,1)S(1)} async-done(((bf16[8,64,1152]{2,1,0:T(8,128)(2,1)}), bf16[8,64,1152]{2,1,0:T(8,128)(2,1)S(1)}, u32[]{:S(2)}, u32[]{:S(2)}) %all-to-all-start) | async-done | bytes 1179680 | tf_op jit(solution)/shard_map/all_to_all | solution.py:210
  48.2 0.3 collect.1
  48.5 0.1 all_to_all.10
  48.6 20.0 %all_to_all.14 = bf16[32,4,1152]{2,1,0:T(4,128)(2,1)S(1)} all-to-all(bf16[32,4,1152]{2,1,0:T(4,128)(2,1)S(1)} %all_to_all.10), channel_id=1, replica_groups=mesh['sens'=32,'hour'=8] {'sens'}, dimensions={0} | all-to-all | bytes 589824 | tf_op jit(solution)/shard_map/all_to_all | solution.py:220
  68.6 0.9 %reshape.33 = f32[128,1152]{1,0:T(8,128)} reshape(bf16[32,4,1152]{2,1,0:T(4,128)(2,1)S(1)} %all_to_all.14) | data formatting | bytes 884736 | tf_op jit(solution)/shard_map/convert_element_type | solution.py:221
  (3 shorter events, 0.0 us)
Async XLA Ops:
  0.0 14.0 %collective-permute-start = (bf16[24,4096]{1,0:T(8,128)(2,1)}, bf16[24,4096]{1,0:T(8,128)(2,1)S(1)}, u32[]{:S(2)}, u32[]{:S(2)}) collective-permute-start(bf16[24,4096]{1,0:T(8,128)(2,1)} %bitcast.7), channel_id=1, source_target_pairs={{0,248},{8,0},{16,8},{24,16},{32,24},{40,32},{48,40},{56,48},{64,5... | collective-permute-start | bytes 589832 | tf_op jit(solution)/shard_map/ppermute | solution.py:158
  3.2 10.7 %collective-permute-start.1 = (bf16[24,4096]{1,0:T(8,128)(2,1)}, bf16[24,4096]{1,0:T(8,128)(2,1)S(1)}, u32[]{:S(2)}, u32[]{:S(2)}) collective-permute-start(bf16[24,4096]{1,0:T(8,128)(2,1)} %bitcast.8), channel_id=1, source_target_pairs={{0,240},{8,248},{16,0},{24,8},{32,16},{40,24},{48,32},{56,40},{64,... | collective-permute-start | bytes 589832 | tf_op jit(solution)/shard_map/ppermute | solution.py:158
  9.6 1.2 %copy-start = (bf16[2,1024,256]{2,1,0:T(8,128)(2,1)S(1)}, bf16[2,1024,256]{2,1,0:T(8,128)(2,1)}, u32[]{:S(2)}) copy-start(bf16[2,1024,256]{2,1,0:T(8,128)(2,1)} %constant.41.clone.common_ref) | copy-start | bytes 3145732
  10.8 0.9 %copy-start.2 = (bf16[1,8,3,4096]{3,1,2,0:T(8,128)(2,1)S(1)}, bf16[1,8,3,4096]{3,1,2,0:T(8,128)(2,1)}, u32[]{:S(2)}) copy-start(bf16[1,8,3,4096]{3,1,2,0:T(8,128)(2,1)} %param.7) | copy-start | bytes 589828
  11.7 0.8 %copy-start.3 = (f32[2,16,512]{2,1,0:T(8,128)S(1)}, f32[2,16,512]{2,1,0:T(8,128)}, u32[]{:S(2)}) copy-start(f32[2,16,512]{2,1,0:T(8,128)} %constant.40.clone.twiddle_ref) | copy-start | bytes 196612
  12.6 1.4 %copy-start.1 = (bf16[2,1024,256]{2,1,0:T(8,128)(2,1)S(1)}, bf16[2,1024,256]{2,1,0:T(8,128)(2,1)}, u32[]{:S(2)}) copy-start(bf16[2,1024,256]{2,1,0:T(8,128)(2,1)} %constant.41.clone.common_ref) | copy-start | bytes 3145732
  12.6 1.4 %copy-start.4 = (f32[2,16,512]{2,1,0:T(8,128)S(1)}, f32[2,16,512]{2,1,0:T(8,128)}, u32[]{:S(2)}) copy-start(f32[2,16,512]{2,1,0:T(8,128)} %constant.40.clone.twiddle_ref) | copy-start | bytes 196612
  26.9 6.4 %copy-start.5 = (s32[64,1]{0,1:T(1,128)S(1)}, s32[64,1]{0,1:T(1,128)}, u32[]{:S(2)}) copy-start(s32[64,1]{0,1:T(1,128)} %param.10) | copy-start | bytes 772
  26.9 21.2 %all-to-all-start = ((bf16[8,64,1152]{2,1,0:T(8,128)(2,1)}), bf16[8,64,1152]{2,1,0:T(8,128)(2,1)S(1)}, u32[]{:S(2)}, u32[]{:S(2)}) async-start(bf16[8,64,1152]{2,1,0:T(8,128)(2,1)} %pairs.1), calls=%async_computation | async-start | bytes 2359296 | tf_op jit(solution)/shard_map/all_to_all | solution.py:210

commit v2 on v1

v2 whole, which is shorter than its diff:
```python
import functools

import jax
import jax.numpy as jnp
import ml_dtypes
import numpy as np
from jax import lax
from jax.experimental import pallas as pl
from jax.experimental.pallas import tpu as pltpu
from jax.sharding import PartitionSpec as P

SAMPLES = 4096
PADDED = 8192
NB = 2048
LAGS = 1024
COMPS = 3
SENSORS = 8
PAIRS = 64
CAP = 4
CHUNKS = 8
SPAN = SAMPLES // CHUNKS
RES = 2 * CHUNKS
BINS = NB // RES
ROWS = COMPS * SENSORS
SLAB = 32
HALF = LAGS // 2
TILE = 128
MIB = 1 << 20


def tables():
    k = np.arange(1, RES + 1)
    q = np.arange(BINS)
    twiddles, commons = [], []
    for early in (0.0, 0.5):
        times = np.arange(SPAN) - early
        angle = 2 * np.pi * (k[:, None] * times[None, :] / PADDED)
        twiddles.append(np.stack([np.cos(angle), -np.sin(angle)]).astype(np.float32))
        angle = 2 * np.pi * (times[:, None] * q[None, :] / (PADDED // RES))
        cos, sin = np.cos(angle), np.sin(angle)
        exact = np.block([[cos, -sin], [sin, cos]])
        high = exact.astype(ml_dtypes.bfloat16)
        commons.append(np.stack([high, (exact - high.astype(np.float64)).astype(ml_dtypes.bfloat16)]))
    bins = (k[:, None] + RES * q[None, :]).reshape(-1)
    angle = 2 * np.pi * (bins[:, None] * (np.arange(HALF) + 0.5)[None, :] / PADDED)
    inverse = np.stack([np.cos(angle), np.sin(angle)]).astype(ml_dtypes.bfloat16)
    flip = np.eye(TILE)[::-1].astype(ml_dtypes.bfloat16)
    return np.stack(twiddles), np.stack(commons), inverse, flip


def forward(rows, twiddle_ref, common_ref, parts_ref, store):
    chunks = [rows[:, SPAN * i : SPAN * (i + 1)].astype(jnp.float32) for i in range(CHUNKS)]

    def combine(weights):
        total = None
        for weight, chunk in zip(weights, chunks):
            weight = float(weight)
            if abs(weight) < 1e-9:
                continue
            term = chunk if abs(weight - 1) < 1e-9 else -chunk if abs(weight + 1) < 1e-9 else chunk * weight
            total = term if total is None else total + term
        return total

    for k in range(0, CHUNKS + 1):
        angle = 2 * np.pi * ((k * np.arange(CHUNKS)) % RES) / RES
        real_part = combine(np.cos(angle))
        imag_part = combine(-np.sin(angle))
        both = ((RES, 1.0),) if k == 0 else ((CHUNKS, 1.0),) if k == CHUNKS else ((k, 1.0), (RES - k, -1.0))
        for residue, sign in both:
            tr = twiddle_ref[0, residue - 1 : residue, :]
            ti = twiddle_ref[1, residue - 1 : residue, :]
            if imag_part is None:
                yr, yi = real_part * tr, real_part * ti
            elif sign > 0:
                yr, yi = real_part * tr - imag_part * ti, real_part * ti + imag_part * tr
            else:
                yr, yi = real_part * tr + imag_part * ti, real_part * ti - imag_part * tr
            at = pl.ds((residue - 1) * ROWS, ROWS)
            parts_ref[at, :SPAN] = yr
            parts_ref[at, SPAN:] = yi
    both = parts_ref[...]
    high = both.astype(jnp.bfloat16)
    low = (both - high.astype(jnp.float32)).astype(jnp.bfloat16)
    spec = jnp.dot(high, common_ref[0], preferred_element_type=jnp.float32)
    spec = spec + jnp.dot(low, common_ref[0], preferred_element_type=jnp.float32)
    spec = spec + jnp.dot(high, common_ref[1], preferred_element_type=jnp.float32)
    real_part, imag_part = spec[:, :BINS], spec[:, BINS:]
    power = real_part * real_part + imag_part * imag_part
    total = power[:ROWS]
    for k in range(1, RES):
        total = total + power[k * ROWS : (k + 1) * ROWS]
    level = jnp.sum(total, axis=1, keepdims=True) * (1.0 / NB)
    floor = 0.1 * level + 1e-06
    for k in range(RES):
        at = slice(k * ROWS, (k + 1) * ROWS)
        scale = lax.rsqrt(power[at] + floor)
        store(k, jnp.concatenate([real_part[at] * scale, imag_part[at] * scale], axis=1))


def padded(value):
    return jnp.concatenate([value, jnp.zeros((SLAB - ROWS, value.shape[1]), value.dtype)], axis=0).astype(jnp.bfloat16)


def whiten_kernel(rows_ref, twiddle_ref, common_ref, *refs):
    *white_refs, parts_ref = refs
    for i, white_ref in enumerate(white_refs):
        def store(k, value, white_ref=white_ref):
            white_ref[k] = padded(value)

        forward(rows_ref[...], twiddle_ref.at[i], common_ref.at[i], parts_ref, store)


def pick_kernel(first_ref, second_ref, pick_ref):
    index = lax.broadcasted_iota(jnp.int32, (4 * SLAB, PAIRS), 0)
    first = first_ref[...] + 3 * SLAB
    second = second_ref[...]
    second = second + (second >> 3) * (SLAB - SENSORS)
    columns = [index == at + c * SENSORS for at in (first, second) for c in range(COMPS)]
    spread = jnp.concatenate([c.astype(jnp.float32) for c in columns], axis=1)
    pick_ref[...] = spread.T.astype(jnp.bfloat16)


def cross_kernel(own_ref, turned_ref, nearer_ref, farther_ref, pick_ref, twiddle_ref, common_ref, cross_ref,
                 parts_ref, all_ref):
    def store(k, value):
        all_ref[k, pl.ds(2 * SLAB, SLAB), :] = padded(value)

    forward(farther_ref[...], twiddle_ref.at[0], common_ref.at[0], parts_ref, store)
    for k in range(RES):
        for i, white_ref in ((0, own_ref), (1, nearer_ref), (3, turned_ref)):
            all_ref[k, pl.ds(i * SLAB, SLAB), :] = white_ref[k]

    def cross(k, carry):
        picked = jnp.dot(pick_ref[...], all_ref[k], preferred_element_type=jnp.float32)
        at_re = pl.ds(pl.multiple_of(k * BINS, BINS), BINS)
        at_im = pl.ds(pl.multiple_of(NB + k * BINS, BINS), BINS)
        for c in range(COMPS):
            first = picked[c * PAIRS : (c + 1) * PAIRS]
            ar, ai = first[:, :BINS], first[:, BINS:]
            for e in range(COMPS):
                second = picked[(COMPS + e) * PAIRS : (COMPS + e + 1) * PAIRS]
                br, bi = second[:, :BINS], second[:, BINS:]
                at = c * COMPS + e
                cross_ref[at, :, at_re] = (ar * br + ai * bi).astype(jnp.bfloat16)
                cross_ref[at, :, at_im] = (ar * bi - ai * br).astype(jnp.bfloat16)
        return carry

    lax.fori_loop(0, RES, cross, 0)


def lags_kernel(distances, hour_ref, cross_ref, inverse_ref, flip_ref, *refs):
    *out_refs, tile_ref = refs
    hour = hour_ref[0]
    count = len(distances) + 1
    base = hour ^ distances[0]
    if count == 3:
        base = (base >> 1) * 2
    block = cross_ref[pl.ds(base, count)].reshape(count * PAIRS, 2 * NB)
    even = jnp.dot(block[:, :NB], inverse_ref[0], preferred_element_type=jnp.float32)
    odd = jnp.dot(block[:, NB:], inverse_ref[1], preferred_element_type=jnp.float32)
    after = (even - odd).astype(jnp.bfloat16)
    before = (even + odd).astype(jnp.bfloat16)
    per_comp, per_half = LAGS // TILE, HALF // TILE
    for tile in range(per_half):
        at = slice(tile * TILE, (tile + 1) * TILE)
        turned = jnp.dot(before[:, at], flip_ref[...], preferred_element_type=jnp.float32).astype(jnp.bfloat16)
        for c in range(count):
            of = slice(c * PAIRS, (c + 1) * PAIRS)
            tile_ref[c * per_comp + per_half - 1 - tile] = turned[of]
            tile_ref[c * per_comp + per_half + tile] = after[of, at]
    for distance, out_ref in zip(distances, out_refs):
        tiles = out_ref.shape[1] // TILE
        start = (hour ^ distance) * tiles - base * per_comp
        for u in range(tiles):
            out_ref[:, u * TILE : (u + 1) * TILE] = tile_ref[start + u]


def collect_kernel(place_ref, *refs):
    *parts_refs, out_ref = refs
    total = parts_refs[0][...].astype(jnp.float32)
    for ref in parts_refs[1:]:
        total = total + ref[...].astype(jnp.float32)
    total = (total * (1.0 / 128.0)).astype(jnp.bfloat16)
    out_ref[...] = jnp.dot(place_ref[...], total, preferred_element_type=jnp.float32).astype(jnp.bfloat16)


def from_behind(value, axis, steps):
    count = lax.axis_size(axis)
    return lax.ppermute(value, axis, [(source, (source + steps) % count) for source in range(count)])


def shards(windows, pair_first, pair_second, owners):
    twiddle, common, inverse, flip = (jnp.asarray(t) for t in tables())
    hours = lax.axis_size("hour")
    hour = lax.axis_index("hour").astype(jnp.int32).reshape(1)
    share = COMPS * COMPS * LAGS // hours
    bf16 = jnp.bfloat16
    rows = windows[0].transpose(1, 0, 2).reshape(ROWS, SAMPLES)
    nearer = from_behind(rows, "sens", -1)
    farther = from_behind(rows, "sens", -2)

    owner = owners[:, 0]
    order = jnp.arange(PAIRS, dtype=jnp.int32)
    same = (owner[:, None] == owner[None, :]) & (order[None, :] < order[:, None])
    target = owner * CAP + jnp.sum(same.astype(jnp.int32), axis=1)
    slots = lax.axis_size("sens") * CAP
    place = (jnp.arange(slots, dtype=jnp.int32)[:, None] == target[None, :]).astype(bf16)

    vmem = pl.BlockSpec(memory_space=pltpu.VMEM)
    smem = pl.BlockSpec(memory_space=pltpu.SMEM)
    spectra = jax.ShapeDtypeStruct((RES, SLAB, 2 * BINS), bf16)
    scratch = pltpu.VMEM((RES * ROWS, 2 * SPAN), jnp.float32)

    def whiten(rows, count, name):
        return pl.pallas_call(
            whiten_kernel,
            out_shape=(spectra,) * count,
            in_specs=[vmem] * 3,
            out_specs=(vmem,) * count,
            scratch_shapes=[scratch],
            compiler_params=pltpu.CompilerParams(vmem_limit_bytes=16 * MIB),
            cost_estimate=pl.CostEstimate(flops=10**9 * count, bytes_accessed=10**6, transcendentals=0),
            name=name,
        )(rows, twiddle, common)

    pick = pl.pallas_call(
        pick_kernel,
        out_shape=jax.ShapeDtypeStruct((2 * COMPS * PAIRS, 4 * SLAB), bf16),
        in_specs=[vmem] * 2,
        out_specs=vmem,
        name="pick",
    )(pair_first.reshape(1, PAIRS), pair_second.reshape(1, PAIRS))
    own, turned = whiten(rows, 2, "whiten_own")
    (near,) = whiten(nearer, 1, "whiten_nearer")
    cross = pl.pallas_call(
        cross_kernel,
        out_shape=jax.ShapeDtypeStruct((COMPS * COMPS, PAIRS, 2 * NB), bf16),
        in_specs=[vmem] * 7,
        out_specs=vmem,
        scratch_shapes=[scratch, pltpu.VMEM((RES, 4 * SLAB, 2 * BINS), bf16)],
        compiler_params=pltpu.CompilerParams(vmem_limit_bytes=16 * MIB),
        cost_estimate=pl.CostEstimate(flops=3 * 10**9, bytes_accessed=10**6, transcendentals=0),
        name="cross",
    )(own, turned, near, farther, pick, twiddle, common)

    def lags(distances):
        one = jax.ShapeDtypeStruct((PAIRS, share), bf16)
        return pl.pallas_call(
            functools.partial(lags_kernel, distances),
            out_shape=(one,) * len(distances),
            in_specs=[smem] + [vmem] * 3,
            out_specs=(vmem,) * len(distances),
            scratch_shapes=[pltpu.VMEM((3 * LAGS // TILE, PAIRS, TILE), bf16)],
            compiler_params=pltpu.CompilerParams(vmem_limit_bytes=16 * MIB),
            cost_estimate=pl.CostEstimate(flops=10**9, bytes_accessed=10**6, transcendentals=0),
            name="lags",
        )(hour, cross, inverse, flip)

    parts = []
    for distances in ((6, 7), (4, 5), (2, 3), (1,), (0,)):
        for distance, part in zip(distances, lags(distances)):
            if distance:
                part = lax.ppermute(part, "hour", [(h, h ^ distance) for h in range(hours)])
            parts.append(part)
    outgoing = pl.pallas_call(
        collect_kernel,
        out_shape=jax.ShapeDtypeStruct((slots, share), bf16),
        in_specs=[vmem] * (1 + hours),
        out_specs=vmem,
        compiler_params=pltpu.CompilerParams(vmem_limit_bytes=16 * MIB),
        cost_estimate=pl.CostEstimate(flops=2 * 10**7, bytes_accessed=2 * 10**6, transcendentals=0),
        name="collect",
    )(place, *parts)
    stacked = lax.all_to_all(outgoing, "sens", split_axis=0, concat_axis=0, tiled=True)
    return stacked.astype(jnp.float32)


def solution(mesh):
    placed = (P("hour", "sens", None, None), P("sens"), P("sens"), P("sens", None))
    return jax.shard_map(
        shards, mesh=mesh, in_specs=placed, out_specs=P("sens", "hour"), check_vma=False
    )
```

time: 69.7 us -> 66.4 us (0.953)
  waiting for transfers between devices: 14.6 us -> 4.97 us
  starting transfers between devices: 14.4 us -> 20.4 us
  Pallas kernels: 14.4 us -> 16.1 us
  blocking collectives: 20 us -> 18.6 us
    all_to_all x1 -> x0, waiting for transfers between devices: 14.6 us -> none  [shards(): lax.all_to_all(partial, 'hour', split_axis=0, concat_axis=0, tiled=True)]
    ppermute x0 -> x7, starting transfers between devices: none -> 12.4 us  [shards(): part = lax.ppermute(part, 'hour', [(h, h ^ distance) for h in range(hours)])]
    all_to_all x1 -> x0, starting transfers between devices: 6.38 us -> none  [shards(): lax.all_to_all(partial, 'hour', split_axis=0, concat_axis=0, tiled=True)]
    ppermute x0 -> x7, waiting for transfers between devices: none -> 4.96 us  [shards(): part = lax.ppermute(part, 'hour', [(h, h ^ distance) for h in range(hours)])]
    pallas_call x2 -> x9, Pallas kernels: 14.1 us -> 15.8 us  [the longest x1 5.72 us: shards(): pl.pallas_call(cross_kernel, out_shape=jax.ShapeDtypeStruct((COMPS * COMP...]
    all_to_all x1, blocking collectives: 20 us -> 18.6 us  [shards(): lax.all_to_all(outgoing, 'sens', split_axis=0, concat_axis=0, tiled=True)]
    add x2 -> x0, other arithmetic: 1.39 us -> none  [the longest x1 0.72 us: shards(): pick_first = (comps + pair_first[None, :]).reshape(-1)]
    reduce_sum x1, other arithmetic: 0.17 us -> 0.91 us  [shards(): target = owner * CAP + jnp.sum(same.astype(jnp.int32), axis=1)]
  transfers between devices with their start and end apart: 3 -> 9, of which waited for: 1 -> 2; matrix products, arithmetic and copies ran while one was open for 3% -> 2% of each run, Pallas kernels for 2% -> 12%
where the time goes in v2:
time: 66.4 us; the launch traced here: 66.1 us
  starting transfers between devices  20.4 us (31%)
  blocking collectives  18.6 us (28%)
  Pallas kernels  16.1 us (24%)
  waiting for transfers between devices  4.97 us (7%)
  local copies, waits for them, and re-layouts  4.37 us (7%)
  other arithmetic  1.59 us (2%)
    all_to_all x1, blocking collectives, shards(): lax.all_to_all(outgoing, 'sens', split_axis=0, concat_axis=0, tiled=True)  18.6 us
    ppermute x7, starting transfers between devices, shards(): part = lax.ppermute(part, 'hour', [(h, h ^ distance) for h in range(hours)])  12.4 us
    ppermute x2, starting transfers between devices, from_behind(): lax.ppermute(value, axis, [(source, (source + steps) % count) for source...  8.01 us
    pallas_call x1, Pallas kernels, shards(): pl.pallas_call(cross_kernel, out_shape=jax.ShapeDtypeStruct((COMPS * COMP...  5.72 us
    pallas_call x5, Pallas kernels, lags(): pl.pallas_call(functools.partial(lags_kernel, distances), out_shape=(one,...  5.37 us
    ppermute x7, waiting for transfers between devices, shards(): part = lax.ppermute(part, 'hour', [(h, h ^ distance) for h in range(hours)])  4.96 us
    unnamed x14, local copies, waits for them, and re-layouts  3.44 us
    pallas_call x2, Pallas kernels, whiten(): pl.pallas_call(whiten_kernel, out_shape=(spectra,) * count, in_specs=[vme...  3.19 us
  transfers between devices with their start and end apart: 9, of which 2 were waited for; matrix products, arithmetic and copies ran while one was open for 2% of the time, Pallas kernels for 12%

profile of v2, /device:TPU:1, one launch (start us, length us, event | category | flops | bytes accessed | tf_op | source)
XLA Modules:
  0.0 66.1 jit_solution(2108733630022213700)
XLA Ops:
  0.0 3.2 %collective-permute-start = (bf16[24,4096]{1,0:T(8,128)(2,1)}, bf16[24,4096]{1,0:T(8,128)(2,1)S(1)}, u32[]{:S(2)}, u32[]{:S(2)}) collective-permute-start(bf16[24,4096]{1,0:T(8,128)(2,1)} %bitcast.10), channel_id=1, source_target_pairs={{0,248},{8,0},{16,8},{24,16},{32,24},{40,32},{48,40},{56,48},{64,5... | collective-permute-start | bytes 589832 | tf_op jit(solution)/shard_map/ppermute | solution.py:189
  3.2 4.8 %collective-permute-start.1 = (bf16[24,4096]{1,0:T(8,128)(2,1)}, bf16[24,4096]{1,0:T(8,128)(2,1)S(1)}, u32[]{:S(2)}, u32[]{:S(2)}) collective-permute-start(bf16[24,4096]{1,0:T(8,128)(2,1)} %bitcast.11), channel_id=1, source_target_pairs={{0,240},{8,248},{16,0},{24,8},{32,16},{40,24},{48,32},{56,40},{64,... | collective-permute-start | bytes 589832 | tf_op jit(solution)/shard_map/ppermute | solution.py:189
  8.0 0.9 %convert_reduce_fusion = s32[64]{0:T(128)S(1)} fusion(s32[64]{0:T(128)} %bitcast.15), kind=kLoop, calls=%fused_computation.2 | loop fusion | flops 20416 | bytes 512 | tf_op jit(solution)/shard_map/reduce_sum | solution.py:205
  8.9 0.7 %multiply_add_fusion = s32[64]{0:T(128)S(1)} fusion(s32[64]{0:T(128)S(1)} %convert_reduce_fusion, s32[64,1]{0,1:T(1,128)} %param.11), kind=kLoop, calls=%fused_computation.5 | loop fusion | flops 128 | bytes 768 | tf_op jit(solution)/shard_map/add | solution.py:205
  9.6 1.5 %pick.1.pick_ref = bf16[384,128]{1,0:T(8,128)(2,1)} custom-call(s32[1,64]{1,0:T(1,128)} %bitcast.13, s32[1,64]{1,0:T(1,128)} %bitcast.14), custom_call_target="tpu_custom_call" | custom-call | tf_op jit(solution)/shard_map/pick/pallas_call | solution.py:226
  11.1 0.9 %copy-done.3 = bf16[1,8,3,4096]{3,1,2,0:T(8,128)(2,1)S(1)} copy-done((bf16[1,8,3,4096]{3,1,2,0:T(8,128)(2,1)S(1)}, bf16[1,8,3,4096]{3,1,2,0:T(8,128)(2,1)}, u32[]{:S(2)}) %copy-start.3) | copy-done | bytes 196632
  12.0 1.6 %copy-done.4 = bf16[2,2,1024,256]{3,2,1,0:T(8,128)(2,1)S(1)} copy-done((bf16[2,2,1024,256]{3,2,1,0:T(8,128)(2,1)S(1)}, bf16[2,2,1024,256]{3,2,1,0:T(8,128)(2,1)}, u32[]{:S(2)}) %copy-start.4) | copy-done | bytes 2097176
  13.6 0.9 %copy-done.6 = f32[2,2,16,512]{3,2,1,0:T(8,128)S(1)} copy-done((f32[2,2,16,512]{3,2,1,0:T(8,128)S(1)}, f32[2,2,16,512]{3,2,1,0:T(8,128)}, u32[]{:S(2)}) %copy-start.6) | copy-done | bytes 131096
  14.5 2.0 %whiten_own.1 = (bf16[16,32,256]{2,1,0:T(8,128)(2,1)S(1)}, bf16[16,32,256]{2,1,0:T(8,128)(2,1)S(1)}) custom-call(bf16[24,4096]{1,0:T(8,128)(2,1)S(1)} %bitcast.12, f32[2,2,16,512]{3,2,1,0:T(8,128)S(1)} %copy-done.6, bf16[2,2,1024,256]{3,2,1,0:T(8,128)(2,1)S(1)} %copy-done.4), custom_call_target="tpu_custom_call" | custom-call | flops 2000000000 | bytes 1000000 | tf_op jit(solution)/shard_map/whiten_own/pallas_call | solution.py:215
  16.5 0.0 collective-permute-done.rows_ref
  16.5 1.2 %whiten_nearer.1.nearer_ref = bf16[16,32,256]{2,1,0:T(8,128)(2,1)S(1)} custom-call(bf16[24,4096]{1,0:T(8,128)(2,1)S(1)} %collective-permute-done.rows_ref, f32[2,2,16,512]{3,2,1,0:T(8,128)S(1)} %copy-done.6, bf16[2,2,1024,256]{3,2,1,0:T(8,128)(2,1)S(1)} %copy-done.4), custom_call_target="tpu_custom_call" | custom-call | flops 1000000000 | bytes 1000000 | tf_op jit(solution)/shard_map/whiten_nearer/pallas_call | solution.py:215
  17.8 0.0 copy-start
  17.8 0.0 copy-start.1
  17.8 5.7 %cross.1.cross_ref = bf16[9,64,4096]{2,1,0:T(8,128)(2,1)S(1)} custom-call(bf16[16,32,256]{2,1,0:T(8,128)(2,1)S(1)} %get-tuple-element.13.own_ref, bf16[16,32,256]{2,1,0:T(8,128)(2,1)S(1)} %get-tuple-element.14.turned_ref, bf16[16,32,256]{2,1,0:T(8,128)(2,1)S(1)} %whiten_nearer.1.nearer_ref, bf16[24,4096]{1,0:T(8,128)(2,1)S(1)} %collective-permute-done.1.farther_ref, ...), custom_call_target="tpu_custom_call" | custom-call | flops 3000000000 | bytes 1000000 | tf_op jit(solution)/shard_map/cross/pallas_call | solution.py:235
  23.5 1.2 %lags.6 = (bf16[64,1152]{1,0:T(8,128)(2,1)S(1)}, bf16[64,1152]{1,0:T(8,128)(2,1)S(1)}) custom-call(s32[1]{0:T(128)} %bitcast.1.hour_ref, bf16[9,64,4096]{2,1,0:T(8,128)(2,1)S(1)} %cross.1.cross_ref, bf16[2,2048,512]{2,1,0:T(8,128)(2,1)S(1)} %copy-done, bf16[128,128]{1,0:T(8,128)(2,1)S(1)} %copy-done.1), custom_call_target="tpu_custom_call" | custom-call | flops 1000000000 | bytes 1000000 | tf_op jit(solution)/shard_map/lags/pallas_call | solution.py:248
  24.7 1.2 %lags.7 = (bf16[64,1152]{1,0:T(8,128)(2,1)S(1)}, bf16[64,1152]{1,0:T(8,128)(2,1)S(1)}) custom-call(s32[1]{0:T(128)} %bitcast.1.hour_ref, bf16[9,64,4096]{2,1,0:T(8,128)(2,1)S(1)} %cross.1.cross_ref, bf16[2,2048,512]{2,1,0:T(8,128)(2,1)S(1)} %copy-done, bf16[128,128]{1,0:T(8,128)(2,1)S(1)} %copy-done.1), custom_call_target="tpu_custom_call" | custom-call | flops 1000000000 | bytes 1000000 | tf_op jit(solution)/shard_map/lags/pallas_call | solution.py:248
  25.9 2.5 %collective-permute-start.4 = (bf16[64,1152]{1,0:T(8,128)(2,1)S(1)}, bf16[64,1152]{1,0:T(8,128)(2,1)S(1)}, u32[]{:S(2)}, u32[]{:S(2)}) collective-permute-start(bf16[64,1152]{1,0:T(8,128)(2,1)S(1)} %get-tuple-element.17), channel_id=1, source_target_pairs={{0,4},{1,5},{2,6},{3,7},{4,0},{5,1},{6,2},{7,3},{8,12},{9,13},{10,... | collective-permute-start | bytes 442376 | tf_op jit(solution)/shard_map/ppermute | solution.py:263
  28.5 1.5 %collective-permute-start.5 = (bf16[64,1152]{1,0:T(8,128)(2,1)S(1)}, bf16[64,1152]{1,0:T(8,128)(2,1)S(1)}, u32[]{:S(2)}, u32[]{:S(2)}) collective-permute-start(bf16[64,1152]{1,0:T(8,128)(2,1)S(1)} %get-tuple-element.18), channel_id=1, source_target_pairs={{0,5},{1,4},{2,7},{3,6},{4,1},{5,0},{6,3},{7,2},{8,13},{9,12},{10,... | collective-permute-start | bytes 442376 | tf_op jit(solution)/shard_map/ppermute | solution.py:263
  30.0 2.7 %collective-permute-start.6 = (bf16[64,1152]{1,0:T(8,128)(2,1)S(1)}, bf16[64,1152]{1,0:T(8,128)(2,1)S(1)}, u32[]{:S(2)}, u32[]{:S(2)}) collective-permute-start(bf16[64,1152]{1,0:T(8,128)(2,1)S(1)} %get-tuple-element.19), channel_id=1, source_target_pairs={{0,2},{1,3},{2,0},{3,1},{4,6},{5,7},{6,4},{7,5},{8,10},{9,11},{10,... | collective-permute-start | bytes 442376 | tf_op jit(solution)/shard_map/ppermute | solution.py:263
  32.7 0.0 collective-permute-start.7
  32.7 1.2 %lags.5 = (bf16[64,1152]{1,0:T(8,128)(2,1)S(1)}, bf16[64,1152]{1,0:T(8,128)(2,1)S(1)}) custom-call(s32[1]{0:T(128)} %bitcast.1.hour_ref, bf16[9,64,4096]{2,1,0:T(8,128)(2,1)S(1)} %cross.1.cross_ref, bf16[2,2048,512]{2,1,0:T(8,128)(2,1)S(1)} %copy-done, bf16[128,128]{1,0:T(8,128)(2,1)S(1)} %copy-done.1), custom_call_target="tpu_custom_call" | custom-call | flops 1000000000 | bytes 1000000 | tf_op jit(solution)/shard_map/lags/pallas_call | solution.py:248
  33.9 3.9 %collective-permute-start.2 = (bf16[64,1152]{1,0:T(8,128)(2,1)S(1)}, bf16[64,1152]{1,0:T(8,128)(2,1)S(1)}, u32[]{:S(2)}, u32[]{:S(2)}) collective-permute-start(bf16[64,1152]{1,0:T(8,128)(2,1)S(1)} %get-tuple-element.15), channel_id=1, source_target_pairs={{0,6},{1,7},{2,4},{3,5},{4,2},{5,3},{6,0},{7,1},{8,14},{9,15},{10,... | collective-permute-start | bytes 442376 | tf_op jit(solution)/shard_map/ppermute | solution.py:263
  37.7 0.9 %lags.8 = bf16[64,1152]{1,0:T(8,128)(2,1)S(1)} custom-call(s32[1]{0:T(128)} %bitcast.1.hour_ref, bf16[9,64,4096]{2,1,0:T(8,128)(2,1)S(1)} %cross.1.cross_ref, bf16[2,2048,512]{2,1,0:T(8,128)(2,1)S(1)} %copy-done, bf16[128,128]{1,0:T(8,128)(2,1)S(1)} %copy-done.1), custom_call_target="tpu_custom_call" | custom-call | flops 1000000000 | bytes 1000000 | tf_op jit(solution)/shard_map/lags/pallas_call | solution.py:248
  38.6 1.1 %collective-permute-start.3 = (bf16[64,1152]{1,0:T(8,128)(2,1)S(1)}, bf16[64,1152]{1,0:T(8,128)(2,1)S(1)}, u32[]{:S(2)}, u32[]{:S(2)}) collective-permute-start(bf16[64,1152]{1,0:T(8,128)(2,1)S(1)} %get-tuple-element.16), channel_id=1, source_target_pairs={{0,7},{1,6},{2,5},{3,4},{4,3},{5,2},{6,1},{7,0},{8,15},{9,14},{10,... | collective-permute-start | bytes 442376 | tf_op jit(solution)/shard_map/ppermute | solution.py:263
  39.8 0.7 %collective-permute-start.8 = (bf16[64,1152]{1,0:T(8,128)(2,1)S(1)}, bf16[64,1152]{1,0:T(8,128)(2,1)S(1)}, u32[]{:S(2)}, u32[]{:S(2)}) collective-permute-start(bf16[64,1152]{1,0:T(8,128)(2,1)S(1)} %lags.8), channel_id=1, source_target_pairs={{0,1},{1,0},{2,3},{3,2},{4,5},{5,4},{6,7},{7,6},{8,9},{9,8},{10,11... | collective-permute-start | bytes 442376 | tf_op jit(solution)/shard_map/ppermute | solution.py:263
  40.4 0.9 %lags.9.refs_7_ = bf16[64,1152]{1,0:T(8,128)(2,1)S(1)} custom-call(s32[1]{0:T(128)} %bitcast.1.hour_ref, bf16[9,64,4096]{2,1,0:T(8,128)(2,1)S(1)} %cross.1.cross_ref, bf16[2,2048,512]{2,1,0:T(8,128)(2,1)S(1)} %copy-done, bf16[128,128]{1,0:T(8,128)(2,1)S(1)} %copy-done.1), custom_call_target="tpu_custom_call" | custom-call | flops 1000000000 | bytes 1000000 | tf_op jit(solution)/shard_map/lags/pallas_call | solution.py:248
  41.4 0.6 collective-permute-done.2.refs_0_
  42.0 4.3 %collective-permute-done.3.refs_1_ = bf16[64,1152]{1,0:T(8,128)(2,1)S(1)} collective-permute-done((bf16[64,1152]{1,0:T(8,128)(2,1)S(1)}, bf16[64,1152]{1,0:T(8,128)(2,1)S(1)}, u32[]{:S(2)}, u32[]{:S(2)}) %collective-permute-start.3) | collective-permute-done | bytes 147488 | tf_op jit(solution)/shard_map/ppermute | solution.py:263
  46.3 0.3 collect.1
  46.6 0.1 all_to_all.6
  46.7 18.6 %all_to_all.9 = bf16[32,4,1152]{2,1,0:T(4,128)(2,1)S(1)} all-to-all(bf16[32,4,1152]{2,1,0:T(4,128)(2,1)S(1)} %all_to_all.6), channel_id=1, replica_groups=mesh['sens'=32,'hour'=8] {'sens'}, dimensions={0} | all-to-all | bytes 589824 | tf_op jit(solution)/shard_map/all_to_all | solution.py:274
  65.3 0.9 %reshape.29 = f32[128,1152]{1,0:T(8,128)} reshape(bf16[32,4,1152]{2,1,0:T(4,128)(2,1)S(1)} %all_to_all.9) | data formatting | bytes 884736 | tf_op jit(solution)/shard_map/convert_element_type | solution.py:275
  (16 shorter events, 0.0 us)
Async XLA Ops:
  0.0 16.5 %collective-permute-start = (bf16[24,4096]{1,0:T(8,128)(2,1)}, bf16[24,4096]{1,0:T(8,128)(2,1)S(1)}, u32[]{:S(2)}, u32[]{:S(2)}) collective-permute-start(bf16[24,4096]{1,0:T(8,128)(2,1)} %bitcast.10), channel_id=1, source_target_pairs={{0,248},{8,0},{16,8},{24,16},{32,24},{40,32},{48,40},{56,48},{64,5... | collective-permute-start | bytes 589832 | tf_op jit(solution)/shard_map/ppermute | solution.py:189
  3.2 14.5 %collective-permute-start.1 = (bf16[24,4096]{1,0:T(8,128)(2,1)}, bf16[24,4096]{1,0:T(8,128)(2,1)S(1)}, u32[]{:S(2)}, u32[]{:S(2)}) collective-permute-start(bf16[24,4096]{1,0:T(8,128)(2,1)} %bitcast.11), channel_id=1, source_target_pairs={{0,240},{8,248},{16,0},{24,8},{32,16},{40,24},{48,32},{56,40},{64,... | collective-permute-start | bytes 589832 | tf_op jit(solution)/shard_map/ppermute | solution.py:189
  11.1 0.9 %copy-start.3 = (bf16[1,8,3,4096]{3,1,2,0:T(8,128)(2,1)S(1)}, bf16[1,8,3,4096]{3,1,2,0:T(8,128)(2,1)}, u32[]{:S(2)}) copy-start(bf16[1,8,3,4096]{3,1,2,0:T(8,128)(2,1)} %param.8) | copy-start | bytes 589828
  12.0 1.6 %copy-start.4 = (bf16[2,2,1024,256]{3,2,1,0:T(8,128)(2,1)S(1)}, bf16[2,2,1024,256]{3,2,1,0:T(8,128)(2,1)}, u32[]{:S(2)}) copy-start(bf16[2,2,1024,256]{3,2,1,0:T(8,128)(2,1)} %constant.17.clone.common_ref) | copy-start | bytes 6291460
  13.6 0.9 %copy-start.6 = (f32[2,2,16,512]{3,2,1,0:T(8,128)S(1)}, f32[2,2,16,512]{3,2,1,0:T(8,128)}, u32[]{:S(2)}) copy-start(f32[2,2,16,512]{3,2,1,0:T(8,128)} %constant.16.clone.twiddle_ref) | copy-start | bytes 393220
  14.5 3.2 %copy-start.2 = (bf16[384,128]{1,0:T(8,128)(2,1)S(1)}, bf16[384,128]{1,0:T(8,128)(2,1)}, u32[]{:S(2)}) copy-start(bf16[384,128]{1,0:T(8,128)(2,1)} %pick.1.pick_ref) | copy-start | bytes 294916
  14.5 3.2 %copy-start.5 = (bf16[2,2,1024,256]{3,2,1,0:T(8,128)(2,1)S(1)}, bf16[2,2,1024,256]{3,2,1,0:T(8,128)(2,1)}, u32[]{:S(2)}) copy-start(bf16[2,2,1024,256]{3,2,1,0:T(8,128)(2,1)} %constant.17.clone.common_ref) | copy-start | bytes 6291460
  17.8 5.8 %copy-start = (bf16[2,2048,512]{2,1,0:T(8,128)(2,1)S(1)}, bf16[2,2048,512]{2,1,0:T(8,128)(2,1)}, u32[]{:S(2)}) copy-start(bf16[2,2048,512]{2,1,0:T(8,128)(2,1)} %constant.18.clone.inverse_ref) | copy-start | bytes 12582916
  17.8 5.8 %copy-start.1 = (bf16[128,128]{1,0:T(8,128)(2,1)S(1)}, bf16[128,128]{1,0:T(8,128)(2,1)}, u32[]{:S(2)}) copy-start(bf16[128,128]{1,0:T(8,128)(2,1)} %constant.19.clone.flip_ref) | copy-start | bytes 98308
  25.9 12.7 %collective-permute-start.4 = (bf16[64,1152]{1,0:T(8,128)(2,1)S(1)}, bf16[64,1152]{1,0:T(8,128)(2,1)S(1)}, u32[]{:S(2)}, u32[]{:S(2)}) collective-permute-start(bf16[64,1152]{1,0:T(8,128)(2,1)S(1)} %get-tuple-element.17), channel_id=1, source_target_pairs={{0,4},{1,5},{2,6},{3,7},{4,0},{5,1},{6,2},{7,3},{8,12},{9,13},{10,... | collective-permute-start | bytes 442376 | tf_op jit(solution)/shard_map/ppermute | solution.py:263
  28.5 11.3 %collective-permute-start.5 = (bf16[64,1152]{1,0:T(8,128)(2,1)S(1)}, bf16[64,1152]{1,0:T(8,128)(2,1)S(1)}, u32[]{:S(2)}, u32[]{:S(2)}) collective-permute-start(bf16[64,1152]{1,0:T(8,128)(2,1)S(1)} %get-tuple-element.18), channel_id=1, source_target_pairs={{0,5},{1,4},{2,7},{3,6},{4,1},{5,0},{6,3},{7,2},{8,13},{9,12},{10,... | collective-permute-start | bytes 442376 | tf_op jit(solution)/shard_map/ppermute | solution.py:263
  30.0 11.4 %collective-permute-start.6 = (bf16[64,1152]{1,0:T(8,128)(2,1)S(1)}, bf16[64,1152]{1,0:T(8,128)(2,1)S(1)}, u32[]{:S(2)}, u32[]{:S(2)}) collective-permute-start(bf16[64,1152]{1,0:T(8,128)(2,1)S(1)} %get-tuple-element.19), channel_id=1, source_target_pairs={{0,2},{1,3},{2,0},{3,1},{4,6},{5,7},{6,4},{7,5},{8,10},{9,11},{10,... | collective-permute-start | bytes 442376 | tf_op jit(solution)/shard_map/ppermute | solution.py:263
  32.7 8.7 %collective-permute-start.7 = (bf16[64,1152]{1,0:T(8,128)(2,1)S(1)}, bf16[64,1152]{1,0:T(8,128)(2,1)S(1)}, u32[]{:S(2)}, u32[]{:S(2)}) collective-permute-start(bf16[64,1152]{1,0:T(8,128)(2,1)S(1)} %get-tuple-element.20), channel_id=1, source_target_pairs={{0,3},{1,2},{2,1},{3,0},{4,7},{5,6},{6,5},{7,4},{8,11},{9,10},{10,... | collective-permute-start | bytes 442376 | tf_op jit(solution)/shard_map/ppermute | solution.py:263
  33.9 8.1 %collective-permute-start.2 = (bf16[64,1152]{1,0:T(8,128)(2,1)S(1)}, bf16[64,1152]{1,0:T(8,128)(2,1)S(1)}, u32[]{:S(2)}, u32[]{:S(2)}) collective-permute-start(bf16[64,1152]{1,0:T(8,128)(2,1)S(1)} %get-tuple-element.15), channel_id=1, source_target_pairs={{0,6},{1,7},{2,4},{3,5},{4,2},{5,3},{6,0},{7,1},{8,14},{9,15},{10,... | collective-permute-start | bytes 442376 | tf_op jit(solution)/shard_map/ppermute | solution.py:263
  38.6 7.7 %collective-permute-start.3 = (bf16[64,1152]{1,0:T(8,128)(2,1)S(1)}, bf16[64,1152]{1,0:T(8,128)(2,1)S(1)}, u32[]{:S(2)}, u32[]{:S(2)}) collective-permute-start(bf16[64,1152]{1,0:T(8,128)(2,1)S(1)} %get-tuple-element.16), channel_id=1, source_target_pairs={{0,7},{1,6},{2,5},{3,4},{4,3},{5,2},{6,1},{7,0},{8,15},{9,14},{10,... | collective-permute-start | bytes 442376 | tf_op jit(solution)/shard_map/ppermute | solution.py:263
  39.8 6.6 %collective-permute-start.8 = (bf16[64,1152]{1,0:T(8,128)(2,1)S(1)}, bf16[64,1152]{1,0:T(8,128)(2,1)S(1)}, u32[]{:S(2)}, u32[]{:S(2)}) collective-permute-start(bf16[64,1152]{1,0:T(8,128)(2,1)S(1)} %lags.8), channel_id=1, source_target_pairs={{0,1},{1,0},{2,3},{3,2},{4,5},{5,4},{6,7},{7,6},{8,9},{9,8},{10,11... | collective-permute-start | bytes 442376 | tf_op jit(solution)/shard_map/ppermute | solution.py:263

commit v3 on v2

v3 whole, which is shorter than its diff:
```python
import functools

import jax
import jax.numpy as jnp
import ml_dtypes
import numpy as np
from jax import lax
from jax.experimental import pallas as pl
from jax.experimental.pallas import tpu as pltpu
from jax.sharding import PartitionSpec as P

SAMPLES = 4096
PADDED = 8192
NB = 2048
LAGS = 1024
COMPS = 3
SENSORS = 8
PAIRS = 64
CAP = 4
CHUNKS = 8
SPAN = SAMPLES // CHUNKS
RES = 2 * CHUNKS
BINS = NB // RES
ROWS = COMPS * SENSORS
SLAB = 32
HALF = LAGS // 2
TILE = 128
MIB = 1 << 20


def tables():
    k = np.arange(1, RES + 1)
    t2 = np.arange(SPAN)
    q = np.arange(BINS)
    angle = 2 * np.pi * ((k[:, None] * t2[None, :]) % PADDED) / PADDED
    twiddle = np.stack([np.cos(angle), -np.sin(angle)]).astype(np.float32)
    period = PADDED // RES
    angle = 2 * np.pi * ((t2[:, None] * q[None, :]) % period) / period
    cos, sin = np.cos(angle), np.sin(angle)
    exact = np.block([[cos, -sin], [sin, cos]])
    high = exact.astype(ml_dtypes.bfloat16)
    common = np.stack([high, (exact - high.astype(np.float64)).astype(ml_dtypes.bfloat16)])
    bins = (k[:, None] + RES * q[None, :]).reshape(-1)
    angle = 2 * np.pi * ((bins[:, None] * np.arange(1, HALF + 1)[None, :]) % PADDED) / PADDED
    cosines = np.zeros((NB, HALF + TILE))
    cosines[:, :HALF] = np.cos(angle)
    cosines[:, -1] = 1.0
    cosines = cosines.astype(ml_dtypes.bfloat16)
    sines = np.sin(angle).astype(ml_dtypes.bfloat16)
    flip = np.eye(TILE)[::-1]
    shift = np.eye(2 * TILE)[:, TILE - 1 : 2 * TILE - 1]
    moves = np.concatenate([flip, shift]).astype(ml_dtypes.bfloat16)
    return twiddle, common, cosines, sines, moves


def forward(rows, twiddle_ref, common_ref, parts_ref, store):
    chunks = [rows[:, SPAN * i : SPAN * (i + 1)].astype(jnp.float32) for i in range(CHUNKS)]

    def combine(weights):
        total = None
        for weight, chunk in zip(weights, chunks):
            weight = float(weight)
            if abs(weight) < 1e-9:
                continue
            term = chunk if abs(weight - 1) < 1e-9 else -chunk if abs(weight + 1) < 1e-9 else chunk * weight
            total = term if total is None else total + term
        return total

    for k in range(0, CHUNKS + 1):
        angle = 2 * np.pi * ((k * np.arange(CHUNKS)) % RES) / RES
        real_part = combine(np.cos(angle))
        imag_part = combine(-np.sin(angle))
        both = ((RES, 1.0),) if k == 0 else ((CHUNKS, 1.0),) if k == CHUNKS else ((k, 1.0), (RES - k, -1.0))
        for residue, sign in both:
            tr = twiddle_ref[0, residue - 1 : residue, :]
            ti = twiddle_ref[1, residue - 1 : residue, :]
            if imag_part is None:
                yr, yi = real_part * tr, real_part * ti
            elif sign > 0:
                yr, yi = real_part * tr - imag_part * ti, real_part * ti + imag_part * tr
            else:
                yr, yi = real_part * tr + imag_part * ti, real_part * ti - imag_part * tr
            at = pl.ds((residue - 1) * ROWS, ROWS)
            parts_ref[at, :SPAN] = yr
            parts_ref[at, SPAN:] = yi
    both = parts_ref[...]
    high = both.astype(jnp.bfloat16)
    low = (both - high.astype(jnp.float32)).astype(jnp.bfloat16)
    spec = jnp.dot(high, common_ref[0], preferred_element_type=jnp.float32)
    spec = spec + jnp.dot(low, common_ref[0], preferred_element_type=jnp.float32)
    spec = spec + jnp.dot(high, common_ref[1], preferred_element_type=jnp.float32)
    real_part, imag_part = spec[:, :BINS], spec[:, BINS:]
    power = real_part * real_part + imag_part * imag_part
    total = power[:ROWS]
    for k in range(1, RES):
        total = total + power[k * ROWS : (k + 1) * ROWS]
    level = jnp.sum(total, axis=1, keepdims=True) * (1.0 / NB)
    floor = 0.1 * level + 1e-06
    for k in range(RES):
        at = slice(k * ROWS, (k + 1) * ROWS)
        scale = lax.rsqrt(power[at] + floor)
        store(k, jnp.concatenate([real_part[at] * scale, imag_part[at] * scale], axis=1))


def padded(value):
    return jnp.concatenate([value, jnp.zeros((SLAB - ROWS, value.shape[1]), value.dtype)], axis=0).astype(jnp.bfloat16)


def one_hot(index, height):
    at = lax.broadcasted_iota(jnp.int32, (height, PAIRS), 0)
    return jnp.concatenate([(at == i).astype(jnp.float32) for i in index], axis=1)


def own_kernel(rows_any, twiddle_any, common_any, first_any, second_any, owner_any,
               white_ref, first_rows_ref, pick_ref, place_ref,
               rows_ref, twiddle_ref, common_ref, first_ref, second_ref, owner_ref, parts_ref, sems):
    sources = (rows_any, twiddle_any, common_any, first_any, second_any, owner_any)
    targets = (rows_ref, twiddle_ref, common_ref, first_ref, second_ref, owner_ref)
    copies = [pltpu.make_async_copy(s, t, sems.at[i]) for i, (s, t) in enumerate(zip(sources, targets))]
    for copy in copies:
        copy.start()
    for copy in copies:
        copy.wait()

    owner = owner_ref[...]
    lanes = jnp.broadcast_to(owner, (PAIRS, PAIRS)).astype(jnp.float32)
    earlier = lax.broadcasted_iota(jnp.int32, (PAIRS, PAIRS), 0) < lax.broadcasted_iota(jnp.int32, (PAIRS, PAIRS), 1)
    same = (lanes == lanes.T) & earlier
    slot = jnp.sum(same.astype(jnp.float32), axis=0, keepdims=True).astype(jnp.int32)
    place_ref[...] = one_hot([owner * CAP + slot], place_ref.shape[0]).astype(jnp.bfloat16)
    second = second_ref[...]
    second = second + (second >> 3) * (SLAB - SENSORS)
    pick_ref[...] = one_hot([second + c * SENSORS for c in range(COMPS)], TILE).T.astype(jnp.bfloat16)
    pick_first = one_hot([first_ref[...] + c * SENSORS for c in range(COMPS)], TILE).T.astype(jnp.bfloat16)[:, :SLAB]

    def store(k, value):
        value = padded(value)
        white_ref[k] = value
        first_rows_ref[k] = jnp.dot(pick_first, value, preferred_element_type=jnp.float32).astype(jnp.bfloat16)

    forward(rows_ref[...], twiddle_ref, common_ref, parts_ref, store)


def nearer_kernel(rows_ref, twiddle_ref, common_ref, white_ref, parts_ref):
    def store(k, value):
        white_ref[k] = padded(value)

    forward(rows_ref[...], twiddle_ref, common_ref, parts_ref, store)


def cross_kernel(first_rows_ref, own_ref, near_ref, farther_ref, pick_ref, twiddle_ref, common_ref, cross_ref,
                 parts_ref, far_ref, second_ref):
    def store(k, value):
        far_ref[k] = padded(value)

    forward(farther_ref[...], twiddle_ref, common_ref, parts_ref, store)
    pick = pick_ref[...]
    group = 16

    def cross(k, carry):
        spectra = jnp.concatenate([own_ref[k], near_ref[k], far_ref[k]], axis=0)
        second_ref[...] = jnp.dot(pick[:, : 3 * SLAB], spectra, preferred_element_type=jnp.float32)
        at_re = pl.ds(pl.multiple_of(k * BINS, BINS), BINS)
        at_im = pl.ds(pl.multiple_of(NB + k * BINS, BINS), BINS)
        for g in range(0, PAIRS, group):
            seconds = [second_ref[e * PAIRS + g : e * PAIRS + g + group, :] for e in range(COMPS)]
            for c in range(COMPS):
                first = first_rows_ref[k, pl.ds(c * PAIRS + g, group), :].astype(jnp.float32)
                ar, ai = first[:, :BINS], first[:, BINS:]
                for e in range(COMPS):
                    br, bi = seconds[e][:, :BINS], seconds[e][:, BINS:]
                    at = c * COMPS + e
                    cross_ref[at, pl.ds(g, group), at_re] = (ar * br + ai * bi).astype(jnp.bfloat16)
                    cross_ref[at, pl.ds(g, group), at_im] = (ar * bi - ai * br).astype(jnp.bfloat16)
        return carry

    lax.fori_loop(0, RES, cross, 0, unroll=2)


def lags_kernel(distances, hour_ref, cross_ref, cosines_ref, sines_ref, moves_ref, *refs):
    *out_refs, tile_ref = refs
    hour = hour_ref[0]
    count = len(distances) + 1
    base = hour ^ distances[0]
    if count == 3:
        base = (base >> 1) * 2
    block = cross_ref[pl.ds(base, count)].reshape(count * PAIRS, 2 * NB)
    even = jnp.dot(block[:, :NB], cosines_ref[...], preferred_element_type=jnp.float32)
    odd = jnp.dot(block[:, NB:], sines_ref[...], preferred_element_type=jnp.float32)
    zero = even[:, HALF:].astype(jnp.bfloat16)
    after = jnp.concatenate([zero, (even[:, :HALF] - odd).astype(jnp.bfloat16)], axis=1)
    before = (even[:, :HALF] + odd).astype(jnp.bfloat16)
    flip, shift = moves_ref[:TILE, :], moves_ref[TILE:, :]
    per_comp, per_half = LAGS // TILE, HALF // TILE
    for tile in range(per_half):
        at = tile * TILE
        turned = jnp.dot(before[:, at : at + TILE], flip, preferred_element_type=jnp.float32).astype(jnp.bfloat16)
        moved = jnp.dot(after[:, at : at + 2 * TILE], shift, preferred_element_type=jnp.float32).astype(jnp.bfloat16)
        for c in range(count):
            of = slice(c * PAIRS, (c + 1) * PAIRS)
            tile_ref[c * per_comp + per_half - 1 - tile] = turned[of]
            tile_ref[c * per_comp + per_half + tile] = moved[of]
    for distance, out_ref in zip(distances, out_refs):
        tiles = out_ref.shape[1] // TILE
        start = (hour ^ distance) * tiles - base * per_comp
        for u in range(tiles):
            out_ref[:, u * TILE : (u + 1) * TILE] = tile_ref[start + u]


def collect_kernel(place_ref, *refs):
    *parts_refs, out_ref = refs
    total = parts_refs[0][...].astype(jnp.float32)
    for ref in parts_refs[1:]:
        total = total + ref[...].astype(jnp.float32)
    total = (total * (1.0 / 128.0)).astype(jnp.bfloat16)
    out_ref[...] = jnp.dot(place_ref[...], total, preferred_element_type=jnp.float32).astype(jnp.bfloat16)


def from_behind(value, axis, steps):
    count = lax.axis_size(axis)
    return lax.ppermute(value, axis, [(source, (source + steps) % count) for source in range(count)])


def shards(windows, pair_first, pair_second, owners):
    twiddle, common, cosines, sines, moves = (jnp.asarray(t) for t in tables())
    hours = lax.axis_size("hour")
    hour = lax.axis_index("hour").astype(jnp.int32).reshape(1)
    share = COMPS * COMPS * LAGS // hours
    slots = lax.axis_size("sens") * CAP
    bf16, f32, i32 = jnp.bfloat16, jnp.float32, jnp.int32
    rows = windows[0].transpose(1, 0, 2).reshape(ROWS, SAMPLES)
    nearer = from_behind(rows, "sens", -1)
    farther = from_behind(rows, "sens", -2)

    vmem = pl.BlockSpec(memory_space=pltpu.VMEM)
    smem = pl.BlockSpec(memory_space=pltpu.SMEM)
    hbm = pl.BlockSpec(memory_space=pltpu.HBM)
    parts_scratch = pltpu.VMEM((RES * ROWS, 2 * SPAN), f32)
    params = pltpu.CompilerParams(vmem_limit_bytes=16 * MIB)

    spectra = jax.ShapeDtypeStruct((RES, SLAB, 2 * BINS), bf16)

    def cost(flops):
        return pl.CostEstimate(flops=flops, bytes_accessed=10**6, transcendentals=0)

    own, first_rows, pick, place = pl.pallas_call(
        own_kernel,
        out_shape=(
            spectra,
            jax.ShapeDtypeStruct((RES, COMPS * PAIRS, 2 * BINS), bf16),
            jax.ShapeDtypeStruct((COMPS * PAIRS, TILE), bf16),
            jax.ShapeDtypeStruct((slots, PAIRS), bf16),
        ),
        in_specs=[hbm] * 6,
        out_specs=(vmem,) * 4,
        scratch_shapes=[
            pltpu.VMEM((ROWS, SAMPLES), bf16),
            pltpu.VMEM(twiddle.shape, f32),
            pltpu.VMEM(common.shape, bf16),
            pltpu.VMEM((1, PAIRS), i32),
            pltpu.VMEM((1, PAIRS), i32),
            pltpu.VMEM((1, PAIRS), i32),
            parts_scratch,
            pltpu.SemaphoreType.DMA((6,)),
        ],
        compiler_params=pltpu.CompilerParams(vmem_limit_bytes=56 * MIB),
        cost_estimate=cost(10**9),
        name="own",
    )(rows, twiddle, common, *(v.reshape(1, PAIRS) for v in (pair_first, pair_second, owners)))
    near = pl.pallas_call(
        nearer_kernel,
        out_shape=spectra,
        in_specs=[vmem] * 3,
        out_specs=vmem,
        scratch_shapes=[parts_scratch],
        compiler_params=params,
        cost_estimate=cost(10**9),
        name="nearer",
    )(nearer, twiddle, common)
    cross = pl.pallas_call(
        cross_kernel,
        out_shape=jax.ShapeDtypeStruct((COMPS * COMPS, PAIRS, 2 * NB), bf16),
        in_specs=[vmem] * 7,
        out_specs=vmem,
        scratch_shapes=[
            parts_scratch,
            pltpu.VMEM((RES, SLAB, 2 * BINS), bf16),
            pltpu.VMEM((COMPS * PAIRS, 2 * BINS), f32),
        ],
        compiler_params=params,
        cost_estimate=cost(3 * 10**9),
        name="cross",
    )(first_rows, own, near, farther, pick, twiddle, common)

    def lags(distances):
        one = jax.ShapeDtypeStruct((PAIRS, share), bf16)
        return pl.pallas_call(
            functools.partial(lags_kernel, distances),
            out_shape=(one,) * len(distances),
            in_specs=[smem] + [vmem] * 4,
            out_specs=(vmem,) * len(distances),
            scratch_shapes=[pltpu.VMEM((3 * LAGS // TILE, PAIRS, TILE), bf16)],
            compiler_params=params,
            cost_estimate=cost(10**9),
            name="lags",
        )(hour, cross, cosines, sines, moves)

    parts = []
    for distances in ((6, 7), (4, 5), (2, 3), (1,), (0,)):
        for distance, part in zip(distances, lags(distances)):
            if distance:
                part = lax.ppermute(part, "hour", [(h, h ^ distance) for h in range(hours)])
            parts.append(part)
    outgoing = pl.pallas_call(
        collect_kernel,
        out_shape=jax.ShapeDtypeStruct((slots, share), bf16),
        in_specs=[vmem] * (1 + hours),
        out_specs=vmem,
        compiler_params=params,
        cost_estimate=cost(2 * 10**7),
        name="collect",
    )(place, *parts)
    stacked = lax.all_to_all(outgoing, "sens", split_axis=0, concat_axis=0, tiled=True)
    return stacked.astype(jnp.float32)


def solution(mesh):
    placed = (P("hour", "sens", None, None), P("sens"), P("sens"), P("sens", None))
    return jax.shard_map(
        shards, mesh=mesh, in_specs=placed, out_specs=P("sens", "hour"), check_vma=False
    )
```

time: 66.4 us -> 65.7 us (0.989)
  local copies, waits for them, and re-layouts: 4.37 us -> 1.11 us
  blocking collectives: 18.6 us -> 21.2 us
  Pallas kernels: 16.1 us -> 17.7 us
  other arithmetic: 1.59 us -> 0 us
    unnamed x14 -> x18, local copies, waits for them, and re-layouts: 3.44 us -> 0.18 us
    all_to_all x1, blocking collectives: 18.6 us -> 21.2 us  [shards(): lax.all_to_all(outgoing, 'sens', split_axis=0, concat_axis=0, tiled=True)]
    pallas_call x3 -> x2, Pallas kernels: 4.69 us -> 6.21 us  [the longest x1 5.01 us: shards(): pl.pallas_call(own_kernel, out_shape=(spectra, jax.ShapeDtypeStruct((RES,...]
    pallas_call x5, Pallas kernels: 5.37 us -> 6.79 us  [lags(): pl.pallas_call(functools.partial(lags_kernel, distances), out_shape=(one,...]
    pallas_call x1, Pallas kernels: 5.72 us -> 4.37 us  [shards(): pl.pallas_call(cross_kernel, out_shape=jax.ShapeDtypeStruct((COMPS * COMP...]
    reduce_sum x1 -> x0, other arithmetic: 0.91 us -> none  [shards(): target = owner * CAP + jnp.sum(same.astype(jnp.int32), axis=1)]
    add x1 -> x0, other arithmetic: 0.67 us -> none  [shards(): target = owner * CAP + jnp.sum(same.astype(jnp.int32), axis=1)]
  transfers between devices with their start and end apart: 9 -> 9, of which waited for: 2 -> 2; matrix products, arithmetic and copies ran while one was open for 2% -> 0% of each run, Pallas kernels for 12% -> 15%
where the time goes in v3:
time: 65.7 us; the launch traced here: 65.5 us
  blocking collectives  21.2 us (32%)
  starting transfers between devices  20.6 us (31%)
  Pallas kernels  17.7 us (27%)
  waiting for transfers between devices  4.76 us (7%)
  local copies, waits for them, and re-layouts  1.11 us (2%)
    all_to_all x1, blocking collectives, shards(): lax.all_to_all(outgoing, 'sens', split_axis=0, concat_axis=0, tiled=True)  21.2 us
    ppermute x7, starting transfers between devices, shards(): part = lax.ppermute(part, 'hour', [(h, h ^ distance) for h in range(hours)])  12.6 us
    ppermute x2, starting transfers between devices, from_behind(): lax.ppermute(value, axis, [(source, (source + steps) % count) for source...  8.01 us
    pallas_call x5, Pallas kernels, lags(): pl.pallas_call(functools.partial(lags_kernel, distances), out_shape=(one,...  6.79 us
    pallas_call x1, Pallas kernels, shards(): pl.pallas_call(own_kernel, out_shape=(spectra, jax.ShapeDtypeStruct((RES,...  5.01 us
    ppermute x7, waiting for transfers between devices, shards(): part = lax.ppermute(part, 'hour', [(h, h ^ distance) for h in range(hours)])  4.76 us
    pallas_call x1, Pallas kernels, shards(): pl.pallas_call(cross_kernel, out_shape=jax.ShapeDtypeStruct((COMPS * COMP...  4.37 us
  transfers between devices with their start and end apart: 9, of which 2 were waited for; matrix products, arithmetic and copies ran while one was open for 0% of the time, Pallas kernels for 15%

profile of v3, /device:TPU:1, one launch (start us, length us, event | category | flops | bytes accessed | tf_op | source)
XLA Modules:
  0.0 65.5 jit_solution(2050380131482842861)
XLA Ops:
  0.0 3.2 %collective-permute-start = (bf16[24,4096]{1,0:T(8,128)(2,1)}, bf16[24,4096]{1,0:T(8,128)(2,1)S(1)}, u32[]{:S(2)}, u32[]{:S(2)}) collective-permute-start(bf16[24,4096]{1,0:T(8,128)(2,1)} %bitcast.9), channel_id=1, source_target_pairs={{0,248},{8,0},{16,8},{24,16},{32,24},{40,32},{48,40},{56,48},{64,5... | collective-permute-start | bytes 589832 | tf_op jit(solution)/shard_map/ppermute | solution.py:221
  3.2 4.8 %collective-permute-start.1 = (bf16[24,4096]{1,0:T(8,128)(2,1)}, bf16[24,4096]{1,0:T(8,128)(2,1)S(1)}, u32[]{:S(2)}, u32[]{:S(2)}) collective-permute-start(bf16[24,4096]{1,0:T(8,128)(2,1)} %bitcast.10), channel_id=1, source_target_pairs={{0,240},{8,248},{16,0},{24,8},{32,16},{40,24},{48,32},{56,40},{64,... | collective-permute-start | bytes 589832 | tf_op jit(solution)/shard_map/ppermute | solution.py:221
  8.0 5.0 %own.1 = (bf16[16,32,256]{2,1,0:T(8,128)(2,1)}, bf16[16,192,256]{2,1,0:T(8,128)(2,1)}, bf16[192,128]{1,0:T(8,128)(2,1)}, bf16[128,64]{1,0:T(8,128)(2,1)}) custom-call(bf16[24,4096]{1,0:T(8,128)(2,1)} %bitcast.11, f32[2,16,512]{2,1,0:T(8,128)} %constant.14.clone.twiddle_any.twiddle_ref, bf16[2,1024,256]{2,1,0:T(8,128)(2,1)} %constant.15.clone.common_any.common_ref, ...), custom_call_target="tpu_custom_call" | custom-call | flops 1000000000 | bytes 1000000 | tf_op jit(solution)/shard_map/own/pallas_call | solution.py:246
  13.0 0.0 copy-start.7
  13.1 0.0 collective-permute-done.rows_ref
  13.1 1.2 %nearer.1.near_ref = bf16[16,32,256]{2,1,0:T(8,128)(2,1)S(1)} custom-call(bf16[24,4096]{1,0:T(8,128)(2,1)S(1)} %collective-permute-done.rows_ref, f32[2,16,512]{2,1,0:T(8,128)S(1)} %copy-done.5, bf16[2,1024,256]{2,1,0:T(8,128)(2,1)S(1)} %copy-done.4), custom_call_target="tpu_custom_call" | custom-call | flops 1000000000 | bytes 1000000 | tf_op jit(solution)/shard_map/nearer/pallas_call | solution.py:270
  14.3 0.0 collective-permute-done.1.farther_ref
  14.3 0.1 copy-done.6
  14.4 0.0 copy-done.7
  14.5 4.4 %cross.1.cross_ref = bf16[9,64,4096]{2,1,0:T(8,128)(2,1)S(1)} custom-call(bf16[16,192,256]{2,1,0:T(8,128)(2,1)S(1)} %copy-done.6, bf16[16,32,256]{2,1,0:T(8,128)(2,1)S(1)} %copy-done.7, bf16[16,32,256]{2,1,0:T(8,128)(2,1)S(1)} %nearer.1.near_ref, bf16[24,4096]{1,0:T(8,128)(2,1)S(1)} %collective-permute-done.1.farther_ref, bf16[192,128]{1,0:T(8,128)(2,1)S(1)} %copy-done.8, ...), custom_call_target="tpu_custom_call" | custom-call | flops 3000000000 | bytes 1000000 | tf_op jit(solution)/shard_map/cross/pallas_call | solution.py:280
  18.9 1.5 %lags.6 = (bf16[64,1152]{1,0:T(8,128)(2,1)S(1)}, bf16[64,1152]{1,0:T(8,128)(2,1)S(1)}) custom-call(s32[1]{0:T(128)} %bitcast.6.hour_ref, bf16[9,64,4096]{2,1,0:T(8,128)(2,1)S(1)} %cross.1.cross_ref, bf16[2048,640]{1,0:T(8,128)(2,1)S(1)} %copy-done, bf16[2048,512]{1,0:T(8,128)(2,1)S(1)} %copy-done.1, bf16[384,128]{1,0:T(8,128)(2,1)S(1)} %copy-done.2), custom_call_target="tpu_custom_call" | custom-call | flops 1000000000 | bytes 1000000 | tf_op jit(solution)/shard_map/lags/pallas_call | solution.py:297
  20.4 1.5 %lags.7 = (bf16[64,1152]{1,0:T(8,128)(2,1)S(1)}, bf16[64,1152]{1,0:T(8,128)(2,1)S(1)}) custom-call(s32[1]{0:T(128)} %bitcast.6.hour_ref, bf16[9,64,4096]{2,1,0:T(8,128)(2,1)S(1)} %cross.1.cross_ref, bf16[2048,640]{1,0:T(8,128)(2,1)S(1)} %copy-done, bf16[2048,512]{1,0:T(8,128)(2,1)S(1)} %copy-done.1, bf16[384,128]{1,0:T(8,128)(2,1)S(1)} %copy-done.2), custom_call_target="tpu_custom_call" | custom-call | flops 1000000000 | bytes 1000000 | tf_op jit(solution)/shard_map/lags/pallas_call | solution.py:297
  21.9 2.6 %collective-permute-start.4 = (bf16[64,1152]{1,0:T(8,128)(2,1)S(1)}, bf16[64,1152]{1,0:T(8,128)(2,1)S(1)}, u32[]{:S(2)}, u32[]{:S(2)}) collective-permute-start(bf16[64,1152]{1,0:T(8,128)(2,1)S(1)} %get-tuple-element.21), channel_id=1, source_target_pairs={{0,4},{1,5},{2,6},{3,7},{4,0},{5,1},{6,2},{7,3},{8,12},{9,13},{10,... | collective-permute-start | bytes 442376 | tf_op jit(solution)/shard_map/ppermute | solution.py:312
  24.5 1.5 %collective-permute-start.5 = (bf16[64,1152]{1,0:T(8,128)(2,1)S(1)}, bf16[64,1152]{1,0:T(8,128)(2,1)S(1)}, u32[]{:S(2)}, u32[]{:S(2)}) collective-permute-start(bf16[64,1152]{1,0:T(8,128)(2,1)S(1)} %get-tuple-element.22), channel_id=1, source_target_pairs={{0,5},{1,4},{2,7},{3,6},{4,1},{5,0},{6,3},{7,2},{8,13},{9,12},{10,... | collective-permute-start | bytes 442376 | tf_op jit(solution)/shard_map/ppermute | solution.py:312
  26.0 2.6 %collective-permute-start.6 = (bf16[64,1152]{1,0:T(8,128)(2,1)S(1)}, bf16[64,1152]{1,0:T(8,128)(2,1)S(1)}, u32[]{:S(2)}, u32[]{:S(2)}) collective-permute-start(bf16[64,1152]{1,0:T(8,128)(2,1)S(1)} %get-tuple-element.23), channel_id=1, source_target_pairs={{0,2},{1,3},{2,0},{3,1},{4,6},{5,7},{6,4},{7,5},{8,10},{9,11},{10,... | collective-permute-start | bytes 442376 | tf_op jit(solution)/shard_map/ppermute | solution.py:312
  28.7 0.0 collective-permute-start.7
  28.7 1.5 %lags.5 = (bf16[64,1152]{1,0:T(8,128)(2,1)S(1)}, bf16[64,1152]{1,0:T(8,128)(2,1)S(1)}) custom-call(s32[1]{0:T(128)} %bitcast.6.hour_ref, bf16[9,64,4096]{2,1,0:T(8,128)(2,1)S(1)} %cross.1.cross_ref, bf16[2048,640]{1,0:T(8,128)(2,1)S(1)} %copy-done, bf16[2048,512]{1,0:T(8,128)(2,1)S(1)} %copy-done.1, bf16[384,128]{1,0:T(8,128)(2,1)S(1)} %copy-done.2), custom_call_target="tpu_custom_call" | custom-call | flops 1000000000 | bytes 1000000 | tf_op jit(solution)/shard_map/lags/pallas_call | solution.py:297
  30.2 4.1 %collective-permute-start.2 = (bf16[64,1152]{1,0:T(8,128)(2,1)S(1)}, bf16[64,1152]{1,0:T(8,128)(2,1)S(1)}, u32[]{:S(2)}, u32[]{:S(2)}) collective-permute-start(bf16[64,1152]{1,0:T(8,128)(2,1)S(1)} %get-tuple-element.19), channel_id=1, source_target_pairs={{0,6},{1,7},{2,4},{3,5},{4,2},{5,3},{6,0},{7,1},{8,14},{9,15},{10,... | collective-permute-start | bytes 442376 | tf_op jit(solution)/shard_map/ppermute | solution.py:312
  34.2 1.1 %lags.8 = bf16[64,1152]{1,0:T(8,128)(2,1)S(1)} custom-call(s32[1]{0:T(128)} %bitcast.6.hour_ref, bf16[9,64,4096]{2,1,0:T(8,128)(2,1)S(1)} %cross.1.cross_ref, bf16[2048,640]{1,0:T(8,128)(2,1)S(1)} %copy-done, bf16[2048,512]{1,0:T(8,128)(2,1)S(1)} %copy-done.1, bf16[384,128]{1,0:T(8,128)(2,1)S(1)} %copy-done.2), custom_call_target="tpu_custom_call" | custom-call | flops 1000000000 | bytes 1000000 | tf_op jit(solution)/shard_map/lags/pallas_call | solution.py:297
  35.4 0.0 collective-permute-done.4.refs_2_
  35.4 1.1 %collective-permute-start.3 = (bf16[64,1152]{1,0:T(8,128)(2,1)S(1)}, bf16[64,1152]{1,0:T(8,128)(2,1)S(1)}, u32[]{:S(2)}, u32[]{:S(2)}) collective-permute-start(bf16[64,1152]{1,0:T(8,128)(2,1)S(1)} %get-tuple-element.20), channel_id=1, source_target_pairs={{0,7},{1,6},{2,5},{3,4},{4,3},{5,2},{6,1},{7,0},{8,15},{9,14},{10,... | collective-permute-start | bytes 442376 | tf_op jit(solution)/shard_map/ppermute | solution.py:312
  36.5 0.0 collective-permute-done.5.refs_3_
  36.5 0.7 %collective-permute-start.8 = (bf16[64,1152]{1,0:T(8,128)(2,1)S(1)}, bf16[64,1152]{1,0:T(8,128)(2,1)S(1)}, u32[]{:S(2)}, u32[]{:S(2)}) collective-permute-start(bf16[64,1152]{1,0:T(8,128)(2,1)S(1)} %lags.8), channel_id=1, source_target_pairs={{0,1},{1,0},{2,3},{3,2},{4,5},{5,4},{6,7},{7,6},{8,9},{9,8},{10,11... | collective-permute-start | bytes 442376 | tf_op jit(solution)/shard_map/ppermute | solution.py:312
  37.2 1.1 %lags.9.refs_7_ = bf16[64,1152]{1,0:T(8,128)(2,1)S(1)} custom-call(s32[1]{0:T(128)} %bitcast.6.hour_ref, bf16[9,64,4096]{2,1,0:T(8,128)(2,1)S(1)} %cross.1.cross_ref, bf16[2048,640]{1,0:T(8,128)(2,1)S(1)} %copy-done, bf16[2048,512]{1,0:T(8,128)(2,1)S(1)} %copy-done.1, bf16[384,128]{1,0:T(8,128)(2,1)S(1)} %copy-done.2), custom_call_target="tpu_custom_call" | custom-call | flops 1000000000 | bytes 1000000 | tf_op jit(solution)/shard_map/lags/pallas_call | solution.py:297
  38.3 0.0 collective-permute-done.6.refs_4_
  38.3 0.1 collective-permute-done.2.refs_0_
  38.4 4.7 %collective-permute-done.3.refs_1_ = bf16[64,1152]{1,0:T(8,128)(2,1)S(1)} collective-permute-done((bf16[64,1152]{1,0:T(8,128)(2,1)S(1)}, bf16[64,1152]{1,0:T(8,128)(2,1)S(1)}, u32[]{:S(2)}, u32[]{:S(2)}) %collective-permute-start.3) | collective-permute-done | bytes 147488 | tf_op jit(solution)/shard_map/ppermute | solution.py:312
  43.1 0.0 collective-permute-done.8.refs_6_
  43.1 0.3 collect.1
  43.4 0.1 all_to_all.6
  43.5 21.2 %all_to_all.9 = bf16[32,4,1152]{2,1,0:T(4,128)(2,1)S(1)} all-to-all(bf16[32,4,1152]{2,1,0:T(4,128)(2,1)S(1)} %all_to_all.6), channel_id=1, replica_groups=mesh['sens'=32,'hour'=8] {'sens'}, dimensions={0} | all-to-all | bytes 589824 | tf_op jit(solution)/shard_map/all_to_all | solution.py:323
  64.7 0.9 %reshape.24 = f32[128,1152]{1,0:T(8,128)} reshape(bf16[32,4,1152]{2,1,0:T(4,128)(2,1)S(1)} %all_to_all.9) | data formatting | bytes 884736 | tf_op jit(solution)/shard_map/convert_element_type | solution.py:324
  (16 shorter events, 0.0 us)
Async XLA Ops:
  0.0 13.1 %copy-start.5 = (f32[2,16,512]{2,1,0:T(8,128)S(1)}, f32[2,16,512]{2,1,0:T(8,128)}, u32[]{:S(2)}) copy-start(f32[2,16,512]{2,1,0:T(8,128)} %constant.14.clone.twiddle_any.twiddle_ref) | copy-start | bytes 196612
  0.0 13.1 %copy-start.4 = (bf16[2,1024,256]{2,1,0:T(8,128)(2,1)S(1)}, bf16[2,1024,256]{2,1,0:T(8,128)(2,1)}, u32[]{:S(2)}) copy-start(bf16[2,1024,256]{2,1,0:T(8,128)(2,1)} %constant.15.clone.common_any.common_ref) | copy-start | bytes 3145732
  0.0 13.1 %collective-permute-start = (bf16[24,4096]{1,0:T(8,128)(2,1)}, bf16[24,4096]{1,0:T(8,128)(2,1)S(1)}, u32[]{:S(2)}, u32[]{:S(2)}) collective-permute-start(bf16[24,4096]{1,0:T(8,128)(2,1)} %bitcast.9), channel_id=1, source_target_pairs={{0,248},{8,0},{16,8},{24,16},{32,24},{40,32},{48,40},{56,48},{64,5... | collective-permute-start | bytes 589832 | tf_op jit(solution)/shard_map/ppermute | solution.py:221
  3.2 11.1 %collective-permute-start.1 = (bf16[24,4096]{1,0:T(8,128)(2,1)}, bf16[24,4096]{1,0:T(8,128)(2,1)S(1)}, u32[]{:S(2)}, u32[]{:S(2)}) collective-permute-start(bf16[24,4096]{1,0:T(8,128)(2,1)} %bitcast.10), channel_id=1, source_target_pairs={{0,240},{8,248},{16,0},{24,8},{32,16},{40,24},{48,32},{56,40},{64,... | collective-permute-start | bytes 589832 | tf_op jit(solution)/shard_map/ppermute | solution.py:221
  13.0 1.4 %copy-start.6 = (bf16[16,192,256]{2,1,0:T(8,128)(2,1)S(1)}, bf16[16,192,256]{2,1,0:T(8,128)(2,1)}, u32[]{:S(2)}) copy-start(bf16[16,192,256]{2,1,0:T(8,128)(2,1)} %get-tuple-element.16.first_rows_ref) | copy-start | bytes 4718596
  13.0 1.4 %copy-start.7 = (bf16[16,32,256]{2,1,0:T(8,128)(2,1)S(1)}, bf16[16,32,256]{2,1,0:T(8,128)(2,1)}, u32[]{:S(2)}) copy-start(bf16[16,32,256]{2,1,0:T(8,128)(2,1)} %get-tuple-element.17.own_ref) | copy-start | bytes 786436
  13.1 1.4 %copy-start.8 = (bf16[192,128]{1,0:T(8,128)(2,1)S(1)}, bf16[192,128]{1,0:T(8,128)(2,1)}, u32[]{:S(2)}) copy-start(bf16[192,128]{1,0:T(8,128)(2,1)} %get-tuple-element.18.pick_ref) | copy-start | bytes 147460
  14.5 4.4 %copy-start = (bf16[2048,640]{1,0:T(8,128)(2,1)S(1)}, bf16[2048,640]{1,0:T(8,128)(2,1)}, u32[]{:S(2)}) copy-start(bf16[2048,640]{1,0:T(8,128)(2,1)} %constant.16.clone.cosines_ref) | copy-start | bytes 7864324
  14.5 4.4 %copy-start.1 = (bf16[2048,512]{1,0:T(8,128)(2,1)S(1)}, bf16[2048,512]{1,0:T(8,128)(2,1)}, u32[]{:S(2)}) copy-start(bf16[2048,512]{1,0:T(8,128)(2,1)} %constant.17.clone.sines_ref) | copy-start | bytes 6291460
  14.5 4.4 %copy-start.2 = (bf16[384,128]{1,0:T(8,128)(2,1)S(1)}, bf16[384,128]{1,0:T(8,128)(2,1)}, u32[]{:S(2)}) copy-start(bf16[384,128]{1,0:T(8,128)(2,1)} %constant.18.clone.moves_ref) | copy-start | bytes 294916
  21.9 13.4 %collective-permute-start.4 = (bf16[64,1152]{1,0:T(8,128)(2,1)S(1)}, bf16[64,1152]{1,0:T(8,128)(2,1)S(1)}, u32[]{:S(2)}, u32[]{:S(2)}) collective-permute-start(bf16[64,1152]{1,0:T(8,128)(2,1)S(1)} %get-tuple-element.21), channel_id=1, source_target_pairs={{0,4},{1,5},{2,6},{3,7},{4,0},{5,1},{6,2},{7,3},{8,12},{9,13},{10,... | collective-permute-start | bytes 442376 | tf_op jit(solution)/shard_map/ppermute | solution.py:312
  24.5 12.0 %collective-permute-start.5 = (bf16[64,1152]{1,0:T(8,128)(2,1)S(1)}, bf16[64,1152]{1,0:T(8,128)(2,1)S(1)}, u32[]{:S(2)}, u32[]{:S(2)}) collective-permute-start(bf16[64,1152]{1,0:T(8,128)(2,1)S(1)} %get-tuple-element.22), channel_id=1, source_target_pairs={{0,5},{1,4},{2,7},{3,6},{4,1},{5,0},{6,3},{7,2},{8,13},{9,12},{10,... | collective-permute-start | bytes 442376 | tf_op jit(solution)/shard_map/ppermute | solution.py:312
  26.0 12.3 %collective-permute-start.6 = (bf16[64,1152]{1,0:T(8,128)(2,1)S(1)}, bf16[64,1152]{1,0:T(8,128)(2,1)S(1)}, u32[]{:S(2)}, u32[]{:S(2)}) collective-permute-start(bf16[64,1152]{1,0:T(8,128)(2,1)S(1)} %get-tuple-element.23), channel_id=1, source_target_pairs={{0,2},{1,3},{2,0},{3,1},{4,6},{5,7},{6,4},{7,5},{8,10},{9,11},{10,... | collective-permute-start | bytes 442376 | tf_op jit(solution)/shard_map/ppermute | solution.py:312
  28.7 9.7 %collective-permute-start.7 = (bf16[64,1152]{1,0:T(8,128)(2,1)S(1)}, bf16[64,1152]{1,0:T(8,128)(2,1)S(1)}, u32[]{:S(2)}, u32[]{:S(2)}) collective-permute-start(bf16[64,1152]{1,0:T(8,128)(2,1)S(1)} %get-tuple-element.24), channel_id=1, source_target_pairs={{0,3},{1,2},{2,1},{3,0},{4,7},{5,6},{6,5},{7,4},{8,11},{9,10},{10,... | collective-permute-start | bytes 442376 | tf_op jit(solution)/shard_map/ppermute | solution.py:312
  30.2 8.2 %collective-permute-start.2 = (bf16[64,1152]{1,0:T(8,128)(2,1)S(1)}, bf16[64,1152]{1,0:T(8,128)(2,1)S(1)}, u32[]{:S(2)}, u32[]{:S(2)}) collective-permute-start(bf16[64,1152]{1,0:T(8,128)(2,1)S(1)} %get-tuple-element.19), channel_id=1, source_target_pairs={{0,6},{1,7},{2,4},{3,5},{4,2},{5,3},{6,0},{7,1},{8,14},{9,15},{10,... | collective-permute-start | bytes 442376 | tf_op jit(solution)/shard_map/ppermute | solution.py:312
  35.4 7.7 %copy-start.3 = (bf16[128,64]{1,0:T(8,128)(2,1)S(1)}, bf16[128,64]{1,0:T(8,128)(2,1)}, u32[]{:S(2)}) copy-start(bf16[128,64]{1,0:T(8,128)(2,1)} %get-tuple-element.15.place_ref) | copy-start | bytes 49156
  35.4 7.7 %collective-permute-start.3 = (bf16[64,1152]{1,0:T(8,128)(2,1)S(1)}, bf16[64,1152]{1,0:T(8,128)(2,1)S(1)}, u32[]{:S(2)}, u32[]{:S(2)}) collective-permute-start(bf16[64,1152]{1,0:T(8,128)(2,1)S(1)} %get-tuple-element.20), channel_id=1, source_target_pairs={{0,7},{1,6},{2,5},{3,4},{4,3},{5,2},{6,1},{7,0},{8,15},{9,14},{10,... | collective-permute-start | bytes 442376 | tf_op jit(solution)/shard_map/ppermute | solution.py:312
  36.5 6.6 %collective-permute-start.8 = (bf16[64,1152]{1,0:T(8,128)(2,1)S(1)}, bf16[64,1152]{1,0:T(8,128)(2,1)S(1)}, u32[]{:S(2)}, u32[]{:S(2)}) collective-permute-start(bf16[64,1152]{1,0:T(8,128)(2,1)S(1)} %lags.8), channel_id=1, source_target_pairs={{0,1},{1,0},{2,3},{3,2},{4,5},{5,4},{6,7},{7,6},{8,9},{9,8},{10,11... | collective-permute-start | bytes 442376 | tf_op jit(solution)/shard_map/ppermute | solution.py:312

commit v4 on v3

--- a/solution.py
+++ b/solution.py
@@ -42,15 +42,10 @@
     common = np.stack([high, (exact - high.astype(np.float64)).astype(ml_dtypes.bfloat16)])
     bins = (k[:, None] + RES * q[None, :]).reshape(-1)
     angle = 2 * np.pi * ((bins[:, None] * np.arange(1, HALF + 1)[None, :]) % PADDED) / PADDED
-    cosines = np.zeros((NB, HALF + TILE))
-    cosines[:, :HALF] = np.cos(angle)
-    cosines[:, -1] = 1.0
-    cosines = cosines.astype(ml_dtypes.bfloat16)
+    cosines = np.cos(angle).astype(ml_dtypes.bfloat16)
     sines = np.sin(angle).astype(ml_dtypes.bfloat16)
-    flip = np.eye(TILE)[::-1]
-    shift = np.eye(2 * TILE)[:, TILE - 1 : 2 * TILE - 1]
-    moves = np.concatenate([flip, shift]).astype(ml_dtypes.bfloat16)
-    return twiddle, common, cosines, sines, moves
+    flip = np.eye(TILE)[::-1].astype(ml_dtypes.bfloat16)
+    return twiddle, common, cosines, sines, flip
 
 
 def forward(rows, twiddle_ref, common_ref, parts_ref, store):
@@ -141,43 +136,56 @@
     forward(rows_ref[...], twiddle_ref, common_ref, parts_ref, store)
 
 
-def nearer_kernel(rows_ref, twiddle_ref, common_ref, white_ref, parts_ref):
+def farther_kernel(rows_ref, twiddle_ref, common_ref, white_ref, parts_ref):
     def store(k, value):
         white_ref[k] = padded(value)
 
     forward(rows_ref[...], twiddle_ref, common_ref, parts_ref, store)
 
 
-def cross_kernel(first_rows_ref, own_ref, near_ref, farther_ref, pick_ref, twiddle_ref, common_ref, cross_ref,
-                 parts_ref, far_ref, second_ref):
+def cross_kernel(odd_ref, first_rows_ref, own_ref, far_ref, sibling_ref, passed_ref, pick_ref, twiddle_ref, common_ref,
+                 cross_ref, parts_ref, near_ref, rows_ref, second_ref):
+    @pl.when(odd_ref[0] == 0)
+    def _():
+        rows_ref[...] = sibling_ref[...]
+
+    @pl.when(odd_ref[0] != 0)
+    def _():
+        rows_ref[...] = passed_ref[...]
+
     def store(k, value):
-        far_ref[k] = padded(value)
-
-    forward(farther_ref[...], twiddle_ref, common_ref, parts_ref, store)
-    pick = pick_ref[...]
+        near_ref[k] = padded(value)
+
+    forward(rows_ref[...], twiddle_ref, common_ref, parts_ref, store)
+    pick = pick_ref[:, : 3 * SLAB]
     group = 16
-
-    def cross(k, carry):
-        spectra = jnp.concatenate([own_ref[k], near_ref[k], far_ref[k]], axis=0)
-        second_ref[...] = jnp.dot(pick[:, : 3 * SLAB], spectra, preferred_element_type=jnp.float32)
-        at_re = pl.ds(pl.multiple_of(k * BINS, BINS), BINS)
-        at_im = pl.ds(pl.multiple_of(NB + k * BINS, BINS), BINS)
-        for g in range(0, PAIRS, group):
-            seconds = [second_ref[e * PAIRS + g : e * PAIRS + g + group, :] for e in range(COMPS)]
-            for c in range(COMPS):
-                first = first_rows_ref[k, pl.ds(c * PAIRS + g, group), :].astype(jnp.float32)
-                ar, ai = first[:, :BINS], first[:, BINS:]
-                for e in range(COMPS):
-                    br, bi = seconds[e][:, :BINS], seconds[e][:, BINS:]
-                    at = c * COMPS + e
-                    cross_ref[at, pl.ds(g, group), at_re] = (ar * br + ai * bi).astype(jnp.bfloat16)
-                    cross_ref[at, pl.ds(g, group), at_im] = (ar * bi - ai * br).astype(jnp.bfloat16)
+    ahead = second_ref.shape[0]
+
+    def cross(step, carry):
+        for i in range(ahead):
+            k = step * ahead + i
+            spectra = jnp.concatenate([own_ref[k], near_ref[k], far_ref[k]], axis=0)
+            second_ref[i] = jnp.dot(pick, spectra, preferred_element_type=jnp.float32)
+        for i in range(ahead):
+            k = step * ahead + i
+            at_re = pl.ds(pl.multiple_of(k * BINS, BINS), BINS)
+            at_im = pl.ds(pl.multiple_of(NB + k * BINS, BINS), BINS)
+            for g in range(0, PAIRS, group):
+                seconds = [second_ref[i, e * PAIRS + g : e * PAIRS + g + group, :] for e in range(COMPS)]
+                for c in range(COMPS):
+                    first = first_rows_ref[k, pl.ds(c * PAIRS + g, group), :].astype(jnp.float32)
+                    ar, ai = first[:, :BINS], first[:, BINS:]
+                    for e in range(COMPS):
+                        br, bi = seconds[e][:, :BINS], seconds[e][:, BINS:]
+                        at = c * COMPS + e
+                        cross_ref[at, pl.ds(g, group), at_re] = (ar * br + ai * bi).astype(jnp.bfloat16)
+                        cross_ref[at, pl.ds(g, group), at_im] = (ar * bi - ai * br).astype(jnp.bfloat16)
         return carry
 
-    lax.fori_loop(0, RES, cross, 0, unroll=2)
-
-
-def lags_kernel(distances, hour_ref, cross_ref, cosines_ref, sines_ref, moves_ref, *refs):
+    lax.fori_loop(0, RES // ahead, cross, 0)
+
+
+def lags_kernel(distances, hour_ref, cross_ref, cosines_ref, sines_ref, flip_ref, *refs):
     *out_refs, tile_ref = refs
     hour = hour_ref[0]
     count = len(distances) + 1
@@ -187,19 +195,20 @@
     block = cross_ref[pl.ds(base, count)].reshape(count * PAIRS, 2 * NB)
     even = jnp.dot(block[:, :NB], cosines_ref[...], preferred_element_type=jnp.float32)
     odd = jnp.dot(block[:, NB:], sines_ref[...], preferred_element_type=jnp.float32)
-    zero = even[:, HALF:].astype(jnp.bfloat16)
-    after = jnp.concatenate([zero, (even[:, :HALF] - odd).astype(jnp.bfloat16)], axis=1)
-    before = (even[:, :HALF] + odd).astype(jnp.bfloat16)
-    flip, shift = moves_ref[:TILE, :], moves_ref[TILE:, :]
+    zero = jnp.sum(block[:, :NB].astype(jnp.float32), axis=1, keepdims=True)
+    later = pltpu.roll(even - odd, 1, axis=1)
+    first = lax.broadcasted_iota(jnp.int32, later.shape, 1) == 0
+    after = jnp.where(first, zero, later).astype(jnp.bfloat16)
+    before = (even + odd).astype(jnp.bfloat16)
     per_comp, per_half = LAGS // TILE, HALF // TILE
     for tile in range(per_half):
         at = tile * TILE
-        turned = jnp.dot(before[:, at : at + TILE], flip, preferred_element_type=jnp.float32).astype(jnp.bfloat16)
-        moved = jnp.dot(after[:, at : at + 2 * TILE], shift, preferred_element_type=jnp.float32).astype(jnp.bfloat16)
+        turned = jnp.dot(before[:, at : at + TILE], flip_ref[...], preferred_element_type=jnp.float32)
+        turned = turned.astype(jnp.bfloat16)
         for c in range(count):
             of = slice(c * PAIRS, (c + 1) * PAIRS)
             tile_ref[c * per_comp + per_half - 1 - tile] = turned[of]
-            tile_ref[c * per_comp + per_half + tile] = moved[of]
+            tile_ref[c * per_comp + per_half + tile] = after[of, at : at + TILE]
     for distance, out_ref in zip(distances, out_refs):
         tiles = out_ref.shape[1] // TILE
         start = (hour ^ distance) * tiles - base * per_comp
@@ -216,21 +225,19 @@
     out_ref[...] = jnp.dot(place_ref[...], total, preferred_element_type=jnp.float32).astype(jnp.bfloat16)
 
 
-def from_behind(value, axis, steps):
-    count = lax.axis_size(axis)
-    return lax.ppermute(value, axis, [(source, (source + steps) % count) for source in range(count)])
-
-
 def shards(windows, pair_first, pair_second, owners):
-    twiddle, common, cosines, sines, moves = (jnp.asarray(t) for t in tables())
+    twiddle, common, cosines, sines, flip = (jnp.asarray(t) for t in tables())
     hours = lax.axis_size("hour")
     hour = lax.axis_index("hour").astype(jnp.int32).reshape(1)
     share = COMPS * COMPS * LAGS // hours
     slots = lax.axis_size("sens") * CAP
     bf16, f32, i32 = jnp.bfloat16, jnp.float32, jnp.int32
     rows = windows[0].transpose(1, 0, 2).reshape(ROWS, SAMPLES)
-    nearer = from_behind(rows, "sens", -1)
-    farther = from_behind(rows, "sens", -2)
+    sens = lax.axis_size("sens")
+    swap = [(s, s ^ 1) for s in range(sens)]
+    farther = lax.ppermute(rows, "sens", [(s, (s - 2) % sens) for s in range(sens)])
+    sibling = lax.ppermute(rows, "sens", swap)
+    odd = (lax.axis_index("sens") & 1).astype(jnp.int32).reshape(1)
 
     vmem = pl.BlockSpec(memory_space=pltpu.VMEM)
     smem = pl.BlockSpec(memory_space=pltpu.SMEM)
@@ -267,30 +274,33 @@
         cost_estimate=cost(10**9),
         name="own",
     )(rows, twiddle, common, *(v.reshape(1, PAIRS) for v in (pair_first, pair_second, owners)))
-    near = pl.pallas_call(
-        nearer_kernel,
+    farther, pick = lax.optimization_barrier((farther, pick))
+    passed = lax.ppermute(farther, "sens", swap)
+    far = pl.pallas_call(
+        farther_kernel,
         out_shape=spectra,
         in_specs=[vmem] * 3,
         out_specs=vmem,
         scratch_shapes=[parts_scratch],
         compiler_params=params,
         cost_estimate=cost(10**9),
-        name="nearer",
-    )(nearer, twiddle, common)
+        name="farther",
+    )(farther, twiddle, common)
     cross = pl.pallas_call(
         cross_kernel,
         out_shape=jax.ShapeDtypeStruct((COMPS * COMPS, PAIRS, 2 * NB), bf16),
-        in_specs=[vmem] * 7,
+        in_specs=[smem] + [vmem] * 8,
         out_specs=vmem,
         scratch_shapes=[
             parts_scratch,
             pltpu.VMEM((RES, SLAB, 2 * BINS), bf16),
-            pltpu.VMEM((COMPS * PAIRS, 2 * BINS), f32),
+            pltpu.VMEM((ROWS, SAMPLES), bf16),
+            pltpu.VMEM((4, COMPS * PAIRS, 2 * BINS), f32),
         ],
         compiler_params=params,
         cost_estimate=cost(3 * 10**9),
         name="cross",
-    )(first_rows, own, near, farther, pick, twiddle, common)
+    )(odd, first_rows, own, far, sibling, passed, pick, twiddle, common)
 
     def lags(distances):
         one = jax.ShapeDtypeStruct((PAIRS, share), bf16)
@@ -303,7 +313,7 @@
             compiler_params=params,
             cost_estimate=cost(10**9),
             name="lags",
-        )(hour, cross, cosines, sines, moves)
+        )(hour, cross, cosines, sines, flip)
 
     parts = []
     for distances in ((6, 7), (4, 5), (2, 3), (1,), (0,)):

time: 65.7 us -> 65.2 us (level)
  waiting for transfers between devices: 4.76 us -> 7.57 us
  blocking collectives: 21.2 us -> 19 us
  Pallas kernels: 17.7 us -> 15.8 us
  starting transfers between devices: 20.6 us -> 21.5 us
    ppermute x7, waiting for transfers between devices: 4.76 us -> 7.39 us  [shards(): part = lax.ppermute(part, 'hour', [(h, h ^ distance) for h in range(hours)])]
    all_to_all x1, blocking collectives: 21.2 us -> 19 us  [shards(): lax.all_to_all(outgoing, 'sens', split_axis=0, concat_axis=0, tiled=True)]
    pallas_call x5, Pallas kernels: 6.79 us -> 5.41 us  [lags(): pl.pallas_call(functools.partial(lags_kernel, distances), out_shape=(one,...]
    ppermute x2 -> x3, starting transfers between devices: 8.01 us -> 8.38 us  [the longest x1 7.33 us: shards(): lax.ppermute(rows, 'sens', [(s, (s - 2) % sens) for s in range(sens)])]
  transfers between devices with their start and end apart: 9 -> 10, of which waited for: 2 -> 3; matrix products, arithmetic and copies ran while one was open for 0% -> 0% of each run, Pallas kernels for 15% -> 15%
where the time goes in v4:
time: 65.2 us; the launch traced here: 65.1 us
  starting transfers between devices  21.5 us (33%)
  blocking collectives  19 us (29%)
  Pallas kernels  15.8 us (24%)
  waiting for transfers between devices  7.57 us (12%)
  local copies, waits for them, and re-layouts  0.98 us (2%)
    all_to_all x1, blocking collectives, shards(): lax.all_to_all(outgoing, 'sens', split_axis=0, concat_axis=0, tiled=True)  19 us
    ppermute x7, starting transfers between devices, shards(): part = lax.ppermute(part, 'hour', [(h, h ^ distance) for h in range(hours)])  13.1 us
    ppermute x7, waiting for transfers between devices, shards(): part = lax.ppermute(part, 'hour', [(h, h ^ distance) for h in range(hours)])  7.39 us
    ppermute x1, starting transfers between devices, shards(): lax.ppermute(rows, 'sens', [(s, (s - 2) % sens) for s in range(sens)])  7.33 us
    pallas_call x5, Pallas kernels, lags(): pl.pallas_call(functools.partial(lags_kernel, distances), out_shape=(one,...  5.41 us
    pallas_call x1, Pallas kernels, shards(): pl.pallas_call(own_kernel, out_shape=(spectra, jax.ShapeDtypeStruct((RES,...  5.02 us
    pallas_call x1, Pallas kernels, shards(): pl.pallas_call(cross_kernel, out_shape=jax.ShapeDtypeStruct((COMPS * COMP...  3.88 us
  transfers between devices with their start and end apart: 10, of which 3 were waited for; matrix products, arithmetic and copies ran while one was open for 0% of the time, Pallas kernels for 15%

profile of v4, /device:TPU:1, one launch (start us, length us, event | category | flops | bytes accessed | tf_op | source)
XLA Modules:
  0.0 65.1 jit_solution(1353829395516388438)
XLA Ops:
  0.0 7.3 %collective-permute-start = (bf16[24,4096]{1,0:T(8,128)(2,1)}, bf16[24,4096]{1,0:T(8,128)(2,1)S(1)}, u32[]{:S(2)}, u32[]{:S(2)}) collective-permute-start(bf16[24,4096]{1,0:T(8,128)(2,1)} %bitcast.10), channel_id=1, source_target_pairs={{0,240},{8,248},{16,0},{24,8},{32,16},{40,24},{48,32},{56,40},{64,... | collective-permute-start | bytes 589832 | tf_op jit(solution)/shard_map/ppermute | solution.py:238
  7.3 1.0 %collective-permute-start.1 = (bf16[24,4096]{1,0:T(8,128)(2,1)}, bf16[24,4096]{1,0:T(8,128)(2,1)S(1)}, u32[]{:S(2)}, u32[]{:S(2)}) collective-permute-start(bf16[24,4096]{1,0:T(8,128)(2,1)} %bitcast.11), channel_id=1, source_target_pairs={{0,8},{8,0},{16,24},{24,16},{32,40},{40,32},{48,56},{56,48},{64,72... | collective-permute-start | bytes 589832 | tf_op jit(solution)/shard_map/ppermute | solution.py:239
  8.3 5.0 %own.1 = (bf16[16,32,256]{2,1,0:T(8,128)(2,1)}, bf16[16,192,256]{2,1,0:T(8,128)(2,1)}, bf16[192,128]{1,0:T(8,128)(2,1)}, bf16[128,64]{1,0:T(8,128)(2,1)}) custom-call(bf16[24,4096]{1,0:T(8,128)(2,1)} %bitcast.12, f32[2,16,512]{2,1,0:T(8,128)} %constant.21.clone.twiddle_any.twiddle_ref, bf16[2,1024,256]{2,1,0:T(8,128)(2,1)} %constant.22.clone.common_any.common_ref, ...), custom_call_target="tpu_custom_call" | custom-call | flops 1000000000 | bytes 1000000 | tf_op jit(solution)/shard_map/own/pallas_call | solution.py:253
  13.3 0.0 copy-start.7
  13.4 0.1 collective-permute-start.2
  13.5 1.2 %farther.1.far_ref = bf16[16,32,256]{2,1,0:T(8,128)(2,1)S(1)} custom-call(bf16[24,4096]{1,0:T(8,128)(2,1)S(1)} %collective-permute-done.rows_ref, f32[2,16,512]{2,1,0:T(8,128)S(1)} %copy-done.5, bf16[2,1024,256]{2,1,0:T(8,128)(2,1)S(1)} %copy-done.4), custom_call_target="tpu_custom_call" | custom-call | flops 1000000000 | bytes 1000000 | tf_op jit(solution)/shard_map/farther/pallas_call | solution.py:279
  14.7 0.0 collective-permute-done.1.sibling_ref
  14.7 0.2 collective-permute-done.2.passed_ref
  14.9 0.0 copy-start
  14.9 0.0 copy-start.1
  14.9 0.0 copy-start.2
  14.9 3.9 %cross.1.cross_ref = bf16[9,64,4096]{2,1,0:T(8,128)(2,1)S(1)} custom-call(s32[1]{0:T(128)} %bitcast.7.odd_ref, bf16[16,192,256]{2,1,0:T(8,128)(2,1)S(1)} %copy-done.6, bf16[16,32,256]{2,1,0:T(8,128)(2,1)S(1)} %copy-done.7, bf16[16,32,256]{2,1,0:T(8,128)(2,1)S(1)} %farther.1.far_ref, bf16[24,4096]{1,0:T(8,128)(2,1)S(1)} %collective-permute-done.1.sibling_ref, ...), custom_call_target="tpu_custom_call" | custom-call | flops 3000000000 | bytes 1000000 | tf_op jit(solution)/shard_map/cross/pallas_call | solution.py:289
  18.9 0.9 %lags.8 = bf16[64,1152]{1,0:T(8,128)(2,1)S(1)} custom-call(s32[1]{0:T(128)} %bitcast.6.hour_ref, bf16[9,64,4096]{2,1,0:T(8,128)(2,1)S(1)} %cross.1.cross_ref, bf16[2048,512]{1,0:T(8,128)(2,1)S(1)} %copy-done.1, bf16[2048,512]{1,0:T(8,128)(2,1)S(1)} %copy-done, bf16[128,128]{1,0:T(8,128)(2,1)S(1)} %copy-done.2), custom_call_target="tpu_custom_call" | custom-call | flops 1000000000 | bytes 1000000 | tf_op jit(solution)/shard_map/lags/pallas_call | solution.py:307
  19.8 1.2 %lags.7 = (bf16[64,1152]{1,0:T(8,128)(2,1)S(1)}, bf16[64,1152]{1,0:T(8,128)(2,1)S(1)}) custom-call(s32[1]{0:T(128)} %bitcast.6.hour_ref, bf16[9,64,4096]{2,1,0:T(8,128)(2,1)S(1)} %cross.1.cross_ref, bf16[2048,512]{1,0:T(8,128)(2,1)S(1)} %copy-done.1, bf16[2048,512]{1,0:T(8,128)(2,1)S(1)} %copy-done, bf16[128,128]{1,0:T(8,128)(2,1)S(1)} %copy-done.2), custom_call_target="tpu_custom_call" | custom-call | flops 1000000000 | bytes 1000000 | tf_op jit(solution)/shard_map/lags/pallas_call | solution.py:307
  21.0 1.4 %collective-permute-start.9 = (bf16[64,1152]{1,0:T(8,128)(2,1)S(1)}, bf16[64,1152]{1,0:T(8,128)(2,1)S(1)}, u32[]{:S(2)}, u32[]{:S(2)}) collective-permute-start(bf16[64,1152]{1,0:T(8,128)(2,1)S(1)} %lags.8), channel_id=1, source_target_pairs={{0,1},{1,0},{2,3},{3,2},{4,5},{5,4},{6,7},{7,6},{8,9},{9,8},{10,11... | collective-permute-start | bytes 442376 | tf_op jit(solution)/shard_map/ppermute | solution.py:322
  22.4 2.6 %collective-permute-start.7 = (bf16[64,1152]{1,0:T(8,128)(2,1)S(1)}, bf16[64,1152]{1,0:T(8,128)(2,1)S(1)}, u32[]{:S(2)}, u32[]{:S(2)}) collective-permute-start(bf16[64,1152]{1,0:T(8,128)(2,1)S(1)} %get-tuple-element.27), channel_id=1, source_target_pairs={{0,2},{1,3},{2,0},{3,1},{4,6},{5,7},{6,4},{7,5},{8,10},{9,11},{10,... | collective-permute-start | bytes 442376 | tf_op jit(solution)/shard_map/ppermute | solution.py:322
  25.0 1.2 %lags.6 = (bf16[64,1152]{1,0:T(8,128)(2,1)S(1)}, bf16[64,1152]{1,0:T(8,128)(2,1)S(1)}) custom-call(s32[1]{0:T(128)} %bitcast.6.hour_ref, bf16[9,64,4096]{2,1,0:T(8,128)(2,1)S(1)} %cross.1.cross_ref, bf16[2048,512]{1,0:T(8,128)(2,1)S(1)} %copy-done.1, bf16[2048,512]{1,0:T(8,128)(2,1)S(1)} %copy-done, bf16[128,128]{1,0:T(8,128)(2,1)S(1)} %copy-done.2), custom_call_target="tpu_custom_call" | custom-call | flops 1000000000 | bytes 1000000 | tf_op jit(solution)/shard_map/lags/pallas_call | solution.py:307
  26.2 2.5 %collective-permute-start.5 = (bf16[64,1152]{1,0:T(8,128)(2,1)S(1)}, bf16[64,1152]{1,0:T(8,128)(2,1)S(1)}, u32[]{:S(2)}, u32[]{:S(2)}) collective-permute-start(bf16[64,1152]{1,0:T(8,128)(2,1)S(1)} %get-tuple-element.25), channel_id=1, source_target_pairs={{0,4},{1,5},{2,6},{3,7},{4,0},{5,1},{6,2},{7,3},{8,12},{9,13},{10,... | collective-permute-start | bytes 442376 | tf_op jit(solution)/shard_map/ppermute | solution.py:322
  28.7 0.3 collective-permute-start.6
  29.0 1.2 %lags.5 = (bf16[64,1152]{1,0:T(8,128)(2,1)S(1)}, bf16[64,1152]{1,0:T(8,128)(2,1)S(1)}) custom-call(s32[1]{0:T(128)} %bitcast.6.hour_ref, bf16[9,64,4096]{2,1,0:T(8,128)(2,1)S(1)} %cross.1.cross_ref, bf16[2048,512]{1,0:T(8,128)(2,1)S(1)} %copy-done.1, bf16[2048,512]{1,0:T(8,128)(2,1)S(1)} %copy-done, bf16[128,128]{1,0:T(8,128)(2,1)S(1)} %copy-done.2), custom_call_target="tpu_custom_call" | custom-call | flops 1000000000 | bytes 1000000 | tf_op jit(solution)/shard_map/lags/pallas_call | solution.py:307
  30.2 6.1 %collective-permute-start.3 = (bf16[64,1152]{1,0:T(8,128)(2,1)S(1)}, bf16[64,1152]{1,0:T(8,128)(2,1)S(1)}, u32[]{:S(2)}, u32[]{:S(2)}) collective-permute-start(bf16[64,1152]{1,0:T(8,128)(2,1)S(1)} %get-tuple-element.23), channel_id=1, source_target_pairs={{0,6},{1,7},{2,4},{3,5},{4,2},{5,3},{6,0},{7,1},{8,14},{9,15},{10,... | collective-permute-start | bytes 442376 | tf_op jit(solution)/shard_map/ppermute | solution.py:322
  36.3 0.0 collective-permute-done.7.refs_4_
  36.3 0.3 collective-permute-start.4
  36.6 0.9 %lags.9.refs_7_ = bf16[64,1152]{1,0:T(8,128)(2,1)S(1)} custom-call(s32[1]{0:T(128)} %bitcast.6.hour_ref, bf16[9,64,4096]{2,1,0:T(8,128)(2,1)S(1)} %cross.1.cross_ref, bf16[2048,512]{1,0:T(8,128)(2,1)S(1)} %copy-done.1, bf16[2048,512]{1,0:T(8,128)(2,1)S(1)} %copy-done, bf16[128,128]{1,0:T(8,128)(2,1)S(1)} %copy-done.2), custom_call_target="tpu_custom_call" | custom-call | flops 1000000000 | bytes 1000000 | tf_op jit(solution)/shard_map/lags/pallas_call | solution.py:307
  37.5 0.0 collective-permute-done.8.refs_5_
  37.5 0.0 collective-permute-done.5.refs_2_
  37.5 2.8 %collective-permute-done.3.refs_0_ = bf16[64,1152]{1,0:T(8,128)(2,1)S(1)} collective-permute-done((bf16[64,1152]{1,0:T(8,128)(2,1)S(1)}, bf16[64,1152]{1,0:T(8,128)(2,1)S(1)}, u32[]{:S(2)}, u32[]{:S(2)}) %collective-permute-start.3) | collective-permute-done | bytes 147488 | tf_op jit(solution)/shard_map/ppermute | solution.py:322
  40.3 4.6 %collective-permute-done.4.refs_1_ = bf16[64,1152]{1,0:T(8,128)(2,1)S(1)} collective-permute-done((bf16[64,1152]{1,0:T(8,128)(2,1)S(1)}, bf16[64,1152]{1,0:T(8,128)(2,1)S(1)}, u32[]{:S(2)}, u32[]{:S(2)}) %collective-permute-start.4) | collective-permute-done | bytes 147488 | tf_op jit(solution)/shard_map/ppermute | solution.py:322
  44.9 0.3 collect.1
  45.2 0.1 all_to_all.6
  45.3 19.0 %all_to_all.9 = bf16[32,4,1152]{2,1,0:T(4,128)(2,1)S(1)} all-to-all(bf16[32,4,1152]{2,1,0:T(4,128)(2,1)S(1)} %all_to_all.6), channel_id=1, replica_groups=mesh['sens'=32,'hour'=8] {'sens'}, dimensions={0} | all-to-all | bytes 589824 | tf_op jit(solution)/shard_map/all_to_all | solution.py:333
  64.2 0.9 %reshape.28 = f32[128,1152]{1,0:T(8,128)} reshape(bf16[32,4,1152]{2,1,0:T(4,128)(2,1)S(1)} %all_to_all.9) | data formatting | bytes 884736 | tf_op jit(solution)/shard_map/convert_element_type | solution.py:334
  (18 shorter events, 0.0 us)
Async XLA Ops:
  0.0 13.5 %copy-start.4 = (bf16[2,1024,256]{2,1,0:T(8,128)(2,1)S(1)}, bf16[2,1024,256]{2,1,0:T(8,128)(2,1)}, u32[]{:S(2)}) copy-start(bf16[2,1024,256]{2,1,0:T(8,128)(2,1)} %constant.22.clone.common_any.common_ref) | copy-start | bytes 3145732
  0.0 13.5 %copy-start.5 = (f32[2,16,512]{2,1,0:T(8,128)S(1)}, f32[2,16,512]{2,1,0:T(8,128)}, u32[]{:S(2)}) copy-start(f32[2,16,512]{2,1,0:T(8,128)} %constant.21.clone.twiddle_any.twiddle_ref) | copy-start | bytes 196612
  0.0 13.3 %collective-permute-start = (bf16[24,4096]{1,0:T(8,128)(2,1)}, bf16[24,4096]{1,0:T(8,128)(2,1)S(1)}, u32[]{:S(2)}, u32[]{:S(2)}) collective-permute-start(bf16[24,4096]{1,0:T(8,128)(2,1)} %bitcast.10), channel_id=1, source_target_pairs={{0,240},{8,248},{16,0},{24,8},{32,16},{40,24},{48,32},{56,40},{64,... | collective-permute-start | bytes 589832 | tf_op jit(solution)/shard_map/ppermute | solution.py:238
  7.3 7.4 %collective-permute-start.1 = (bf16[24,4096]{1,0:T(8,128)(2,1)}, bf16[24,4096]{1,0:T(8,128)(2,1)S(1)}, u32[]{:S(2)}, u32[]{:S(2)}) collective-permute-start(bf16[24,4096]{1,0:T(8,128)(2,1)} %bitcast.11), channel_id=1, source_target_pairs={{0,8},{8,0},{16,24},{24,16},{32,40},{40,32},{48,56},{56,48},{64,72... | collective-permute-start | bytes 589832 | tf_op jit(solution)/shard_map/ppermute | solution.py:239
  13.3 1.6 %copy-start.6 = (bf16[16,192,256]{2,1,0:T(8,128)(2,1)S(1)}, bf16[16,192,256]{2,1,0:T(8,128)(2,1)}, u32[]{:S(2)}) copy-start(bf16[16,192,256]{2,1,0:T(8,128)(2,1)} %get-tuple-element.18.first_rows_ref) | copy-start | bytes 4718596
  13.3 1.6 %copy-start.7 = (bf16[16,32,256]{2,1,0:T(8,128)(2,1)S(1)}, bf16[16,32,256]{2,1,0:T(8,128)(2,1)}, u32[]{:S(2)}) copy-start(bf16[16,32,256]{2,1,0:T(8,128)(2,1)} %get-tuple-element.19.own_ref) | copy-start | bytes 786436
  13.4 1.5 %collective-permute-start.2 = (bf16[24,4096]{1,0:T(8,128)(2,1)S(1)}, bf16[24,4096]{1,0:T(8,128)(2,1)S(1)}, u32[]{:S(2)}, u32[]{:S(2)}) collective-permute-start(bf16[24,4096]{1,0:T(8,128)(2,1)S(1)} %collective-permute-done.rows_ref), channel_id=1, source_target_pairs={{0,8},{8,0},{16,24},{24,16},{32,40},{40,32},{48,56},{56,48},{64,72... | collective-permute-start | bytes 589832 | tf_op jit(solution)/shard_map/ppermute | solution.py:278
  13.5 1.4 %copy-start.8 = (bf16[192,128]{1,0:T(8,128)(2,1)S(1)}, bf16[192,128]{1,0:T(8,128)(2,1)}, u32[]{:S(2)}) copy-start(bf16[192,128]{1,0:T(8,128)(2,1)} %get-tuple-element.22.pick_ref) | copy-start | bytes 147460
  14.9 3.9 %copy-start = (bf16[2048,512]{1,0:T(8,128)(2,1)S(1)}, bf16[2048,512]{1,0:T(8,128)(2,1)}, u32[]{:S(2)}) copy-start(bf16[2048,512]{1,0:T(8,128)(2,1)} %constant.24.clone.sines_ref) | copy-start | bytes 6291460
  14.9 3.9 %copy-start.1 = (bf16[2048,512]{1,0:T(8,128)(2,1)S(1)}, bf16[2048,512]{1,0:T(8,128)(2,1)}, u32[]{:S(2)}) copy-start(bf16[2048,512]{1,0:T(8,128)(2,1)} %constant.23.clone.cosines_ref) | copy-start | bytes 6291460
  14.9 3.9 %copy-start.2 = (bf16[128,128]{1,0:T(8,128)(2,1)S(1)}, bf16[128,128]{1,0:T(8,128)(2,1)}, u32[]{:S(2)}) copy-start(bf16[128,128]{1,0:T(8,128)(2,1)} %constant.25.clone.flip_ref) | copy-start | bytes 98308
  21.0 9.2 %collective-permute-start.9 = (bf16[64,1152]{1,0:T(8,128)(2,1)S(1)}, bf16[64,1152]{1,0:T(8,128)(2,1)S(1)}, u32[]{:S(2)}, u32[]{:S(2)}) collective-permute-start(bf16[64,1152]{1,0:T(8,128)(2,1)S(1)} %lags.8), channel_id=1, source_target_pairs={{0,1},{1,0},{2,3},{3,2},{4,5},{5,4},{6,7},{7,6},{8,9},{9,8},{10,11... | collective-permute-start | bytes 442376 | tf_op jit(solution)/shard_map/ppermute | solution.py:322
  22.4 13.9 %collective-permute-start.7 = (bf16[64,1152]{1,0:T(8,128)(2,1)S(1)}, bf16[64,1152]{1,0:T(8,128)(2,1)S(1)}, u32[]{:S(2)}, u32[]{:S(2)}) collective-permute-start(bf16[64,1152]{1,0:T(8,128)(2,1)S(1)} %get-tuple-element.27), channel_id=1, source_target_pairs={{0,2},{1,3},{2,0},{3,1},{4,6},{5,7},{6,4},{7,5},{8,10},{9,11},{10,... | collective-permute-start | bytes 442376 | tf_op jit(solution)/shard_map/ppermute | solution.py:322
  25.0 12.5 %collective-permute-start.8 = (bf16[64,1152]{1,0:T(8,128)(2,1)S(1)}, bf16[64,1152]{1,0:T(8,128)(2,1)S(1)}, u32[]{:S(2)}, u32[]{:S(2)}) collective-permute-start(bf16[64,1152]{1,0:T(8,128)(2,1)S(1)} %get-tuple-element.28), channel_id=1, source_target_pairs={{0,3},{1,2},{2,1},{3,0},{4,7},{5,6},{6,5},{7,4},{8,11},{9,10},{10,... | collective-permute-start | bytes 442376 | tf_op jit(solution)/shard_map/ppermute | solution.py:322
  26.2 11.3 %collective-permute-start.5 = (bf16[64,1152]{1,0:T(8,128)(2,1)S(1)}, bf16[64,1152]{1,0:T(8,128)(2,1)S(1)}, u32[]{:S(2)}, u32[]{:S(2)}) collective-permute-start(bf16[64,1152]{1,0:T(8,128)(2,1)S(1)} %get-tuple-element.25), channel_id=1, source_target_pairs={{0,4},{1,5},{2,6},{3,7},{4,0},{5,1},{6,2},{7,3},{8,12},{9,13},{10,... | collective-permute-start | bytes 442376 | tf_op jit(solution)/shard_map/ppermute | solution.py:322
  28.7 8.8 %collective-permute-start.6 = (bf16[64,1152]{1,0:T(8,128)(2,1)S(1)}, bf16[64,1152]{1,0:T(8,128)(2,1)S(1)}, u32[]{:S(2)}, u32[]{:S(2)}) collective-permute-start(bf16[64,1152]{1,0:T(8,128)(2,1)S(1)} %get-tuple-element.26), channel_id=1, source_target_pairs={{0,5},{1,4},{2,7},{3,6},{4,1},{5,0},{6,3},{7,2},{8,13},{9,12},{10,... | collective-permute-start | bytes 442376 | tf_op jit(solution)/shard_map/ppermute | solution.py:322
  30.2 10.1 %collective-permute-start.3 = (bf16[64,1152]{1,0:T(8,128)(2,1)S(1)}, bf16[64,1152]{1,0:T(8,128)(2,1)S(1)}, u32[]{:S(2)}, u32[]{:S(2)}) collective-permute-start(bf16[64,1152]{1,0:T(8,128)(2,1)S(1)} %get-tuple-element.23), channel_id=1, source_target_pairs={{0,6},{1,7},{2,4},{3,5},{4,2},{5,3},{6,0},{7,1},{8,14},{9,15},{10,... | collective-permute-start | bytes 442376 | tf_op jit(solution)/shard_map/ppermute | solution.py:322
  36.3 8.6 %copy-start.3 = (bf16[128,64]{1,0:T(8,128)(2,1)S(1)}, bf16[128,64]{1,0:T(8,128)(2,1)}, u32[]{:S(2)}) copy-start(bf16[128,64]{1,0:T(8,128)(2,1)} %get-tuple-element.17.place_ref) | copy-start | bytes 49156
  36.3 8.6 %collective-permute-start.4 = (bf16[64,1152]{1,0:T(8,128)(2,1)S(1)}, bf16[64,1152]{1,0:T(8,128)(2,1)S(1)}, u32[]{:S(2)}, u32[]{:S(2)}) collective-permute-start(bf16[64,1152]{1,0:T(8,128)(2,1)S(1)} %get-tuple-element.24), channel_id=1, source_target_pairs={{0,7},{1,6},{2,5},{3,4},{4,3},{5,2},{6,1},{7,0},{8,15},{9,14},{10,... | collective-permute-start | bytes 442376 | tf_op jit(solution)/shard_map/ppermute | solution.py:322

commit v5 on v4

--- a/solution.py
+++ b/solution.py
@@ -24,6 +24,7 @@
 ROWS = COMPS * SENSORS
 SLAB = 32
 HALF = LAGS // 2
+PICKED = COMPS * PAIRS
 TILE = 128
 MIB = 1 << 20
 
@@ -107,7 +108,7 @@
 
 
 def own_kernel(rows_any, twiddle_any, common_any, first_any, second_any, owner_any,
-               white_ref, first_rows_ref, pick_ref, place_ref,
+               kept_ref, place_ref,
                rows_ref, twiddle_ref, common_ref, first_ref, second_ref, owner_ref, parts_ref, sems):
     sources = (rows_any, twiddle_any, common_any, first_any, second_any, owner_any)
     targets = (rows_ref, twiddle_ref, common_ref, first_ref, second_ref, owner_ref)
@@ -125,13 +126,15 @@
     place_ref[...] = one_hot([owner * CAP + slot], place_ref.shape[0]).astype(jnp.bfloat16)
     second = second_ref[...]
     second = second + (second >> 3) * (SLAB - SENSORS)
-    pick_ref[...] = one_hot([second + c * SENSORS for c in range(COMPS)], TILE).T.astype(jnp.bfloat16)
+    kept_ref[RES] = jnp.zeros(kept_ref.shape[1:], jnp.bfloat16)
+    kept_ref[RES, pl.ds(0, PICKED), pl.ds(0, TILE)] = one_hot([second + c * SENSORS for c in range(COMPS)], TILE).T.astype(jnp.bfloat16)
     pick_first = one_hot([first_ref[...] + c * SENSORS for c in range(COMPS)], TILE).T.astype(jnp.bfloat16)[:, :SLAB]
 
     def store(k, value):
         value = padded(value)
-        white_ref[k] = value
-        first_rows_ref[k] = jnp.dot(pick_first, value, preferred_element_type=jnp.float32).astype(jnp.bfloat16)
+        kept_ref[k, pl.ds(PICKED, SLAB), :] = value
+        first = jnp.dot(pick_first, value, preferred_element_type=jnp.float32)
+        kept_ref[k, pl.ds(0, PICKED), :] = first.astype(jnp.bfloat16)
 
     forward(rows_ref[...], twiddle_ref, common_ref, parts_ref, store)
 
@@ -143,62 +146,37 @@
     forward(rows_ref[...], twiddle_ref, common_ref, parts_ref, store)
 
 
-def cross_kernel(odd_ref, first_rows_ref, own_ref, far_ref, sibling_ref, passed_ref, pick_ref, twiddle_ref, common_ref,
-                 cross_ref, parts_ref, near_ref, rows_ref, second_ref):
-    @pl.when(odd_ref[0] == 0)
-    def _():
-        rows_ref[...] = sibling_ref[...]
-
-    @pl.when(odd_ref[0] != 0)
-    def _():
-        rows_ref[...] = passed_ref[...]
-
-    def store(k, value):
-        near_ref[k] = padded(value)
-
-    forward(rows_ref[...], twiddle_ref, common_ref, parts_ref, store)
-    pick = pick_ref[:, : 3 * SLAB]
+def shares(distances, hour, kept_ref, second_rows_ref, cosines_ref, sines_ref, flip_ref, out_refs, cross_ref, tile_ref):
+    count = cross_ref.shape[0]
+    base = ((hour ^ distances[0]) >> 2) * (count - 1)
+    comps = [base + i for i in range(count)]
+    firsts = [lax.div(i, COMPS) for i in comps]
+    seconds = [i - f * COMPS for i, f in zip(comps, firsts)]
     group = 16
-    ahead = second_ref.shape[0]
-
-    def cross(step, carry):
-        for i in range(ahead):
-            k = step * ahead + i
-            spectra = jnp.concatenate([own_ref[k], near_ref[k], far_ref[k]], axis=0)
-            second_ref[i] = jnp.dot(pick, spectra, preferred_element_type=jnp.float32)
-        for i in range(ahead):
-            k = step * ahead + i
-            at_re = pl.ds(pl.multiple_of(k * BINS, BINS), BINS)
-            at_im = pl.ds(pl.multiple_of(NB + k * BINS, BINS), BINS)
+
+    def cross(k, carry):
+        at_re = pl.ds(pl.multiple_of(k * BINS, BINS), BINS)
+        at_im = pl.ds(pl.multiple_of(NB + k * BINS, BINS), BINS)
+        for i in range(count):
             for g in range(0, PAIRS, group):
-                seconds = [second_ref[i, e * PAIRS + g : e * PAIRS + g + group, :] for e in range(COMPS)]
-                for c in range(COMPS):
-                    first = first_rows_ref[k, pl.ds(c * PAIRS + g, group), :].astype(jnp.float32)
-                    ar, ai = first[:, :BINS], first[:, BINS:]
-                    for e in range(COMPS):
-                        br, bi = seconds[e][:, :BINS], seconds[e][:, BINS:]
-                        at = c * COMPS + e
-                        cross_ref[at, pl.ds(g, group), at_re] = (ar * br + ai * bi).astype(jnp.bfloat16)
-                        cross_ref[at, pl.ds(g, group), at_im] = (ar * bi - ai * br).astype(jnp.bfloat16)
+                first_at = pl.ds(pl.multiple_of(firsts[i] * PAIRS + g, group), group)
+                second_at = pl.ds(pl.multiple_of(seconds[i] * PAIRS + g, group), group)
+                first = kept_ref[k, first_at, :].astype(jnp.float32)
+                second = second_rows_ref[k, second_at, :].astype(jnp.float32)
+                ar, ai = first[:, :BINS], first[:, BINS:]
+                br, bi = second[:, :BINS], second[:, BINS:]
+                cross_ref[i, pl.ds(g, group), at_re] = (ar * br + ai * bi).astype(jnp.bfloat16)
+                cross_ref[i, pl.ds(g, group), at_im] = (ar * bi - ai * br).astype(jnp.bfloat16)
         return carry
 
-    lax.fori_loop(0, RES // ahead, cross, 0)
-
-
-def lags_kernel(distances, hour_ref, cross_ref, cosines_ref, sines_ref, flip_ref, *refs):
-    *out_refs, tile_ref = refs
-    hour = hour_ref[0]
-    count = len(distances) + 1
-    base = hour ^ distances[0]
-    if count == 3:
-        base = (base >> 1) * 2
-    block = cross_ref[pl.ds(base, count)].reshape(count * PAIRS, 2 * NB)
+    lax.fori_loop(0, RES, cross, 0)
+    block = cross_ref[...].reshape(count * PAIRS, 2 * NB)
     even = jnp.dot(block[:, :NB], cosines_ref[...], preferred_element_type=jnp.float32)
     odd = jnp.dot(block[:, NB:], sines_ref[...], preferred_element_type=jnp.float32)
     zero = jnp.sum(block[:, :NB].astype(jnp.float32), axis=1, keepdims=True)
     later = pltpu.roll(even - odd, 1, axis=1)
-    first = lax.broadcasted_iota(jnp.int32, later.shape, 1) == 0
-    after = jnp.where(first, zero, later).astype(jnp.bfloat16)
+    start = lax.broadcasted_iota(jnp.int32, later.shape, 1) == 0
+    after = jnp.where(start, zero, later).astype(jnp.bfloat16)
     before = (even + odd).astype(jnp.bfloat16)
     per_comp, per_half = LAGS // TILE, HALF // TILE
     for tile in range(per_half):
@@ -211,9 +189,40 @@
             tile_ref[c * per_comp + per_half + tile] = after[of, at : at + TILE]
     for distance, out_ref in zip(distances, out_refs):
         tiles = out_ref.shape[1] // TILE
-        start = (hour ^ distance) * tiles - base * per_comp
+        begin = (hour ^ distance) * tiles - base * per_comp
         for u in range(tiles):
-            out_ref[:, u * TILE : (u + 1) * TILE] = tile_ref[start + u]
+            out_ref[:, u * TILE : (u + 1) * TILE] = tile_ref[begin + u]
+
+
+def across_kernel(distances, where_ref, kept_ref, far_ref, sibling_ref, passed_ref, twiddle_ref, common_ref,
+                  cosines_ref, sines_ref, flip_ref, *refs):
+    *out_refs, second_rows_ref, cross_ref, tile_ref, parts_ref, near_ref, rows_ref = refs
+
+    @pl.when(where_ref[1] == 0)
+    def _():
+        rows_ref[...] = sibling_ref[...]
+
+    @pl.when(where_ref[1] != 0)
+    def _():
+        rows_ref[...] = passed_ref[...]
+
+    def store(k, value):
+        near_ref[k] = padded(value)
+
+    forward(rows_ref[...], twiddle_ref, common_ref, parts_ref, store)
+    pick = kept_ref[RES, pl.ds(0, PICKED), pl.ds(0, TILE)][:, : 3 * SLAB]
+    for k in range(RES):
+        spectra = jnp.concatenate([kept_ref[k, pl.ds(PICKED, SLAB), :], near_ref[k], far_ref[k]], axis=0)
+        second = jnp.dot(pick, spectra, preferred_element_type=jnp.float32)
+        second_rows_ref[k] = second.astype(jnp.bfloat16)
+    shares(distances, where_ref[0], kept_ref, second_rows_ref, cosines_ref, sines_ref, flip_ref, out_refs, cross_ref,
+           tile_ref)
+
+
+def along_kernel(distances, where_ref, kept_ref, second_rows_ref, cosines_ref, sines_ref, flip_ref, *refs):
+    *out_refs, cross_ref, tile_ref = refs
+    shares(distances, where_ref[0], kept_ref, second_rows_ref, cosines_ref, sines_ref, flip_ref, out_refs, cross_ref,
+           tile_ref)
 
 
 def collect_kernel(place_ref, *refs):
@@ -228,7 +237,6 @@
 def shards(windows, pair_first, pair_second, owners):
     twiddle, common, cosines, sines, flip = (jnp.asarray(t) for t in tables())
     hours = lax.axis_size("hour")
-    hour = lax.axis_index("hour").astype(jnp.int32).reshape(1)
     share = COMPS * COMPS * LAGS // hours
     slots = lax.axis_size("sens") * CAP
     bf16, f32, i32 = jnp.bfloat16, jnp.float32, jnp.int32
@@ -237,7 +245,7 @@
     swap = [(s, s ^ 1) for s in range(sens)]
     farther = lax.ppermute(rows, "sens", [(s, (s - 2) % sens) for s in range(sens)])
     sibling = lax.ppermute(rows, "sens", swap)
-    odd = (lax.axis_index("sens") & 1).astype(jnp.int32).reshape(1)
+    where = jnp.stack([lax.axis_index("hour"), lax.axis_index("sens") & 1]).astype(jnp.int32)
 
     vmem = pl.BlockSpec(memory_space=pltpu.VMEM)
     smem = pl.BlockSpec(memory_space=pltpu.SMEM)
@@ -250,16 +258,14 @@
     def cost(flops):
         return pl.CostEstimate(flops=flops, bytes_accessed=10**6, transcendentals=0)
 
-    own, first_rows, pick, place = pl.pallas_call(
+    kept, place = pl.pallas_call(
         own_kernel,
         out_shape=(
-            spectra,
-            jax.ShapeDtypeStruct((RES, COMPS * PAIRS, 2 * BINS), bf16),
-            jax.ShapeDtypeStruct((COMPS * PAIRS, TILE), bf16),
-            jax.ShapeDtypeStruct((slots, PAIRS), bf16),
+            pltpu.VMEM((RES + 1, PICKED + SLAB, 2 * BINS), bf16),
+            pltpu.VMEM((slots, PAIRS), bf16),
         ),
         in_specs=[hbm] * 6,
-        out_specs=(vmem,) * 4,
+        out_specs=(vmem,) * 2,
         scratch_shapes=[
             pltpu.VMEM((ROWS, SAMPLES), bf16),
             pltpu.VMEM(twiddle.shape, f32),
@@ -274,7 +280,7 @@
         cost_estimate=cost(10**9),
         name="own",
     )(rows, twiddle, common, *(v.reshape(1, PAIRS) for v in (pair_first, pair_second, owners)))
-    farther, pick = lax.optimization_barrier((farther, pick))
+    farther, place = lax.optimization_barrier((farther, place))
     passed = lax.ppermute(farther, "sens", swap)
     far = pl.pallas_call(
         farther_kernel,
@@ -286,41 +292,36 @@
         cost_estimate=cost(10**9),
         name="farther",
     )(farther, twiddle, common)
-    cross = pl.pallas_call(
-        cross_kernel,
-        out_shape=jax.ShapeDtypeStruct((COMPS * COMPS, PAIRS, 2 * NB), bf16),
-        in_specs=[smem] + [vmem] * 8,
-        out_specs=vmem,
-        scratch_shapes=[
-            parts_scratch,
-            pltpu.VMEM((RES, SLAB, 2 * BINS), bf16),
-            pltpu.VMEM((ROWS, SAMPLES), bf16),
-            pltpu.VMEM((4, COMPS * PAIRS, 2 * BINS), f32),
-        ],
-        compiler_params=params,
+    one = jax.ShapeDtypeStruct((PAIRS, share), bf16)
+    half = COMPS * COMPS // 2 + 1
+    shares_scratch = [pltpu.VMEM((half, PAIRS, 2 * NB), bf16), pltpu.VMEM((half * LAGS // TILE, PAIRS, TILE), bf16)]
+    big = pltpu.CompilerParams(vmem_limit_bytes=24 * MIB)
+    other, same = (7, 6, 5, 4), (3, 2, 1, 0)
+    *across, second_rows = pl.pallas_call(
+        functools.partial(across_kernel, other),
+        out_shape=(one,) * 4 + (jax.ShapeDtypeStruct((RES, PICKED, 2 * BINS), bf16),),
+        in_specs=[smem] + [vmem] * 9,
+        out_specs=(vmem,) * 5,
+        scratch_shapes=shares_scratch + [parts_scratch, pltpu.VMEM((RES, SLAB, 2 * BINS), bf16), pltpu.VMEM((ROWS, SAMPLES), bf16)],
+        compiler_params=big,
         cost_estimate=cost(3 * 10**9),
-        name="cross",
-    )(odd, first_rows, own, far, sibling, passed, pick, twiddle, common)
-
-    def lags(distances):
-        one = jax.ShapeDtypeStruct((PAIRS, share), bf16)
-        return pl.pallas_call(
-            functools.partial(lags_kernel, distances),
-            out_shape=(one,) * len(distances),
-            in_specs=[smem] + [vmem] * 4,
-            out_specs=(vmem,) * len(distances),
-            scratch_shapes=[pltpu.VMEM((3 * LAGS // TILE, PAIRS, TILE), bf16)],
-            compiler_params=params,
-            cost_estimate=cost(10**9),
-            name="lags",
-        )(hour, cross, cosines, sines, flip)
-
+        name="across",
+    )(where, kept, far, sibling, passed, twiddle, common, cosines, sines, flip)
+    along = pl.pallas_call(
+        functools.partial(along_kernel, same),
+        out_shape=(one,) * 4,
+        in_specs=[smem] + [vmem] * 5,
+        out_specs=(vmem,) * 4,
+        scratch_shapes=shares_scratch,
+        compiler_params=big,
+        cost_estimate=cost(3 * 10**9),
+        name="along",
+    )(where, kept, second_rows, cosines, sines, flip)
     parts = []
-    for distances in ((6, 7), (4, 5), (2, 3), (1,), (0,)):
-        for distance, part in zip(distances, lags(distances)):
-            if distance:
-                part = lax.ppermute(part, "hour", [(h, h ^ distance) for h in range(hours)])
-            parts.append(part)
+    for distance, part in zip(other + same, [*across, *along]):
+        if distance:
+            part = lax.ppermute(part, "hour", [(h, h ^ distance) for h in range(hours)])
+        parts.append(part)
     outgoing = pl.pallas_call(
         collect_kernel,
         out_shape=jax.ShapeDtypeStruct((slots, share), bf16),

time: 65.2 us -> 64.3 us (0.986)
  blocking collectives: 19 us -> 21.2 us
  waiting for transfers between devices: 7.57 us -> 5.74 us
  starting transfers between devices: 21.5 us -> 20.7 us
    all_to_all x1, blocking collectives: 19 us -> 21.2 us  [shards(): lax.all_to_all(outgoing, 'sens', split_axis=0, concat_axis=0, tiled=True)]
    ppermute x7, waiting for transfers between devices: 7.39 us -> 5.73 us  [shards(): part = lax.ppermute(part, 'hour', [(h, h ^ distance) for h in range(hours)])]
    ppermute x7, starting transfers between devices: 13.1 us -> 11.9 us  [shards(): part = lax.ppermute(part, 'hour', [(h, h ^ distance) for h in range(hours)])]
    pallas_call x7 -> x3, Pallas kernels: 14.3 us -> 14 us  [the longest x1 6.28 us: shards(): pl.pallas_call(functools.partial(across_kernel, other), out_shape=(one,)...]
  transfers between devices with their start and end apart: 10 -> 10, of which waited for: 3 -> 3; matrix products, arithmetic and copies ran while one was open for 0% -> 0% of each run, Pallas kernels for 15% -> 14%
where the time goes in v5:
time: 64.3 us; the launch traced here: 64.2 us
  blocking collectives  21.2 us (33%)
  starting transfers between devices  20.7 us (32%)
  Pallas kernels  15.5 us (24%)
  waiting for transfers between devices  5.74 us (9%)
  local copies, waits for them, and re-layouts  0.96 us (1%)
    all_to_all x1, blocking collectives, shards(): lax.all_to_all(outgoing, 'sens', split_axis=0, concat_axis=0, tiled=True)  21.2 us
    ppermute x7, starting transfers between devices, shards(): part = lax.ppermute(part, 'hour', [(h, h ^ distance) for h in range(hours)])  11.9 us
    ppermute x1, starting transfers between devices, shards(): lax.ppermute(rows, 'sens', [(s, (s - 2) % sens) for s in range(sens)])  7.33 us
    pallas_call x1, Pallas kernels, shards(): pl.pallas_call(functools.partial(across_kernel, other), out_shape=(one,)...  6.28 us
    ppermute x7, waiting for transfers between devices, shards(): part = lax.ppermute(part, 'hour', [(h, h ^ distance) for h in range(hours)])  5.73 us
    pallas_call x1, Pallas kernels, shards(): pl.pallas_call(own_kernel, out_shape=(pltpu.VMEM((RES + 1, PICKED + SLAB,...  3.97 us
    pallas_call x1, Pallas kernels, shards(): pl.pallas_call(functools.partial(along_kernel, same), out_shape=(one,) *...  3.72 us
  transfers between devices with their start and end apart: 10, of which 3 were waited for; matrix products, arithmetic and copies ran while one was open for 0% of the time, Pallas kernels for 14%

profile of v5, /device:TPU:1, one launch (start us, length us, event | category | flops | bytes accessed | tf_op | source)
XLA Modules:
  0.0 64.2 jit_solution(13443110764945907025)
XLA Ops:
  0.0 7.3 %collective-permute-start = (bf16[24,4096]{1,0:T(8,128)(2,1)}, bf16[24,4096]{1,0:T(8,128)(2,1)S(1)}, u32[]{:S(2)}, u32[]{:S(2)}) collective-permute-start(bf16[24,4096]{1,0:T(8,128)(2,1)} %bitcast.10), channel_id=1, source_target_pairs={{0,240},{8,248},{16,0},{24,8},{32,16},{40,24},{48,32},{56,40},{64,... | collective-permute-start | bytes 589832 | tf_op jit(solution)/shard_map/ppermute | solution.py:246
  7.3 1.0 %collective-permute-start.1 = (bf16[24,4096]{1,0:T(8,128)(2,1)}, bf16[24,4096]{1,0:T(8,128)(2,1)S(1)}, u32[]{:S(2)}, u32[]{:S(2)}) collective-permute-start(bf16[24,4096]{1,0:T(8,128)(2,1)} %bitcast.11), channel_id=1, source_target_pairs={{0,8},{8,0},{16,24},{24,16},{32,40},{40,32},{48,56},{56,48},{64,72... | collective-permute-start | bytes 589832 | tf_op jit(solution)/shard_map/ppermute | solution.py:247
  8.3 4.0 %own.1 = (bf16[17,224,256]{2,1,0:T(8,128)(2,1)S(1)}, bf16[128,64]{1,0:T(8,128)(2,1)S(1)}) custom-call(bf16[24,4096]{1,0:T(8,128)(2,1)} %bitcast.12, f32[2,16,512]{2,1,0:T(8,128)} %constant.21.clone.twiddle_any.twiddle_ref, bf16[2,1024,256]{2,1,0:T(8,128)(2,1)} %constant.22.clone.common_any.common_ref, s32[1,64]{1,0:T(1,128)} %bitcast.13, s32[1,64]{1,0:T(1,128)} %bitcast.14, ...), custom_call_target="tpu_custom_call" | custom-call | flops 1000000000 | bytes 1000000 | tf_op jit(solution)/shard_map/own/pallas_call | solution.py:261
  12.3 0.0 copy-start
  12.3 0.0 copy-start.4
  12.3 0.0 collective-permute-done.rows_ref
  12.3 0.5 collective-permute-start.2
  12.8 0.1 pad_add_fusion.where_ref
  12.8 0.0 copy-done.2
  12.8 1.2 %farther.1.far_ref = bf16[16,32,256]{2,1,0:T(8,128)(2,1)S(1)} custom-call(bf16[24,4096]{1,0:T(8,128)(2,1)S(1)} %collective-permute-done.rows_ref, f32[2,16,512]{2,1,0:T(8,128)S(1)} %copy-done.3, bf16[2,1024,256]{2,1,0:T(8,128)(2,1)S(1)} %copy-done.2), custom_call_target="tpu_custom_call" | custom-call | flops 1000000000 | bytes 1000000 | tf_op jit(solution)/shard_map/farther/pallas_call | solution.py:285
  14.1 0.0 collective-permute-done.1.sibling_ref
  14.1 0.0 collective-permute-done.2.passed_ref
  14.1 6.3 %across.1 = (bf16[64,1152]{1,0:T(8,128)(2,1)S(1)}, bf16[64,1152]{1,0:T(8,128)(2,1)S(1)}, bf16[64,1152]{1,0:T(8,128)(2,1)S(1)}, bf16[64,1152]{1,0:T(8,128)(2,1)S(1)}, bf16[16,192,256]{2,1,0:T(8,128)(2,1)S(1)}) custom-call(s32[2]{0:T(128)S(1)} %pad_add_fusion.where_ref, bf16[17,224,256]{2,1,0:T(8,128)(2,1)S(1)} %get-tuple-element.20.kept_ref, ...), custom_call_target="tpu_custom_call" | custom-call | flops 3000000000 | bytes 1000000 | tf_op jit(solution)/shard_map/across/pallas_call | solution.py:300
  20.4 5.0 %collective-permute-start.3 = (bf16[64,1152]{1,0:T(8,128)(2,1)S(1)}, bf16[64,1152]{1,0:T(8,128)(2,1)S(1)}, u32[]{:S(2)}, u32[]{:S(2)}) collective-permute-start(bf16[64,1152]{1,0:T(8,128)(2,1)S(1)} %get-tuple-element.22), channel_id=1, source_target_pairs={{0,7},{1,6},{2,5},{3,4},{4,3},{5,2},{6,1},{7,0},{8,15},{9,14},{10,... | collective-permute-start | bytes 442376 | tf_op jit(solution)/shard_map/ppermute | solution.py:323
  25.4 0.6 collective-permute-start.4
  26.0 2.3 %collective-permute-start.5 = (bf16[64,1152]{1,0:T(8,128)(2,1)S(1)}, bf16[64,1152]{1,0:T(8,128)(2,1)S(1)}, u32[]{:S(2)}, u32[]{:S(2)}) collective-permute-start(bf16[64,1152]{1,0:T(8,128)(2,1)S(1)} %get-tuple-element.24), channel_id=1, source_target_pairs={{0,5},{1,4},{2,7},{3,6},{4,1},{5,0},{6,3},{7,2},{8,13},{9,12},{10,... | collective-permute-start | bytes 442376 | tf_op jit(solution)/shard_map/ppermute | solution.py:323
  28.3 0.5 collective-permute-start.6
  28.8 3.7 %along.1 = (bf16[64,1152]{1,0:T(8,128)(2,1)S(1)}, bf16[64,1152]{1,0:T(8,128)(2,1)S(1)}, bf16[64,1152]{1,0:T(8,128)(2,1)S(1)}, bf16[64,1152]{1,0:T(8,128)(2,1)S(1)}) custom-call(s32[2]{0:T(128)S(1)} %pad_add_fusion.where_ref, bf16[17,224,256]{2,1,0:T(8,128)(2,1)S(1)} %get-tuple-element.20.kept_ref, ...), custom_call_target="tpu_custom_call" | custom-call | flops 3000000000 | bytes 1000000 | tf_op jit(solution)/shard_map/along/pallas_call | solution.py:310
  32.6 2.8 %collective-permute-start.7 = (bf16[64,1152]{1,0:T(8,128)(2,1)S(1)}, bf16[64,1152]{1,0:T(8,128)(2,1)S(1)}, u32[]{:S(2)}, u32[]{:S(2)}) collective-permute-start(bf16[64,1152]{1,0:T(8,128)(2,1)S(1)} %get-tuple-element.27), channel_id=1, source_target_pairs={{0,3},{1,2},{2,1},{3,0},{4,7},{5,6},{6,5},{7,4},{8,11},{9,10},{10,... | collective-permute-start | bytes 442376 | tf_op jit(solution)/shard_map/ppermute | solution.py:323
  35.4 0.0 collective-permute-done.3.refs_0_
  35.4 0.4 collective-permute-start.8
  35.7 0.0 collective-permute-done.4.refs_1_
  35.7 0.3 collective-permute-start.9
  36.1 0.0 collective-permute-done.5.refs_2_
  36.1 3.1 %collective-permute-done.6.refs_3_ = bf16[64,1152]{1,0:T(8,128)(2,1)S(1)} collective-permute-done((bf16[64,1152]{1,0:T(8,128)(2,1)S(1)}, bf16[64,1152]{1,0:T(8,128)(2,1)S(1)}, u32[]{:S(2)}, u32[]{:S(2)}) %collective-permute-start.6) | collective-permute-done | bytes 147488 | tf_op jit(solution)/shard_map/ppermute | solution.py:323
  39.2 2.3 %collective-permute-done.7.refs_4_ = bf16[64,1152]{1,0:T(8,128)(2,1)S(1)} collective-permute-done((bf16[64,1152]{1,0:T(8,128)(2,1)S(1)}, bf16[64,1152]{1,0:T(8,128)(2,1)S(1)}, u32[]{:S(2)}, u32[]{:S(2)}) %collective-permute-start.7) | collective-permute-done | bytes 147488 | tf_op jit(solution)/shard_map/ppermute | solution.py:323
  41.5 0.0 collective-permute-done.8.refs_5_
  41.5 0.3 collective-permute-done.9.refs_6_
  41.8 0.3 collect.1
  42.1 0.1 all_to_all.6
  42.2 21.2 %all_to_all.9 = bf16[32,4,1152]{2,1,0:T(4,128)(2,1)S(1)} all-to-all(bf16[32,4,1152]{2,1,0:T(4,128)(2,1)S(1)} %all_to_all.6), channel_id=1, replica_groups=mesh['sens'=32,'hour'=8] {'sens'}, dimensions={0} | all-to-all | bytes 589824 | tf_op jit(solution)/shard_map/all_to_all | solution.py:334
  63.4 0.9 %reshape.20 = f32[128,1152]{1,0:T(8,128)} reshape(bf16[32,4,1152]{2,1,0:T(4,128)(2,1)S(1)} %all_to_all.9) | data formatting | bytes 884736 | tf_op jit(solution)/shard_map/convert_element_type | solution.py:335
  (7 shorter events, 0.0 us)
Async XLA Ops:
  0.0 12.8 %copy-start.2 = (bf16[2,1024,256]{2,1,0:T(8,128)(2,1)S(1)}, bf16[2,1024,256]{2,1,0:T(8,128)(2,1)}, u32[]{:S(2)}) copy-start(bf16[2,1024,256]{2,1,0:T(8,128)(2,1)} %constant.22.clone.common_any.common_ref) | copy-start | bytes 3145732
  0.0 12.3 %collective-permute-start = (bf16[24,4096]{1,0:T(8,128)(2,1)}, bf16[24,4096]{1,0:T(8,128)(2,1)S(1)}, u32[]{:S(2)}, u32[]{:S(2)}) collective-permute-start(bf16[24,4096]{1,0:T(8,128)(2,1)} %bitcast.10), channel_id=1, source_target_pairs={{0,240},{8,248},{16,0},{24,8},{32,16},{40,24},{48,32},{56,40},{64,... | collective-permute-start | bytes 589832 | tf_op jit(solution)/shard_map/ppermute | solution.py:246
  7.3 6.7 %collective-permute-start.1 = (bf16[24,4096]{1,0:T(8,128)(2,1)}, bf16[24,4096]{1,0:T(8,128)(2,1)S(1)}, u32[]{:S(2)}, u32[]{:S(2)}) collective-permute-start(bf16[24,4096]{1,0:T(8,128)(2,1)} %bitcast.11), channel_id=1, source_target_pairs={{0,8},{8,0},{16,24},{24,16},{32,40},{40,32},{48,56},{56,48},{64,72... | collective-permute-start | bytes 589832 | tf_op jit(solution)/shard_map/ppermute | solution.py:247
  8.3 4.6 %copy-start.3 = (f32[2,16,512]{2,1,0:T(8,128)S(1)}, f32[2,16,512]{2,1,0:T(8,128)}, u32[]{:S(2)}) copy-start(f32[2,16,512]{2,1,0:T(8,128)} %constant.21.clone.twiddle_any.twiddle_ref) | copy-start | bytes 196612
  8.3 5.8 %copy-start.1 = (bf16[2048,512]{1,0:T(8,128)(2,1)S(1)}, bf16[2048,512]{1,0:T(8,128)(2,1)}, u32[]{:S(2)}) copy-start(bf16[2048,512]{1,0:T(8,128)(2,1)} %constant.23.clone.cosines_ref) | copy-start | bytes 6291460
  12.3 1.8 %copy-start = (bf16[2048,512]{1,0:T(8,128)(2,1)S(1)}, bf16[2048,512]{1,0:T(8,128)(2,1)}, u32[]{:S(2)}) copy-start(bf16[2048,512]{1,0:T(8,128)(2,1)} %constant.24.clone.sines_ref) | copy-start | bytes 6291460
  12.3 1.8 %copy-start.4 = (bf16[128,128]{1,0:T(8,128)(2,1)S(1)}, bf16[128,128]{1,0:T(8,128)(2,1)}, u32[]{:S(2)}) copy-start(bf16[128,128]{1,0:T(8,128)(2,1)} %constant.25.clone.flip_ref) | copy-start | bytes 98308
  12.3 1.8 %collective-permute-start.2 = (bf16[24,4096]{1,0:T(8,128)(2,1)S(1)}, bf16[24,4096]{1,0:T(8,128)(2,1)S(1)}, u32[]{:S(2)}, u32[]{:S(2)}) collective-permute-start(bf16[24,4096]{1,0:T(8,128)(2,1)S(1)} %collective-permute-done.rows_ref), channel_id=1, source_target_pairs={{0,8},{8,0},{16,24},{24,16},{32,40},{40,32},{48,56},{56,48},{64,72... | collective-permute-start | bytes 589832 | tf_op jit(solution)/shard_map/ppermute | solution.py:284
  20.4 15.0 %collective-permute-start.3 = (bf16[64,1152]{1,0:T(8,128)(2,1)S(1)}, bf16[64,1152]{1,0:T(8,128)(2,1)S(1)}, u32[]{:S(2)}, u32[]{:S(2)}) collective-permute-start(bf16[64,1152]{1,0:T(8,128)(2,1)S(1)} %get-tuple-element.22), channel_id=1, source_target_pairs={{0,7},{1,6},{2,5},{3,4},{4,3},{5,2},{6,1},{7,0},{8,15},{9,14},{10,... | collective-permute-start | bytes 442376 | tf_op jit(solution)/shard_map/ppermute | solution.py:323
  25.4 10.4 %collective-permute-start.4 = (bf16[64,1152]{1,0:T(8,128)(2,1)S(1)}, bf16[64,1152]{1,0:T(8,128)(2,1)S(1)}, u32[]{:S(2)}, u32[]{:S(2)}) collective-permute-start(bf16[64,1152]{1,0:T(8,128)(2,1)S(1)} %get-tuple-element.23), channel_id=1, source_target_pairs={{0,6},{1,7},{2,4},{3,5},{4,2},{5,3},{6,0},{7,1},{8,14},{9,15},{10,... | collective-permute-start | bytes 442376 | tf_op jit(solution)/shard_map/ppermute | solution.py:323
  26.0 10.1 %collective-permute-start.5 = (bf16[64,1152]{1,0:T(8,128)(2,1)S(1)}, bf16[64,1152]{1,0:T(8,128)(2,1)S(1)}, u32[]{:S(2)}, u32[]{:S(2)}) collective-permute-start(bf16[64,1152]{1,0:T(8,128)(2,1)S(1)} %get-tuple-element.24), channel_id=1, source_target_pairs={{0,5},{1,4},{2,7},{3,6},{4,1},{5,0},{6,3},{7,2},{8,13},{9,12},{10,... | collective-permute-start | bytes 442376 | tf_op jit(solution)/shard_map/ppermute | solution.py:323
  28.3 10.9 %collective-permute-start.6 = (bf16[64,1152]{1,0:T(8,128)(2,1)S(1)}, bf16[64,1152]{1,0:T(8,128)(2,1)S(1)}, u32[]{:S(2)}, u32[]{:S(2)}) collective-permute-start(bf16[64,1152]{1,0:T(8,128)(2,1)S(1)} %get-tuple-element.25), channel_id=1, source_target_pairs={{0,4},{1,5},{2,6},{3,7},{4,0},{5,1},{6,2},{7,3},{8,12},{9,13},{10,... | collective-permute-start | bytes 442376 | tf_op jit(solution)/shard_map/ppermute | solution.py:323
  32.6 8.9 %collective-permute-start.7 = (bf16[64,1152]{1,0:T(8,128)(2,1)S(1)}, bf16[64,1152]{1,0:T(8,128)(2,1)S(1)}, u32[]{:S(2)}, u32[]{:S(2)}) collective-permute-start(bf16[64,1152]{1,0:T(8,128)(2,1)S(1)} %get-tuple-element.27), channel_id=1, source_target_pairs={{0,3},{1,2},{2,1},{3,0},{4,7},{5,6},{6,5},{7,4},{8,11},{9,10},{10,... | collective-permute-start | bytes 442376 | tf_op jit(solution)/shard_map/ppermute | solution.py:323
  35.4 6.1 %collective-permute-start.8 = (bf16[64,1152]{1,0:T(8,128)(2,1)S(1)}, bf16[64,1152]{1,0:T(8,128)(2,1)S(1)}, u32[]{:S(2)}, u32[]{:S(2)}) collective-permute-start(bf16[64,1152]{1,0:T(8,128)(2,1)S(1)} %get-tuple-element.28), channel_id=1, source_target_pairs={{0,2},{1,3},{2,0},{3,1},{4,6},{5,7},{6,4},{7,5},{8,10},{9,11},{10,... | collective-permute-start | bytes 442376 | tf_op jit(solution)/shard_map/ppermute | solution.py:323
  35.7 6.0 %collective-permute-start.9 = (bf16[64,1152]{1,0:T(8,128)(2,1)S(1)}, bf16[64,1152]{1,0:T(8,128)(2,1)S(1)}, u32[]{:S(2)}, u32[]{:S(2)}) collective-permute-start(bf16[64,1152]{1,0:T(8,128)(2,1)S(1)} %get-tuple-element.29), channel_id=1, source_target_pairs={{0,1},{1,0},{2,3},{3,2},{4,5},{5,4},{6,7},{7,6},{8,9},{9,8},{10,11... | collective-permute-start | bytes 442376 | tf_op jit(solution)/shard_map/ppermute | solution.py:323

commit v6 on v5

--- a/solution.py
+++ b/solution.py
@@ -225,12 +225,21 @@
            tile_ref)
 
 
-def collect_kernel(place_ref, *refs):
-    *parts_refs, out_ref = refs
+def total_of(parts_refs):
     total = parts_refs[0][...].astype(jnp.float32)
     for ref in parts_refs[1:]:
         total = total + ref[...].astype(jnp.float32)
-    total = (total * (1.0 / 128.0)).astype(jnp.bfloat16)
+    return total
+
+
+def fold_kernel(*refs):
+    *parts_refs, out_ref = refs
+    out_ref[...] = total_of(parts_refs).astype(jnp.bfloat16)
+
+
+def collect_kernel(place_ref, *refs):
+    *parts_refs, out_ref = refs
+    total = (total_of(parts_refs) * (1.0 / 128.0)).astype(jnp.bfloat16)
     out_ref[...] = jnp.dot(place_ref[...], total, preferred_element_type=jnp.float32).astype(jnp.bfloat16)
 
 
@@ -317,15 +326,23 @@
         cost_estimate=cost(3 * 10**9),
         name="along",
     )(where, kept, second_rows, cosines, sines, flip)
-    parts = []
-    for distance, part in zip(other + same, [*across, *along]):
-        if distance:
-            part = lax.ppermute(part, "hour", [(h, h ^ distance) for h in range(hours)])
-        parts.append(part)
+    def exchanged(part, distance):
+        return lax.ppermute(part, "hour", [(h, h ^ distance) for h in range(hours)]) if distance else part
+
+    folded = pl.pallas_call(
+        fold_kernel,
+        out_shape=one,
+        in_specs=[vmem] * 4,
+        out_specs=vmem,
+        compiler_params=params,
+        cost_estimate=cost(10**7),
+        name="fold",
+    )(*(exchanged(part, distance & 3) for distance, part in zip(other, across)))
+    parts = [exchanged(folded, 4)] + [exchanged(part, distance) for distance, part in zip(same, along)]
     outgoing = pl.pallas_call(
         collect_kernel,
         out_shape=jax.ShapeDtypeStruct((slots, share), bf16),
-        in_specs=[vmem] * (1 + hours),
+        in_specs=[vmem] * (1 + len(parts)),
         out_specs=vmem,
         compiler_params=params,
         cost_estimate=cost(2 * 10**7),

time: 64.3 us -> 59.4 us (0.924)
  starting transfers between devices: 20.7 us -> 18.3 us
  waiting for transfers between devices: 5.74 us -> 3.41 us
    ppermute x7, starting transfers between devices: 11.9 us -> 9.56 us  [exchanged(): lax.ppermute(part, 'hour', [(h, h ^ distance) for h in range(hours)])]
    ppermute x7, waiting for transfers between devices: 5.73 us -> 3.4 us  [exchanged(): lax.ppermute(part, 'hour', [(h, h ^ distance) for h in range(hours)])]
  transfers between devices with their start and end apart: 10 -> 10, of which waited for: 3 -> 2; matrix products, arithmetic and copies ran while one was open for 0% -> 0% of each run, Pallas kernels for 14% -> 15%
where the time goes in v6:
time: 59.4 us; the launch traced here: 59.3 us
  blocking collectives  20.9 us (35%)
  starting transfers between devices  18.3 us (31%)
  Pallas kernels  15.5 us (26%)
  waiting for transfers between devices  3.41 us (6%)
  local copies, waits for them, and re-layouts  0.95 us (2%)
    all_to_all x1, blocking collectives, shards(): lax.all_to_all(outgoing, 'sens', split_axis=0, concat_axis=0, tiled=True)  20.9 us
    ppermute x7, starting transfers between devices, exchanged(): lax.ppermute(part, 'hour', [(h, h ^ distance) for h in range(hours)])  9.56 us
    ppermute x1, starting transfers between devices, shards(): lax.ppermute(rows, 'sens', [(s, (s - 2) % sens) for s in range(sens)])  7.33 us
    pallas_call x1, Pallas kernels, shards(): pl.pallas_call(functools.partial(across_kernel, other), out_shape=(one,)...  6.28 us
    pallas_call x1, Pallas kernels, shards(): pl.pallas_call(own_kernel, out_shape=(pltpu.VMEM((RES + 1, PICKED + SLAB,...  3.97 us
    pallas_call x1, Pallas kernels, shards(): pl.pallas_call(functools.partial(along_kernel, same), out_shape=(one,) *...  3.73 us
    ppermute x7, waiting for transfers between devices, exchanged(): lax.ppermute(part, 'hour', [(h, h ^ distance) for h in range(hours)])  3.4 us
    pallas_call x1, Pallas kernels, shards(): pl.pallas_call(farther_kernel, out_shape=spectra, in_specs=[vmem] * 3, ou...  1.19 us
  transfers between devices with their start and end apart: 10, of which 2 were waited for; matrix products, arithmetic and copies ran while one was open for 0% of the time, Pallas kernels for 15%

profile of v6, /device:TPU:1, one launch (start us, length us, event | category | flops | bytes accessed | tf_op | source)
XLA Modules:
  0.0 59.3 jit_solution(16232175377135361946)
XLA Ops:
  0.0 7.3 %collective-permute-start = (bf16[24,4096]{1,0:T(8,128)(2,1)}, bf16[24,4096]{1,0:T(8,128)(2,1)S(1)}, u32[]{:S(2)}, u32[]{:S(2)}) collective-permute-start(bf16[24,4096]{1,0:T(8,128)(2,1)} %bitcast.10), channel_id=1, source_target_pairs={{0,240},{8,248},{16,0},{24,8},{32,16},{40,24},{48,32},{56,40},{64,... | collective-permute-start | bytes 589832 | tf_op jit(solution)/shard_map/ppermute | solution.py:255
  7.3 1.0 %collective-permute-start.1 = (bf16[24,4096]{1,0:T(8,128)(2,1)}, bf16[24,4096]{1,0:T(8,128)(2,1)S(1)}, u32[]{:S(2)}, u32[]{:S(2)}) collective-permute-start(bf16[24,4096]{1,0:T(8,128)(2,1)} %bitcast.11), channel_id=1, source_target_pairs={{0,8},{8,0},{16,24},{24,16},{32,40},{40,32},{48,56},{56,48},{64,72... | collective-permute-start | bytes 589832 | tf_op jit(solution)/shard_map/ppermute | solution.py:256
  8.3 4.0 %own.1 = (bf16[17,224,256]{2,1,0:T(8,128)(2,1)S(1)}, bf16[128,64]{1,0:T(8,128)(2,1)S(1)}) custom-call(bf16[24,4096]{1,0:T(8,128)(2,1)} %bitcast.12, f32[2,16,512]{2,1,0:T(8,128)} %constant.21.clone.twiddle_any.twiddle_ref, bf16[2,1024,256]{2,1,0:T(8,128)(2,1)} %constant.22.clone.common_any.common_ref, s32[1,64]{1,0:T(1,128)} %bitcast.13, s32[1,64]{1,0:T(1,128)} %bitcast.14, ...), custom_call_target="tpu_custom_call" | custom-call | flops 1000000000 | bytes 1000000 | tf_op jit(solution)/shard_map/own/pallas_call | solution.py:270
  12.3 0.0 copy-start
  12.3 0.0 copy-start.4
  12.3 0.0 collective-permute-done.rows_ref
  12.3 0.5 collective-permute-start.2
  12.8 0.1 pad_add_fusion.where_ref
  12.8 1.2 %farther.1.far_ref = bf16[16,32,256]{2,1,0:T(8,128)(2,1)S(1)} custom-call(bf16[24,4096]{1,0:T(8,128)(2,1)S(1)} %collective-permute-done.rows_ref, f32[2,16,512]{2,1,0:T(8,128)S(1)} %copy-done.3, bf16[2,1024,256]{2,1,0:T(8,128)(2,1)S(1)} %copy-done.2), custom_call_target="tpu_custom_call" | custom-call | flops 1000000000 | bytes 1000000 | tf_op jit(solution)/shard_map/farther/pallas_call | solution.py:294
  14.1 0.0 collective-permute-done.1.sibling_ref
  14.1 0.0 collective-permute-done.2.passed_ref
  14.1 6.3 %across.1 = (bf16[64,1152]{1,0:T(8,128)(2,1)S(1)}, bf16[64,1152]{1,0:T(8,128)(2,1)S(1)}, bf16[64,1152]{1,0:T(8,128)(2,1)S(1)}, bf16[64,1152]{1,0:T(8,128)(2,1)S(1)}, bf16[16,192,256]{2,1,0:T(8,128)(2,1)S(1)}) custom-call(s32[2]{0:T(128)S(1)} %pad_add_fusion.where_ref, bf16[17,224,256]{2,1,0:T(8,128)(2,1)S(1)} %get-tuple-element.20.kept_ref, ...), custom_call_target="tpu_custom_call" | custom-call | flops 3000000000 | bytes 1000000 | tf_op jit(solution)/shard_map/across/pallas_call | solution.py:309
  20.4 2.8 %collective-permute-start.3 = (bf16[64,1152]{1,0:T(8,128)(2,1)S(1)}, bf16[64,1152]{1,0:T(8,128)(2,1)S(1)}, u32[]{:S(2)}, u32[]{:S(2)}) collective-permute-start(bf16[64,1152]{1,0:T(8,128)(2,1)S(1)} %get-tuple-element.22), channel_id=1, source_target_pairs={{0,3},{1,2},{2,1},{3,0},{4,7},{5,6},{6,5},{7,4},{8,11},{9,10},{10,... | collective-permute-start | bytes 442376 | tf_op jit(solution)/shard_map/ppermute | solution.py:330
  23.2 0.3 collective-permute-start.4
  23.6 0.3 collective-permute-start.5
  23.9 3.7 %along.1 = (bf16[64,1152]{1,0:T(8,128)(2,1)S(1)}, bf16[64,1152]{1,0:T(8,128)(2,1)S(1)}, bf16[64,1152]{1,0:T(8,128)(2,1)S(1)}, bf16[64,1152]{1,0:T(8,128)(2,1)S(1)}) custom-call(s32[2]{0:T(128)S(1)} %pad_add_fusion.where_ref, bf16[17,224,256]{2,1,0:T(8,128)(2,1)S(1)} %get-tuple-element.20.kept_ref, ...), custom_call_target="tpu_custom_call" | custom-call | flops 3000000000 | bytes 1000000 | tf_op jit(solution)/shard_map/along/pallas_call | solution.py:319
  27.6 2.8 %collective-permute-start.7 = (bf16[64,1152]{1,0:T(8,128)(2,1)S(1)}, bf16[64,1152]{1,0:T(8,128)(2,1)S(1)}, u32[]{:S(2)}, u32[]{:S(2)}) collective-permute-start(bf16[64,1152]{1,0:T(8,128)(2,1)S(1)} %get-tuple-element.27), channel_id=1, source_target_pairs={{0,3},{1,2},{2,1},{3,0},{4,7},{5,6},{6,5},{7,4},{8,11},{9,10},{10,... | collective-permute-start | bytes 442376 | tf_op jit(solution)/shard_map/ppermute | solution.py:330
  30.5 0.3 collective-permute-start.8
  30.8 0.0 collective-permute-done.3.refs_0_
  30.8 0.3 collective-permute-start.9
  31.2 0.0 collective-permute-done.4.refs_1_
  31.2 0.0 collective-permute-done.5.refs_2_
  31.2 0.1 fold.1
  31.2 2.5 %collective-permute-start.6 = (bf16[64,1152]{1,0:T(8,128)(2,1)S(1)}, bf16[64,1152]{1,0:T(8,128)(2,1)S(1)}, u32[]{:S(2)}, u32[]{:S(2)}) collective-permute-start(bf16[64,1152]{1,0:T(8,128)(2,1)S(1)} %fold.1), channel_id=1, source_target_pairs={{0,4},{1,5},{2,6},{3,7},{4,0},{5,1},{6,2},{7,3},{8,12},{9,13},{10,... | collective-permute-start | bytes 442376 | tf_op jit(solution)/shard_map/ppermute | solution.py:330
  33.8 2.8 %collective-permute-done.7.refs_1_ = bf16[64,1152]{1,0:T(8,128)(2,1)S(1)} collective-permute-done((bf16[64,1152]{1,0:T(8,128)(2,1)S(1)}, bf16[64,1152]{1,0:T(8,128)(2,1)S(1)}, u32[]{:S(2)}, u32[]{:S(2)}) %collective-permute-start.7) | collective-permute-done | bytes 147488 | tf_op jit(solution)/shard_map/ppermute | solution.py:330
  36.6 0.0 collective-permute-done.8.refs_2_
  36.6 0.6 collective-permute-done.9.refs_3_
  37.2 0.0 collective-permute-done.6.refs_0_
  37.2 0.3 collect.1
  37.4 0.1 all_to_all.6
  37.5 20.9 %all_to_all.9 = bf16[32,4,1152]{2,1,0:T(4,128)(2,1)S(1)} all-to-all(bf16[32,4,1152]{2,1,0:T(4,128)(2,1)S(1)} %all_to_all.6), channel_id=1, replica_groups=mesh['sens'=32,'hour'=8] {'sens'}, dimensions={0} | all-to-all | bytes 589824 | tf_op jit(solution)/shard_map/all_to_all | solution.py:351
  58.4 0.9 %reshape.20 = f32[128,1152]{1,0:T(8,128)} reshape(bf16[32,4,1152]{2,1,0:T(4,128)(2,1)S(1)} %all_to_all.9) | data formatting | bytes 884736 | tf_op jit(solution)/shard_map/convert_element_type | solution.py:352
  (8 shorter events, 0.0 us)
Async XLA Ops:
  0.0 12.8 %copy-start.2 = (bf16[2,1024,256]{2,1,0:T(8,128)(2,1)S(1)}, bf16[2,1024,256]{2,1,0:T(8,128)(2,1)}, u32[]{:S(2)}) copy-start(bf16[2,1024,256]{2,1,0:T(8,128)(2,1)} %constant.22.clone.common_any.common_ref) | copy-start | bytes 3145732
  0.0 12.3 %collective-permute-start = (bf16[24,4096]{1,0:T(8,128)(2,1)}, bf16[24,4096]{1,0:T(8,128)(2,1)S(1)}, u32[]{:S(2)}, u32[]{:S(2)}) collective-permute-start(bf16[24,4096]{1,0:T(8,128)(2,1)} %bitcast.10), channel_id=1, source_target_pairs={{0,240},{8,248},{16,0},{24,8},{32,16},{40,24},{48,32},{56,40},{64,... | collective-permute-start | bytes 589832 | tf_op jit(solution)/shard_map/ppermute | solution.py:255
  7.3 6.7 %collective-permute-start.1 = (bf16[24,4096]{1,0:T(8,128)(2,1)}, bf16[24,4096]{1,0:T(8,128)(2,1)S(1)}, u32[]{:S(2)}, u32[]{:S(2)}) collective-permute-start(bf16[24,4096]{1,0:T(8,128)(2,1)} %bitcast.11), channel_id=1, source_target_pairs={{0,8},{8,0},{16,24},{24,16},{32,40},{40,32},{48,56},{56,48},{64,72... | collective-permute-start | bytes 589832 | tf_op jit(solution)/shard_map/ppermute | solution.py:256
  8.3 4.6 %copy-start.3 = (f32[2,16,512]{2,1,0:T(8,128)S(1)}, f32[2,16,512]{2,1,0:T(8,128)}, u32[]{:S(2)}) copy-start(f32[2,16,512]{2,1,0:T(8,128)} %constant.21.clone.twiddle_any.twiddle_ref) | copy-start | bytes 196612
  8.3 5.8 %copy-start.1 = (bf16[2048,512]{1,0:T(8,128)(2,1)S(1)}, bf16[2048,512]{1,0:T(8,128)(2,1)}, u32[]{:S(2)}) copy-start(bf16[2048,512]{1,0:T(8,128)(2,1)} %constant.23.clone.cosines_ref) | copy-start | bytes 6291460
  12.3 1.8 %copy-start = (bf16[2048,512]{1,0:T(8,128)(2,1)S(1)}, bf16[2048,512]{1,0:T(8,128)(2,1)}, u32[]{:S(2)}) copy-start(bf16[2048,512]{1,0:T(8,128)(2,1)} %constant.24.clone.sines_ref) | copy-start | bytes 6291460
  12.3 1.8 %copy-start.4 = (bf16[128,128]{1,0:T(8,128)(2,1)S(1)}, bf16[128,128]{1,0:T(8,128)(2,1)}, u32[]{:S(2)}) copy-start(bf16[128,128]{1,0:T(8,128)(2,1)} %constant.25.clone.flip_ref) | copy-start | bytes 98308
  12.3 1.8 %collective-permute-start.2 = (bf16[24,4096]{1,0:T(8,128)(2,1)S(1)}, bf16[24,4096]{1,0:T(8,128)(2,1)S(1)}, u32[]{:S(2)}, u32[]{:S(2)}) collective-permute-start(bf16[24,4096]{1,0:T(8,128)(2,1)S(1)} %collective-permute-done.rows_ref), channel_id=1, source_target_pairs={{0,8},{8,0},{16,24},{24,16},{32,40},{40,32},{48,56},{56,48},{64,72... | collective-permute-start | bytes 589832 | tf_op jit(solution)/shard_map/ppermute | solution.py:293
  20.4 10.4 %collective-permute-start.3 = (bf16[64,1152]{1,0:T(8,128)(2,1)S(1)}, bf16[64,1152]{1,0:T(8,128)(2,1)S(1)}, u32[]{:S(2)}, u32[]{:S(2)}) collective-permute-start(bf16[64,1152]{1,0:T(8,128)(2,1)S(1)} %get-tuple-element.22), channel_id=1, source_target_pairs={{0,3},{1,2},{2,1},{3,0},{4,7},{5,6},{6,5},{7,4},{8,11},{9,10},{10,... | collective-permute-start | bytes 442376 | tf_op jit(solution)/shard_map/ppermute | solution.py:330
  23.2 7.9 %collective-permute-start.4 = (bf16[64,1152]{1,0:T(8,128)(2,1)S(1)}, bf16[64,1152]{1,0:T(8,128)(2,1)S(1)}, u32[]{:S(2)}, u32[]{:S(2)}) collective-permute-start(bf16[64,1152]{1,0:T(8,128)(2,1)S(1)} %get-tuple-element.23), channel_id=1, source_target_pairs={{0,2},{1,3},{2,0},{3,1},{4,6},{5,7},{6,4},{7,5},{8,10},{9,11},{10,... | collective-permute-start | bytes 442376 | tf_op jit(solution)/shard_map/ppermute | solution.py:330
  23.6 7.6 %collective-permute-start.5 = (bf16[64,1152]{1,0:T(8,128)(2,1)S(1)}, bf16[64,1152]{1,0:T(8,128)(2,1)S(1)}, u32[]{:S(2)}, u32[]{:S(2)}) collective-permute-start(bf16[64,1152]{1,0:T(8,128)(2,1)S(1)} %get-tuple-element.24), channel_id=1, source_target_pairs={{0,1},{1,0},{2,3},{3,2},{4,5},{5,4},{6,7},{7,6},{8,9},{9,8},{10,11... | collective-permute-start | bytes 442376 | tf_op jit(solution)/shard_map/ppermute | solution.py:330
  27.6 9.0 %collective-permute-start.7 = (bf16[64,1152]{1,0:T(8,128)(2,1)S(1)}, bf16[64,1152]{1,0:T(8,128)(2,1)S(1)}, u32[]{:S(2)}, u32[]{:S(2)}) collective-permute-start(bf16[64,1152]{1,0:T(8,128)(2,1)S(1)} %get-tuple-element.27), channel_id=1, source_target_pairs={{0,3},{1,2},{2,1},{3,0},{4,7},{5,6},{6,5},{7,4},{8,11},{9,10},{10,... | collective-permute-start | bytes 442376 | tf_op jit(solution)/shard_map/ppermute | solution.py:330
  30.5 6.1 %collective-permute-start.8 = (bf16[64,1152]{1,0:T(8,128)(2,1)S(1)}, bf16[64,1152]{1,0:T(8,128)(2,1)S(1)}, u32[]{:S(2)}, u32[]{:S(2)}) collective-permute-start(bf16[64,1152]{1,0:T(8,128)(2,1)S(1)} %get-tuple-element.28), channel_id=1, source_target_pairs={{0,2},{1,3},{2,0},{3,1},{4,6},{5,7},{6,4},{7,5},{8,10},{9,11},{10,... | collective-permute-start | bytes 442376 | tf_op jit(solution)/shard_map/ppermute | solution.py:330
  30.8 6.3 %collective-permute-start.9 = (bf16[64,1152]{1,0:T(8,128)(2,1)S(1)}, bf16[64,1152]{1,0:T(8,128)(2,1)S(1)}, u32[]{:S(2)}, u32[]{:S(2)}) collective-permute-start(bf16[64,1152]{1,0:T(8,128)(2,1)S(1)} %get-tuple-element.29), channel_id=1, source_target_pairs={{0,1},{1,0},{2,3},{3,2},{4,5},{5,4},{6,7},{7,6},{8,9},{9,8},{10,11... | collective-permute-start | bytes 442376 | tf_op jit(solution)/shard_map/ppermute | solution.py:330
  31.2 5.9 %collective-permute-start.6 = (bf16[64,1152]{1,0:T(8,128)(2,1)S(1)}, bf16[64,1152]{1,0:T(8,128)(2,1)S(1)}, u32[]{:S(2)}, u32[]{:S(2)}) collective-permute-start(bf16[64,1152]{1,0:T(8,128)(2,1)S(1)} %fold.1), channel_id=1, source_target_pairs={{0,4},{1,5},{2,6},{3,7},{4,0},{5,1},{6,2},{7,3},{8,12},{9,13},{10,... | collective-permute-start | bytes 442376 | tf_op jit(solution)/shard_map/ppermute | solution.py:330

commit v7 on v6

--- a/solution.py
+++ b/solution.py
@@ -49,12 +49,12 @@
     return twiddle, common, cosines, sines, flip
 
 
-def forward(rows, twiddle_ref, common_ref, parts_ref, store):
-    chunks = [rows[:, SPAN * i : SPAN * (i + 1)].astype(jnp.float32) for i in range(CHUNKS)]
-
-    def combine(weights):
+def forward(load, twiddle_ref, common_ref, parts_ref, store):
+    chunks = [load(slice(SPAN * i, SPAN * (i + 1))).astype(jnp.float32) for i in range(CHUNKS)]
+
+    def combine(weights, first):
         total = None
-        for weight, chunk in zip(weights, chunks):
+        for weight, chunk in zip(weights[first::2], chunks[first::2]):
             weight = float(weight)
             if abs(weight) < 1e-9:
                 continue
@@ -62,23 +62,35 @@
             total = term if total is None else total + term
         return total
 
-    for k in range(0, CHUNKS + 1):
+    def plus(x, y):
+        return y if x is None else x if y is None else x + y
+
+    def minus(x, y):
+        return x if y is None else -y if x is None else x - y
+
+    def emit(residue, real_part, imag_part):
+        tr = twiddle_ref[0, residue - 1 : residue, :]
+        ti = twiddle_ref[1, residue - 1 : residue, :]
+        at = pl.ds((residue - 1) * ROWS, ROWS)
+        if imag_part is None:
+            parts_ref[at, :SPAN] = real_part * tr
+            parts_ref[at, SPAN:] = real_part * ti
+        else:
+            parts_ref[at, :SPAN] = real_part * tr - imag_part * ti
+            parts_ref[at, SPAN:] = real_part * ti + imag_part * tr
+
+    half = CHUNKS // 2
+    for k in range(half + 1):
         angle = 2 * np.pi * ((k * np.arange(CHUNKS)) % RES) / RES
-        real_part = combine(np.cos(angle))
-        imag_part = combine(-np.sin(angle))
-        both = ((RES, 1.0),) if k == 0 else ((CHUNKS, 1.0),) if k == CHUNKS else ((k, 1.0), (RES - k, -1.0))
-        for residue, sign in both:
-            tr = twiddle_ref[0, residue - 1 : residue, :]
-            ti = twiddle_ref[1, residue - 1 : residue, :]
-            if imag_part is None:
-                yr, yi = real_part * tr, real_part * ti
-            elif sign > 0:
-                yr, yi = real_part * tr - imag_part * ti, real_part * ti + imag_part * tr
-            else:
-                yr, yi = real_part * tr + imag_part * ti, real_part * ti - imag_part * tr
-            at = pl.ds((residue - 1) * ROWS, ROWS)
-            parts_ref[at, :SPAN] = yr
-            parts_ref[at, SPAN:] = yi
+        re_even, re_odd = combine(np.cos(angle), 0), combine(np.cos(angle), 1)
+        im_even, im_odd = combine(-np.sin(angle), 0), combine(-np.sin(angle), 1)
+        sums = {k: (plus(re_even, re_odd), plus(im_even, im_odd))}
+        if k != half:
+            sums[CHUNKS - k] = (minus(re_even, re_odd), minus(im_odd, im_even))
+        for residue, (real_part, imag_part) in sums.items():
+            emit(residue or RES, real_part, imag_part)
+            if residue % CHUNKS:
+                emit(RES - residue, real_part, -imag_part)
     both = parts_ref[...]
     high = both.astype(jnp.bfloat16)
     low = (both - high.astype(jnp.float32)).astype(jnp.bfloat16)
@@ -136,17 +148,30 @@
         first = jnp.dot(pick_first, value, preferred_element_type=jnp.float32)
         kept_ref[k, pl.ds(0, PICKED), :] = first.astype(jnp.bfloat16)
 
-    forward(rows_ref[...], twiddle_ref, common_ref, parts_ref, store)
+    forward(lambda columns: rows_ref[:, columns], twiddle_ref, common_ref, parts_ref, store)
 
 
 def farther_kernel(rows_ref, twiddle_ref, common_ref, white_ref, parts_ref):
     def store(k, value):
         white_ref[k] = padded(value)
 
-    forward(rows_ref[...], twiddle_ref, common_ref, parts_ref, store)
-
-
-def shares(distances, hour, kept_ref, second_rows_ref, cosines_ref, sines_ref, flip_ref, out_refs, cross_ref, tile_ref):
+    forward(lambda columns: rows_ref[:, columns], twiddle_ref, common_ref, parts_ref, store)
+
+
+def nearer_kernel(where_ref, sibling_ref, passed_ref, twiddle_ref, common_ref, white_ref, parts_ref):
+    odd = where_ref[1] != 0
+
+    def store(k, value):
+        white_ref[k] = padded(value)
+
+    def load(columns):
+        return jnp.where(odd, passed_ref[:, columns].astype(jnp.float32), sibling_ref[:, columns].astype(jnp.float32))
+
+    forward(load, twiddle_ref, common_ref, parts_ref, store)
+
+
+def shares(distances, hour, kept_ref, second_rows_ref, cosines_ref, sines_ref, flip_ref, out_refs, cross_ref, tile_ref,
+           prepare=lambda k: None):
     count = cross_ref.shape[0]
     base = ((hour ^ distances[0]) >> 2) * (count - 1)
     comps = [base + i for i in range(count)]
@@ -154,9 +179,7 @@
     seconds = [i - f * COMPS for i, f in zip(comps, firsts)]
     group = 16
 
-    def cross(k, carry):
-        at_re = pl.ds(pl.multiple_of(k * BINS, BINS), BINS)
-        at_im = pl.ds(pl.multiple_of(NB + k * BINS, BINS), BINS)
+    def cross(k):
         for i in range(count):
             for g in range(0, PAIRS, group):
                 first_at = pl.ds(pl.multiple_of(firsts[i] * PAIRS + g, group), group)
@@ -165,15 +188,31 @@
                 second = second_rows_ref[k, second_at, :].astype(jnp.float32)
                 ar, ai = first[:, :BINS], first[:, BINS:]
                 br, bi = second[:, :BINS], second[:, BINS:]
-                cross_ref[i, pl.ds(g, group), at_re] = (ar * br + ai * bi).astype(jnp.bfloat16)
-                cross_ref[i, pl.ds(g, group), at_im] = (ar * bi - ai * br).astype(jnp.bfloat16)
-        return carry
-
-    lax.fori_loop(0, RES, cross, 0)
-    block = cross_ref[...].reshape(count * PAIRS, 2 * NB)
-    even = jnp.dot(block[:, :NB], cosines_ref[...], preferred_element_type=jnp.float32)
-    odd = jnp.dot(block[:, NB:], sines_ref[...], preferred_element_type=jnp.float32)
-    zero = jnp.sum(block[:, :NB].astype(jnp.float32), axis=1, keepdims=True)
+                at = pl.ds(g, group)
+                cross_ref[i, at, pl.ds(k * BINS, BINS)] = (ar * br + ai * bi).astype(jnp.bfloat16)
+                cross_ref[i, at, pl.ds(NB + k * BINS, BINS)] = (ar * bi - ai * br).astype(jnp.bfloat16)
+
+    def rows(start, width):
+        return cross_ref[:, :, pl.ds(start, width)].reshape(count * PAIRS, width)
+
+    def plus(x, y):
+        return y if x is None else x + y
+
+    steps = 4
+    each = RES // steps
+    width = NB // steps
+    even = odd = zero = None
+    for step in range(steps + 1):
+        for k in range(each * 2) if step == 0 else range((step + 1) * each, min((step + 2) * each, RES)):
+            prepare(k)
+        for k in range(step * each, min((step + 1) * each, RES)):
+            cross(k)
+        if step:
+            at = (step - 1) * width
+            real_part, imag_part = rows(at, width), rows(NB + at, width)
+            even = plus(even, jnp.dot(real_part, cosines_ref[pl.ds(at, width), :], preferred_element_type=jnp.float32))
+            odd = plus(odd, jnp.dot(imag_part, sines_ref[pl.ds(at, width), :], preferred_element_type=jnp.float32))
+            zero = plus(zero, jnp.sum(real_part.astype(jnp.float32), axis=1, keepdims=True))
     later = pltpu.roll(even - odd, 1, axis=1)
     start = lax.broadcasted_iota(jnp.int32, later.shape, 1) == 0
     after = jnp.where(start, zero, later).astype(jnp.bfloat16)
@@ -194,29 +233,17 @@
             out_ref[:, u * TILE : (u + 1) * TILE] = tile_ref[begin + u]
 
 
-def across_kernel(distances, where_ref, kept_ref, far_ref, sibling_ref, passed_ref, twiddle_ref, common_ref,
-                  cosines_ref, sines_ref, flip_ref, *refs):
-    *out_refs, second_rows_ref, cross_ref, tile_ref, parts_ref, near_ref, rows_ref = refs
-
-    @pl.when(where_ref[1] == 0)
-    def _():
-        rows_ref[...] = sibling_ref[...]
-
-    @pl.when(where_ref[1] != 0)
-    def _():
-        rows_ref[...] = passed_ref[...]
-
-    def store(k, value):
-        near_ref[k] = padded(value)
-
-    forward(rows_ref[...], twiddle_ref, common_ref, parts_ref, store)
+def across_kernel(distances, where_ref, kept_ref, near_ref, far_ref, cosines_ref, sines_ref, flip_ref, *refs):
+    *out_refs, second_rows_ref, cross_ref, tile_ref = refs
     pick = kept_ref[RES, pl.ds(0, PICKED), pl.ds(0, TILE)][:, : 3 * SLAB]
-    for k in range(RES):
+
+    def prepare(k):
         spectra = jnp.concatenate([kept_ref[k, pl.ds(PICKED, SLAB), :], near_ref[k], far_ref[k]], axis=0)
         second = jnp.dot(pick, spectra, preferred_element_type=jnp.float32)
         second_rows_ref[k] = second.astype(jnp.bfloat16)
+
     shares(distances, where_ref[0], kept_ref, second_rows_ref, cosines_ref, sines_ref, flip_ref, out_refs, cross_ref,
-           tile_ref)
+           tile_ref, prepare)
 
 
 def along_kernel(distances, where_ref, kept_ref, second_rows_ref, cosines_ref, sines_ref, flip_ref, *refs):
@@ -291,16 +318,21 @@
     )(rows, twiddle, common, *(v.reshape(1, PAIRS) for v in (pair_first, pair_second, owners)))
     farther, place = lax.optimization_barrier((farther, place))
     passed = lax.ppermute(farther, "sens", swap)
-    far = pl.pallas_call(
-        farther_kernel,
-        out_shape=spectra,
-        in_specs=[vmem] * 3,
-        out_specs=vmem,
-        scratch_shapes=[parts_scratch],
-        compiler_params=params,
-        cost_estimate=cost(10**9),
-        name="farther",
-    )(farther, twiddle, common)
+
+    def whitened(kernel, name, in_specs, args):
+        return pl.pallas_call(
+            kernel,
+            out_shape=spectra,
+            in_specs=in_specs,
+            out_specs=vmem,
+            scratch_shapes=[parts_scratch],
+            compiler_params=params,
+            cost_estimate=cost(10**9),
+            name=name,
+        )(*args, twiddle, common)
+
+    far = whitened(farther_kernel, "farther", [vmem] * 3, (farther,))
+    near = whitened(nearer_kernel, "nearer", [smem] + [vmem] * 4, (where, sibling, passed))
     one = jax.ShapeDtypeStruct((PAIRS, share), bf16)
     half = COMPS * COMPS // 2 + 1
     shares_scratch = [pltpu.VMEM((half, PAIRS, 2 * NB), bf16), pltpu.VMEM((half * LAGS // TILE, PAIRS, TILE), bf16)]
@@ -309,13 +341,13 @@
     *across, second_rows = pl.pallas_call(
         functools.partial(across_kernel, other),
         out_shape=(one,) * 4 + (jax.ShapeDtypeStruct((RES, PICKED, 2 * BINS), bf16),),
-        in_specs=[smem] + [vmem] * 9,
+        in_specs=[smem] + [vmem] * 6,
         out_specs=(vmem,) * 5,
-        scratch_shapes=shares_scratch + [parts_scratch, pltpu.VMEM((RES, SLAB, 2 * BINS), bf16), pltpu.VMEM((ROWS, SAMPLES), bf16)],
+        scratch_shapes=shares_scratch,
         compiler_params=big,
         cost_estimate=cost(3 * 10**9),
         name="across",
-    )(where, kept, far, sibling, passed, twiddle, common, cosines, sines, flip)
+    )(where, kept, near, far, cosines, sines, flip)
     along = pl.pallas_call(
         functools.partial(along_kernel, same),
         out_shape=(one,) * 4,

time: 59.4 us -> 58.3 us (0.981)
  Pallas kernels: 15.5 us -> 14 us
    pallas_call x1, Pallas kernels: 6.28 us -> 4.13 us  [shards(): pl.pallas_call(functools.partial(across_kernel, other), out_shape=(one,)...]
    pallas_call x1 -> x2, Pallas kernels: 1.19 us -> 2.71 us  [whitened(): pl.pallas_call(kernel, out_shape=spectra, in_specs=in_specs, out_specs=vm...]
    pallas_call x1, Pallas kernels: 3.73 us -> 3.07 us  [shards(): pl.pallas_call(functools.partial(along_kernel, same), out_shape=(one,) *...]
  transfers between devices with their start and end apart: 10 -> 10, of which waited for: 2 -> 4; matrix products, arithmetic and copies ran while one was open for 0% -> 0% of each run, Pallas kernels for 15% -> 14%
where the time goes in v7:
time: 58.3 us; the launch traced here: 57.8 us
  blocking collectives  20.5 us (35%)
  starting transfers between devices  18.4 us (32%)
  Pallas kernels  14 us (24%)
  waiting for transfers between devices  3.74 us (6%)
  local copies, waits for them, and re-layouts  0.97 us (2%)
    all_to_all x1, blocking collectives, shards(): lax.all_to_all(outgoing, 'sens', split_axis=0, concat_axis=0, tiled=True)  20.5 us
    ppermute x7, starting transfers between devices, exchanged(): lax.ppermute(part, 'hour', [(h, h ^ distance) for h in range(hours)])  9.37 us
    ppermute x1, starting transfers between devices, shards(): lax.ppermute(rows, 'sens', [(s, (s - 2) % sens) for s in range(sens)])  7.33 us
    pallas_call x1, Pallas kernels, shards(): pl.pallas_call(functools.partial(across_kernel, other), out_shape=(one,)...  4.13 us
    pallas_call x1, Pallas kernels, shards(): pl.pallas_call(own_kernel, out_shape=(pltpu.VMEM((RES + 1, PICKED + SLAB,...  3.74 us
    ppermute x7, waiting for transfers between devices, exchanged(): lax.ppermute(part, 'hour', [(h, h ^ distance) for h in range(hours)])  3.73 us
    pallas_call x1, Pallas kernels, shards(): pl.pallas_call(functools.partial(along_kernel, same), out_shape=(one,) *...  3.07 us
    pallas_call x2, Pallas kernels, whitened(): pl.pallas_call(kernel, out_shape=spectra, in_specs=in_specs, out_specs=vm...  2.71 us
  transfers between devices with their start and end apart: 10, of which 4 were waited for; matrix products, arithmetic and copies ran while one was open for 0% of the time, Pallas kernels for 14%

profile of v7, /device:TPU:1, one launch (start us, length us, event | category | flops | bytes accessed | tf_op | source)
XLA Modules:
  0.0 57.8 jit_solution(8893025247019797122)
XLA Ops:
  0.0 7.3 %collective-permute-start = (bf16[24,4096]{1,0:T(8,128)(2,1)}, bf16[24,4096]{1,0:T(8,128)(2,1)S(1)}, u32[]{:S(2)}, u32[]{:S(2)}) collective-permute-start(bf16[24,4096]{1,0:T(8,128)(2,1)} %bitcast.10), channel_id=1, source_target_pairs={{0,240},{8,248},{16,0},{24,8},{32,16},{40,24},{48,32},{56,40},{64,... | collective-permute-start | bytes 589832 | tf_op jit(solution)/shard_map/ppermute | solution.py:282
  7.3 1.0 %collective-permute-start.1 = (bf16[24,4096]{1,0:T(8,128)(2,1)}, bf16[24,4096]{1,0:T(8,128)(2,1)S(1)}, u32[]{:S(2)}, u32[]{:S(2)}) collective-permute-start(bf16[24,4096]{1,0:T(8,128)(2,1)} %bitcast.11), channel_id=1, source_target_pairs={{0,8},{8,0},{16,24},{24,16},{32,40},{40,32},{48,56},{56,48},{64,72... | collective-permute-start | bytes 589832 | tf_op jit(solution)/shard_map/ppermute | solution.py:283
  8.3 3.7 %own.1 = (bf16[17,224,256]{2,1,0:T(8,128)(2,1)S(1)}, bf16[128,64]{1,0:T(8,128)(2,1)S(1)}) custom-call(bf16[24,4096]{1,0:T(8,128)(2,1)} %bitcast.12, f32[2,16,512]{2,1,0:T(8,128)} %constant.21.clone.twiddle_any.twiddle_ref, bf16[2,1024,256]{2,1,0:T(8,128)(2,1)} %constant.22.clone.common_any.common_ref, s32[1,64]{1,0:T(1,128)} %bitcast.13, s32[1,64]{1,0:T(1,128)} %bitcast.14, ...), custom_call_target="tpu_custom_call" | custom-call | flops 1000000000 | bytes 1000000 | tf_op jit(solution)/shard_map/own/pallas_call | solution.py:297
  12.0 0.0 collective-permute-done.rows_ref
  12.1 0.7 %collective-permute-start.2 = (bf16[24,4096]{1,0:T(8,128)(2,1)S(1)}, bf16[24,4096]{1,0:T(8,128)(2,1)S(1)}, u32[]{:S(2)}, u32[]{:S(2)}) collective-permute-start(bf16[24,4096]{1,0:T(8,128)(2,1)S(1)} %collective-permute-done.rows_ref), channel_id=1, source_target_pairs={{0,8},{8,0},{16,24},{24,16},{32,40},{40,32},{48,56},{56,48},{64,72... | collective-permute-start | bytes 589832 | tf_op jit(solution)/shard_map/ppermute | solution.py:320
  12.8 0.1 pad_add_fusion.where_ref
  12.9 1.1 %farther.1.far_ref = bf16[16,32,256]{2,1,0:T(8,128)(2,1)S(1)} custom-call(bf16[24,4096]{1,0:T(8,128)(2,1)S(1)} %collective-permute-done.rows_ref, f32[2,16,512]{2,1,0:T(8,128)S(1)} %copy-done.3, bf16[2,1024,256]{2,1,0:T(8,128)(2,1)S(1)} %copy-done.2), custom_call_target="tpu_custom_call" | custom-call | flops 1000000000 | bytes 1000000 | tf_op jit(solution)/shard_map/farther/pallas_call | solution.py:323
  13.9 0.0 copy-start
  13.9 0.0 copy-start.4
  14.0 0.0 collective-permute-done.2.passed_ref
  14.0 1.6 %nearer.1.near_ref = bf16[16,32,256]{2,1,0:T(8,128)(2,1)S(1)} custom-call(s32[2]{0:T(128)S(1)} %pad_add_fusion.where_ref, bf16[24,4096]{1,0:T(8,128)(2,1)S(1)} %collective-permute-done.1.sibling_ref, bf16[24,4096]{1,0:T(8,128)(2,1)S(1)} %collective-permute-done.2.passed_ref, f32[2,16,512]{2,1,0:T(8,128)S(1)} %copy-done.3, bf16[2,1024,256]{2,1,0:T(8,128)(2,1)S(1)} %copy-done.2), custom_call_target="tpu_custom_call" | custom-call | flops 1000000000 | bytes 1000000 | tf_op jit(solution)/shard_map/nearer/pallas_call | solution.py:323
  15.6 0.0 copy-done
  15.7 4.1 %across.1 = (bf16[64,1152]{1,0:T(8,128)(2,1)S(1)}, bf16[64,1152]{1,0:T(8,128)(2,1)S(1)}, bf16[64,1152]{1,0:T(8,128)(2,1)S(1)}, bf16[64,1152]{1,0:T(8,128)(2,1)S(1)}, bf16[16,192,256]{2,1,0:T(8,128)(2,1)S(1)}) custom-call(s32[2]{0:T(128)S(1)} %pad_add_fusion.where_ref, bf16[17,224,256]{2,1,0:T(8,128)(2,1)S(1)} %get-tuple-element.20.kept_ref, ...), custom_call_target="tpu_custom_call" | custom-call | flops 3000000000 | bytes 1000000 | tf_op jit(solution)/shard_map/across/pallas_call | solution.py:341
  19.8 2.8 %collective-permute-start.3 = (bf16[64,1152]{1,0:T(8,128)(2,1)S(1)}, bf16[64,1152]{1,0:T(8,128)(2,1)S(1)}, u32[]{:S(2)}, u32[]{:S(2)}) collective-permute-start(bf16[64,1152]{1,0:T(8,128)(2,1)S(1)} %get-tuple-element.22), channel_id=1, source_target_pairs={{0,3},{1,2},{2,1},{3,0},{4,7},{5,6},{6,5},{7,4},{8,11},{9,10},{10,... | collective-permute-start | bytes 442376 | tf_op jit(solution)/shard_map/ppermute | solution.py:362
  22.6 0.4 collective-permute-start.4
  23.0 0.3 collective-permute-start.5
  23.3 3.1 %along.1 = (bf16[64,1152]{1,0:T(8,128)(2,1)S(1)}, bf16[64,1152]{1,0:T(8,128)(2,1)S(1)}, bf16[64,1152]{1,0:T(8,128)(2,1)S(1)}, bf16[64,1152]{1,0:T(8,128)(2,1)S(1)}) custom-call(s32[2]{0:T(128)S(1)} %pad_add_fusion.where_ref, bf16[17,224,256]{2,1,0:T(8,128)(2,1)S(1)} %get-tuple-element.20.kept_ref, ...), custom_call_target="tpu_custom_call" | custom-call | flops 3000000000 | bytes 1000000 | tf_op jit(solution)/shard_map/along/pallas_call | solution.py:351
  26.4 2.7 %collective-permute-start.7 = (bf16[64,1152]{1,0:T(8,128)(2,1)S(1)}, bf16[64,1152]{1,0:T(8,128)(2,1)S(1)}, u32[]{:S(2)}, u32[]{:S(2)}) collective-permute-start(bf16[64,1152]{1,0:T(8,128)(2,1)S(1)} %get-tuple-element.27), channel_id=1, source_target_pairs={{0,3},{1,2},{2,1},{3,0},{4,7},{5,6},{6,5},{7,4},{8,11},{9,10},{10,... | collective-permute-start | bytes 442376 | tf_op jit(solution)/shard_map/ppermute | solution.py:362
  29.0 0.4 collective-permute-start.8
  29.4 0.0 collective-permute-done.3.refs_0_
  29.4 0.3 collective-permute-start.9
  29.7 0.0 collective-permute-done.4.refs_1_
  29.7 0.4 collective-permute-done.5.refs_2_
  30.1 0.1 fold.1
  30.2 2.5 %collective-permute-start.6 = (bf16[64,1152]{1,0:T(8,128)(2,1)S(1)}, bf16[64,1152]{1,0:T(8,128)(2,1)S(1)}, u32[]{:S(2)}, u32[]{:S(2)}) collective-permute-start(bf16[64,1152]{1,0:T(8,128)(2,1)S(1)} %fold.1), channel_id=1, source_target_pairs={{0,4},{1,5},{2,6},{3,7},{4,0},{5,1},{6,2},{7,3},{8,12},{9,13},{10,... | collective-permute-start | bytes 442376 | tf_op jit(solution)/shard_map/ppermute | solution.py:362
  32.7 2.4 %collective-permute-done.7.refs_1_ = bf16[64,1152]{1,0:T(8,128)(2,1)S(1)} collective-permute-done((bf16[64,1152]{1,0:T(8,128)(2,1)S(1)}, bf16[64,1152]{1,0:T(8,128)(2,1)S(1)}, u32[]{:S(2)}, u32[]{:S(2)}) %collective-permute-start.7) | collective-permute-done | bytes 147488 | tf_op jit(solution)/shard_map/ppermute | solution.py:362
  35.1 0.5 collective-permute-done.9.refs_3_
  35.6 0.4 collective-permute-done.6.refs_0_
  36.1 0.3 collect.1
  36.3 0.1 all_to_all.6
  36.4 20.5 %all_to_all.9 = bf16[32,4,1152]{2,1,0:T(4,128)(2,1)S(1)} all-to-all(bf16[32,4,1152]{2,1,0:T(4,128)(2,1)S(1)} %all_to_all.6), channel_id=1, replica_groups=mesh['sens'=32,'hour'=8] {'sens'}, dimensions={0} | all-to-all | bytes 589824 | tf_op jit(solution)/shard_map/all_to_all | solution.py:383
  57.0 0.9 %reshape.20 = f32[128,1152]{1,0:T(8,128)} reshape(bf16[32,4,1152]{2,1,0:T(4,128)(2,1)S(1)} %all_to_all.9) | data formatting | bytes 884736 | tf_op jit(solution)/shard_map/convert_element_type | solution.py:384
  (9 shorter events, 0.0 us)
Async XLA Ops:
  0.0 12.8 %copy-start.3 = (f32[2,16,512]{2,1,0:T(8,128)S(1)}, f32[2,16,512]{2,1,0:T(8,128)}, u32[]{:S(2)}) copy-start(f32[2,16,512]{2,1,0:T(8,128)} %constant.21.clone.twiddle_any.twiddle_ref) | copy-start | bytes 196612
  0.0 12.8 %copy-start.2 = (bf16[2,1024,256]{2,1,0:T(8,128)(2,1)S(1)}, bf16[2,1024,256]{2,1,0:T(8,128)(2,1)}, u32[]{:S(2)}) copy-start(bf16[2,1024,256]{2,1,0:T(8,128)(2,1)} %constant.22.clone.common_any.common_ref) | copy-start | bytes 3145732
  0.0 12.0 %collective-permute-start = (bf16[24,4096]{1,0:T(8,128)(2,1)}, bf16[24,4096]{1,0:T(8,128)(2,1)S(1)}, u32[]{:S(2)}, u32[]{:S(2)}) collective-permute-start(bf16[24,4096]{1,0:T(8,128)(2,1)} %bitcast.10), channel_id=1, source_target_pairs={{0,240},{8,248},{16,0},{24,8},{32,16},{40,24},{48,32},{56,40},{64,... | collective-permute-start | bytes 589832 | tf_op jit(solution)/shard_map/ppermute | solution.py:282
  7.3 6.6 %collective-permute-start.1 = (bf16[24,4096]{1,0:T(8,128)(2,1)}, bf16[24,4096]{1,0:T(8,128)(2,1)S(1)}, u32[]{:S(2)}, u32[]{:S(2)}) collective-permute-start(bf16[24,4096]{1,0:T(8,128)(2,1)} %bitcast.11), channel_id=1, source_target_pairs={{0,8},{8,0},{16,24},{24,16},{32,40},{40,32},{48,56},{56,48},{64,72... | collective-permute-start | bytes 589832 | tf_op jit(solution)/shard_map/ppermute | solution.py:283
  12.1 1.9 %collective-permute-start.2 = (bf16[24,4096]{1,0:T(8,128)(2,1)S(1)}, bf16[24,4096]{1,0:T(8,128)(2,1)S(1)}, u32[]{:S(2)}, u32[]{:S(2)}) collective-permute-start(bf16[24,4096]{1,0:T(8,128)(2,1)S(1)} %collective-permute-done.rows_ref), channel_id=1, source_target_pairs={{0,8},{8,0},{16,24},{24,16},{32,40},{40,32},{48,56},{56,48},{64,72... | collective-permute-start | bytes 589832 | tf_op jit(solution)/shard_map/ppermute | solution.py:320
  12.9 2.8 %copy-start.1 = (bf16[2048,512]{1,0:T(8,128)(2,1)S(1)}, bf16[2048,512]{1,0:T(8,128)(2,1)}, u32[]{:S(2)}) copy-start(bf16[2048,512]{1,0:T(8,128)(2,1)} %constant.24.clone.sines_ref) | copy-start | bytes 6291460
  13.9 1.7 %copy-start = (bf16[2048,512]{1,0:T(8,128)(2,1)S(1)}, bf16[2048,512]{1,0:T(8,128)(2,1)}, u32[]{:S(2)}) copy-start(bf16[2048,512]{1,0:T(8,128)(2,1)} %constant.23.clone.cosines_ref) | copy-start | bytes 6291460
  13.9 1.7 %copy-start.4 = (bf16[128,128]{1,0:T(8,128)(2,1)S(1)}, bf16[128,128]{1,0:T(8,128)(2,1)}, u32[]{:S(2)}) copy-start(bf16[128,128]{1,0:T(8,128)(2,1)} %constant.25.clone.flip_ref) | copy-start | bytes 98308
  19.8 9.6 %collective-permute-start.3 = (bf16[64,1152]{1,0:T(8,128)(2,1)S(1)}, bf16[64,1152]{1,0:T(8,128)(2,1)S(1)}, u32[]{:S(2)}, u32[]{:S(2)}) collective-permute-start(bf16[64,1152]{1,0:T(8,128)(2,1)S(1)} %get-tuple-element.22), channel_id=1, source_target_pairs={{0,3},{1,2},{2,1},{3,0},{4,7},{5,6},{6,5},{7,4},{8,11},{9,10},{10,... | collective-permute-start | bytes 442376 | tf_op jit(solution)/shard_map/ppermute | solution.py:362
  22.6 7.1 %collective-permute-start.4 = (bf16[64,1152]{1,0:T(8,128)(2,1)S(1)}, bf16[64,1152]{1,0:T(8,128)(2,1)S(1)}, u32[]{:S(2)}, u32[]{:S(2)}) collective-permute-start(bf16[64,1152]{1,0:T(8,128)(2,1)S(1)} %get-tuple-element.23), channel_id=1, source_target_pairs={{0,2},{1,3},{2,0},{3,1},{4,6},{5,7},{6,4},{7,5},{8,10},{9,11},{10,... | collective-permute-start | bytes 442376 | tf_op jit(solution)/shard_map/ppermute | solution.py:362
  23.0 7.1 %collective-permute-start.5 = (bf16[64,1152]{1,0:T(8,128)(2,1)S(1)}, bf16[64,1152]{1,0:T(8,128)(2,1)S(1)}, u32[]{:S(2)}, u32[]{:S(2)}) collective-permute-start(bf16[64,1152]{1,0:T(8,128)(2,1)S(1)} %get-tuple-element.24), channel_id=1, source_target_pairs={{0,1},{1,0},{2,3},{3,2},{4,5},{5,4},{6,7},{7,6},{8,9},{9,8},{10,11... | collective-permute-start | bytes 442376 | tf_op jit(solution)/shard_map/ppermute | solution.py:362
  26.4 8.8 %collective-permute-start.7 = (bf16[64,1152]{1,0:T(8,128)(2,1)S(1)}, bf16[64,1152]{1,0:T(8,128)(2,1)S(1)}, u32[]{:S(2)}, u32[]{:S(2)}) collective-permute-start(bf16[64,1152]{1,0:T(8,128)(2,1)S(1)} %get-tuple-element.27), channel_id=1, source_target_pairs={{0,3},{1,2},{2,1},{3,0},{4,7},{5,6},{6,5},{7,4},{8,11},{9,10},{10,... | collective-permute-start | bytes 442376 | tf_op jit(solution)/shard_map/ppermute | solution.py:362
  29.0 6.1 %collective-permute-start.8 = (bf16[64,1152]{1,0:T(8,128)(2,1)S(1)}, bf16[64,1152]{1,0:T(8,128)(2,1)S(1)}, u32[]{:S(2)}, u32[]{:S(2)}) collective-permute-start(bf16[64,1152]{1,0:T(8,128)(2,1)S(1)} %get-tuple-element.28), channel_id=1, source_target_pairs={{0,2},{1,3},{2,0},{3,1},{4,6},{5,7},{6,4},{7,5},{8,10},{9,11},{10,... | collective-permute-start | bytes 442376 | tf_op jit(solution)/shard_map/ppermute | solution.py:362
  29.4 6.3 %collective-permute-start.9 = (bf16[64,1152]{1,0:T(8,128)(2,1)S(1)}, bf16[64,1152]{1,0:T(8,128)(2,1)S(1)}, u32[]{:S(2)}, u32[]{:S(2)}) collective-permute-start(bf16[64,1152]{1,0:T(8,128)(2,1)S(1)} %get-tuple-element.29), channel_id=1, source_target_pairs={{0,1},{1,0},{2,3},{3,2},{4,5},{5,4},{6,7},{7,6},{8,9},{9,8},{10,11... | collective-permute-start | bytes 442376 | tf_op jit(solution)/shard_map/ppermute | solution.py:362
  30.2 5.9 %collective-permute-start.6 = (bf16[64,1152]{1,0:T(8,128)(2,1)S(1)}, bf16[64,1152]{1,0:T(8,128)(2,1)S(1)}, u32[]{:S(2)}, u32[]{:S(2)}) collective-permute-start(bf16[64,1152]{1,0:T(8,128)(2,1)S(1)} %fold.1), channel_id=1, source_target_pairs={{0,4},{1,5},{2,6},{3,7},{4,0},{5,1},{6,2},{7,3},{8,12},{9,13},{10,... | collective-permute-start | bytes 442376 | tf_op jit(solution)/shard_map/ppermute | solution.py:362

commit v8 on v7

--- a/solution.py
+++ b/solution.py
@@ -158,16 +158,16 @@
     forward(lambda columns: rows_ref[:, columns], twiddle_ref, common_ref, parts_ref, store)
 
 
-def nearer_kernel(where_ref, sibling_ref, passed_ref, twiddle_ref, common_ref, white_ref, parts_ref):
-    odd = where_ref[1] != 0
+def nearer_kernel(sibling_ref, passed_ref, twiddle_ref, common_ref, white_ref, parts_ref):
+    odd = lax.axis_index("sens") & 1
 
     def store(k, value):
         white_ref[k] = padded(value)
 
-    def load(columns):
-        return jnp.where(odd, passed_ref[:, columns].astype(jnp.float32), sibling_ref[:, columns].astype(jnp.float32))
-
-    forward(load, twiddle_ref, common_ref, parts_ref, store)
+    for parity, rows_ref in ((0, sibling_ref), (1, passed_ref)):
+        @pl.when(odd == parity)
+        def _(rows_ref=rows_ref):
+            forward(lambda columns: rows_ref[:, columns], twiddle_ref, common_ref, parts_ref, store)
 
 
 def shares(distances, hour, kept_ref, second_rows_ref, cosines_ref, sines_ref, flip_ref, out_refs, cross_ref, tile_ref,
@@ -233,7 +233,7 @@
             out_ref[:, u * TILE : (u + 1) * TILE] = tile_ref[begin + u]
 
 
-def across_kernel(distances, where_ref, kept_ref, near_ref, far_ref, cosines_ref, sines_ref, flip_ref, *refs):
+def across_kernel(distances, kept_ref, near_ref, far_ref, cosines_ref, sines_ref, flip_ref, *refs):
     *out_refs, second_rows_ref, cross_ref, tile_ref = refs
     pick = kept_ref[RES, pl.ds(0, PICKED), pl.ds(0, TILE)][:, : 3 * SLAB]
 
@@ -242,13 +242,13 @@
         second = jnp.dot(pick, spectra, preferred_element_type=jnp.float32)
         second_rows_ref[k] = second.astype(jnp.bfloat16)
 
-    shares(distances, where_ref[0], kept_ref, second_rows_ref, cosines_ref, sines_ref, flip_ref, out_refs, cross_ref,
+    shares(distances, lax.axis_index("hour"), kept_ref, second_rows_ref, cosines_ref, sines_ref, flip_ref, out_refs, cross_ref,
            tile_ref, prepare)
 
 
-def along_kernel(distances, where_ref, kept_ref, second_rows_ref, cosines_ref, sines_ref, flip_ref, *refs):
+def along_kernel(distances, kept_ref, second_rows_ref, cosines_ref, sines_ref, flip_ref, *refs):
     *out_refs, cross_ref, tile_ref = refs
-    shares(distances, where_ref[0], kept_ref, second_rows_ref, cosines_ref, sines_ref, flip_ref, out_refs, cross_ref,
+    shares(distances, lax.axis_index("hour"), kept_ref, second_rows_ref, cosines_ref, sines_ref, flip_ref, out_refs, cross_ref,
            tile_ref)
 
 
@@ -281,10 +281,8 @@
     swap = [(s, s ^ 1) for s in range(sens)]
     farther = lax.ppermute(rows, "sens", [(s, (s - 2) % sens) for s in range(sens)])
     sibling = lax.ppermute(rows, "sens", swap)
-    where = jnp.stack([lax.axis_index("hour"), lax.axis_index("sens") & 1]).astype(jnp.int32)
 
     vmem = pl.BlockSpec(memory_space=pltpu.VMEM)
-    smem = pl.BlockSpec(memory_space=pltpu.SMEM)
     hbm = pl.BlockSpec(memory_space=pltpu.HBM)
     parts_scratch = pltpu.VMEM((RES * ROWS, 2 * SPAN), f32)
     params = pltpu.CompilerParams(vmem_limit_bytes=16 * MIB)
@@ -313,7 +311,7 @@
             pltpu.SemaphoreType.DMA((6,)),
         ],
         compiler_params=pltpu.CompilerParams(vmem_limit_bytes=56 * MIB),
-        cost_estimate=cost(10**9),
+        cost_estimate=cost(10000000000),
         name="own",
     )(rows, twiddle, common, *(v.reshape(1, PAIRS) for v in (pair_first, pair_second, owners)))
     farther, place = lax.optimization_barrier((farther, place))
@@ -327,12 +325,12 @@
             out_specs=vmem,
             scratch_shapes=[parts_scratch],
             compiler_params=params,
-            cost_estimate=cost(10**9),
+            cost_estimate=cost(700000000),
             name=name,
         )(*args, twiddle, common)
 
     far = whitened(farther_kernel, "farther", [vmem] * 3, (farther,))
-    near = whitened(nearer_kernel, "nearer", [smem] + [vmem] * 4, (where, sibling, passed))
+    near = whitened(nearer_kernel, "nearer", [vmem] * 4, (sibling, passed))
     one = jax.ShapeDtypeStruct((PAIRS, share), bf16)
     half = COMPS * COMPS // 2 + 1
     shares_scratch = [pltpu.VMEM((half, PAIRS, 2 * NB), bf16), pltpu.VMEM((half * LAGS // TILE, PAIRS, TILE), bf16)]
@@ -341,36 +339,48 @@
     *across, second_rows = pl.pallas_call(
         functools.partial(across_kernel, other),
         out_shape=(one,) * 4 + (jax.ShapeDtypeStruct((RES, PICKED, 2 * BINS), bf16),),
-        in_specs=[smem] + [vmem] * 6,
+        in_specs=[vmem] * 6,
         out_specs=(vmem,) * 5,
         scratch_shapes=shares_scratch,
         compiler_params=big,
         cost_estimate=cost(3 * 10**9),
         name="across",
-    )(where, kept, near, far, cosines, sines, flip)
+    )(kept, near, far, cosines, sines, flip)
     along = pl.pallas_call(
         functools.partial(along_kernel, same),
         out_shape=(one,) * 4,
-        in_specs=[smem] + [vmem] * 5,
+        in_specs=[vmem] * 5,
         out_specs=(vmem,) * 4,
         scratch_shapes=shares_scratch,
         compiler_params=big,
         cost_estimate=cost(3 * 10**9),
         name="along",
-    )(where, kept, second_rows, cosines, sines, flip)
+    )(kept, second_rows, cosines, sines, flip)
     def exchanged(part, distance):
         return lax.ppermute(part, "hour", [(h, h ^ distance) for h in range(hours)]) if distance else part
 
-    folded = pl.pallas_call(
-        fold_kernel,
-        out_shape=one,
-        in_specs=[vmem] * 4,
-        out_specs=vmem,
-        compiler_params=params,
-        cost_estimate=cost(10**7),
-        name="fold",
-    )(*(exchanged(part, distance & 3) for distance, part in zip(other, across)))
-    parts = [exchanged(folded, 4)] + [exchanged(part, distance) for distance, part in zip(same, along)]
+    def fold(*shares_here):
+        return pl.pallas_call(
+            fold_kernel,
+            out_shape=one,
+            in_specs=[vmem] * len(shares_here),
+            out_specs=vmem,
+            compiler_params=params,
+            cost_estimate=cost(10**7),
+            name="fold",
+        )(*shares_here)
+
+    far_y, far_two, far_one, far_here = across
+    same_y, same_two, same_one, same_here = along
+    joined = exchanged(far_two, 4)
+    folded = fold(exchanged(far_y, 3), exchanged(far_one, 1), far_here)
+    parts = [
+        exchanged(folded, 4),
+        exchanged(same_y, 3),
+        exchanged(same_one, 1),
+        exchanged(fold(same_two, joined), 2),
+        same_here,
+    ]
     outgoing = pl.pallas_call(
         collect_kernel,
         out_shape=jax.ShapeDtypeStruct((slots, share), bf16),

time: 58.3 us -> 57.2 us (0.981)
  Pallas kernels: 14 us -> 12.3 us
  waiting for transfers between devices: 3.74 us -> 4.88 us
    ppermute x7, waiting for transfers between devices: 3.73 us -> 4.87 us  [exchanged(): lax.ppermute(part, 'hour', [(h, h ^ distance) for h in range(hours)])]
    pallas_call x1, Pallas kernels: 4.13 us -> 3.51 us  [shards(): pl.pallas_call(functools.partial(across_kernel, other), out_shape=(one,)...]
    pallas_call x1, Pallas kernels: 3.07 us -> 2.45 us  [shards(): pl.pallas_call(functools.partial(along_kernel, same), out_shape=(one,) *...]
  transfers between devices with their start and end apart: 10 -> 10, of which waited for: 4 -> 3; matrix products, arithmetic and copies ran while one was open for 0% -> 0% of each run, Pallas kernels for 14% -> 13%
where the time goes in v8:
time: 57.2 us; the launch traced here: 57.1 us
  blocking collectives  20 us (35%)
  starting transfers between devices  18.8 us (33%)
  Pallas kernels  12.3 us (22%)
  waiting for transfers between devices  4.88 us (9%)
  local copies, waits for them, and re-layouts  0.96 us (2%)
    all_to_all x1, blocking collectives, shards(): lax.all_to_all(outgoing, 'sens', split_axis=0, concat_axis=0, tiled=True)  20 us
    ppermute x7, starting transfers between devices, exchanged(): lax.ppermute(part, 'hour', [(h, h ^ distance) for h in range(hours)])  9.91 us
    ppermute x1, starting transfers between devices, shards(): lax.ppermute(rows, 'sens', [(s, (s - 2) % sens) for s in range(sens)])  7.33 us
    ppermute x7, waiting for transfers between devices, exchanged(): lax.ppermute(part, 'hour', [(h, h ^ distance) for h in range(hours)])  4.87 us
    pallas_call x1, Pallas kernels, shards(): pl.pallas_call(own_kernel, out_shape=(pltpu.VMEM((RES + 1, PICKED + SLAB,...  3.81 us
    pallas_call x1, Pallas kernels, shards(): pl.pallas_call(functools.partial(across_kernel, other), out_shape=(one,)...  3.51 us
    pallas_call x1, Pallas kernels, shards(): pl.pallas_call(functools.partial(along_kernel, same), out_shape=(one,) *...  2.45 us
    pallas_call x2, Pallas kernels, whitened(): pl.pallas_call(kernel, out_shape=spectra, in_specs=in_specs, out_specs=vm...  2.16 us
  transfers between devices with their start and end apart: 10, of which 3 were waited for; matrix products, arithmetic and copies ran while one was open for 0% of the time, Pallas kernels for 13%

profile of v8, /device:TPU:1, one launch (start us, length us, event | category | flops | bytes accessed | tf_op | source)
XLA Modules:
  0.0 57.1 jit_solution(3527270733963531661)
XLA Ops:
  0.0 7.3 %collective-permute-start = (bf16[24,4096]{1,0:T(8,128)(2,1)}, bf16[24,4096]{1,0:T(8,128)(2,1)S(1)}, u32[]{:S(2)}, u32[]{:S(2)}) collective-permute-start(bf16[24,4096]{1,0:T(8,128)(2,1)} %bitcast.8), channel_id=1, source_target_pairs={{0,240},{8,248},{16,0},{24,8},{32,16},{40,24},{48,32},{56,40},{64,... | collective-permute-start | bytes 589832 | tf_op jit(solution)/shard_map/ppermute | solution.py:282
  7.3 1.0 %collective-permute-start.1 = (bf16[24,4096]{1,0:T(8,128)(2,1)}, bf16[24,4096]{1,0:T(8,128)(2,1)S(1)}, u32[]{:S(2)}, u32[]{:S(2)}) collective-permute-start(bf16[24,4096]{1,0:T(8,128)(2,1)} %bitcast.9), channel_id=1, source_target_pairs={{0,8},{8,0},{16,24},{24,16},{32,40},{40,32},{48,56},{56,48},{64,72... | collective-permute-start | bytes 589832 | tf_op jit(solution)/shard_map/ppermute | solution.py:283
  8.3 3.8 %own.1 = (bf16[17,224,256]{2,1,0:T(8,128)(2,1)S(1)}, bf16[128,64]{1,0:T(8,128)(2,1)S(1)}) custom-call(bf16[24,4096]{1,0:T(8,128)(2,1)} %bitcast.10, f32[2,16,512]{2,1,0:T(8,128)} %constant.10.clone.twiddle_any.twiddle_ref, bf16[2,1024,256]{2,1,0:T(8,128)(2,1)} %constant.11.clone.common_any.common_ref, s32[1,64]{1,0:T(1,128)} %bitcast.11, s32[1,64]{1,0:T(1,128)} %bitcast.12, ...), custom_call_target="tpu_custom_call" | custom-call | flops 10000000000 | bytes 1000000 | tf_op jit(solution)/shard_map/own/pallas_call | solution.py:295
  12.1 0.0 collective-permute-done.rows_ref
  12.1 0.0 copy-start
  12.1 0.0 copy-start.1
  12.1 0.0 copy-start.4
  12.2 0.6 %collective-permute-start.2 = (bf16[24,4096]{1,0:T(8,128)(2,1)S(1)}, bf16[24,4096]{1,0:T(8,128)(2,1)S(1)}, u32[]{:S(2)}, u32[]{:S(2)}) collective-permute-start(bf16[24,4096]{1,0:T(8,128)(2,1)S(1)} %collective-permute-done.rows_ref), channel_id=1, source_target_pairs={{0,8},{8,0},{16,24},{24,16},{32,40},{40,32},{48,56},{56,48},{64,72... | collective-permute-start | bytes 589832 | tf_op jit(solution)/shard_map/ppermute | solution.py:318
  12.8 1.1 %farther.1.far_ref = bf16[16,32,256]{2,1,0:T(8,128)(2,1)S(1)} custom-call(bf16[24,4096]{1,0:T(8,128)(2,1)S(1)} %collective-permute-done.rows_ref, f32[2,16,512]{2,1,0:T(8,128)S(1)} %copy-done.3, bf16[2,1024,256]{2,1,0:T(8,128)(2,1)S(1)} %copy-done.2), custom_call_target="tpu_custom_call" | custom-call | flops 700000000 | bytes 1000000 | tf_op jit(solution)/shard_map/farther/pallas_call | solution.py:321
  13.9 0.0 collective-permute-done.1.sibling_ref
  13.9 0.0 collective-permute-done.2.passed_ref
  13.9 1.1 %nearer.1.near_ref = bf16[16,32,256]{2,1,0:T(8,128)(2,1)S(1)} custom-call(bf16[24,4096]{1,0:T(8,128)(2,1)S(1)} %collective-permute-done.1.sibling_ref, bf16[24,4096]{1,0:T(8,128)(2,1)S(1)} %collective-permute-done.2.passed_ref, f32[2,16,512]{2,1,0:T(8,128)S(1)} %copy-done.3, bf16[2,1024,256]{2,1,0:T(8,128)(2,1)S(1)} %copy-done.2), custom_call_target="tpu_custom_call" | custom-call | flops 700000000 | bytes 1000000 | tf_op jit(solution)/shard_map/nearer/pallas_call | solution.py:321
  15.0 3.5 %across.1 = (bf16[64,1152]{1,0:T(8,128)(2,1)S(1)}, bf16[64,1152]{1,0:T(8,128)(2,1)S(1)}, bf16[64,1152]{1,0:T(8,128)(2,1)S(1)}, bf16[64,1152]{1,0:T(8,128)(2,1)S(1)}, bf16[16,192,256]{2,1,0:T(8,128)(2,1)S(1)}) custom-call(bf16[17,224,256]{2,1,0:T(8,128)(2,1)S(1)} %get-tuple-element.20.kept_ref, bf16[16,32,256]{2,1,0:T(8,128)(2,1)S(1)} %nearer.1.near_ref, ...), custom_call_target="tpu_custom_call" | custom-call | flops 3000000000 | bytes 1000000 | tf_op jit(solution)/shard_map/across/pallas_call | solution.py:339
  18.5 2.8 %collective-permute-start.3 = (bf16[64,1152]{1,0:T(8,128)(2,1)S(1)}, bf16[64,1152]{1,0:T(8,128)(2,1)S(1)}, u32[]{:S(2)}, u32[]{:S(2)}) collective-permute-start(bf16[64,1152]{1,0:T(8,128)(2,1)S(1)} %get-tuple-element.22), channel_id=1, source_target_pairs={{0,3},{1,2},{2,1},{3,0},{4,7},{5,6},{6,5},{7,4},{8,11},{9,10},{10,... | collective-permute-start | bytes 442376 | tf_op jit(solution)/shard_map/ppermute | solution.py:360
  21.3 0.0 collective-permute-start.4
  21.3 2.5 %collective-permute-start.8 = (bf16[64,1152]{1,0:T(8,128)(2,1)S(1)}, bf16[64,1152]{1,0:T(8,128)(2,1)S(1)}, u32[]{:S(2)}, u32[]{:S(2)}) collective-permute-start(bf16[64,1152]{1,0:T(8,128)(2,1)S(1)} %get-tuple-element.29), channel_id=1, source_target_pairs={{0,4},{1,5},{2,6},{3,7},{4,0},{5,1},{6,2},{7,3},{8,12},{9,13},{10,... | collective-permute-start | bytes 442376 | tf_op jit(solution)/shard_map/ppermute | solution.py:360
  23.8 2.5 %along.1 = (bf16[64,1152]{1,0:T(8,128)(2,1)S(1)}, bf16[64,1152]{1,0:T(8,128)(2,1)S(1)}, bf16[64,1152]{1,0:T(8,128)(2,1)S(1)}, bf16[64,1152]{1,0:T(8,128)(2,1)S(1)}) custom-call(bf16[17,224,256]{2,1,0:T(8,128)(2,1)S(1)} %get-tuple-element.20.kept_ref, bf16[16,192,256]{2,1,0:T(8,128)(2,1)S(1)} %get-tuple-element.25.second_rows_ref, ...), custom_call_target="tpu_custom_call" | custom-call | flops 3000000000 | bytes 1000000 | tf_op jit(solution)/shard_map/along/pallas_call | solution.py:349
  26.3 0.7 %collective-permute-start.6 = (bf16[64,1152]{1,0:T(8,128)(2,1)S(1)}, bf16[64,1152]{1,0:T(8,128)(2,1)S(1)}, u32[]{:S(2)}, u32[]{:S(2)}) collective-permute-start(bf16[64,1152]{1,0:T(8,128)(2,1)S(1)} %get-tuple-element.26), channel_id=1, source_target_pairs={{0,3},{1,2},{2,1},{3,0},{4,7},{5,6},{6,5},{7,4},{8,11},{9,10},{10,... | collective-permute-start | bytes 442376 | tf_op jit(solution)/shard_map/ppermute | solution.py:360
  27.0 0.9 %collective-permute-start.7 = (bf16[64,1152]{1,0:T(8,128)(2,1)S(1)}, bf16[64,1152]{1,0:T(8,128)(2,1)S(1)}, u32[]{:S(2)}, u32[]{:S(2)}) collective-permute-start(bf16[64,1152]{1,0:T(8,128)(2,1)S(1)} %get-tuple-element.27), channel_id=1, source_target_pairs={{0,1},{1,0},{2,3},{3,2},{4,5},{5,4},{6,7},{7,6},{8,9},{9,8},{10,11... | collective-permute-start | bytes 442376 | tf_op jit(solution)/shard_map/ppermute | solution.py:360
  27.9 0.0 collective-permute-done.3.refs_0_
  27.9 0.0 collective-permute-done.4.refs_1_
  27.9 0.1 fold.2
  28.0 0.8 %collective-permute-start.5 = (bf16[64,1152]{1,0:T(8,128)(2,1)S(1)}, bf16[64,1152]{1,0:T(8,128)(2,1)S(1)}, u32[]{:S(2)}, u32[]{:S(2)}) collective-permute-start(bf16[64,1152]{1,0:T(8,128)(2,1)S(1)} %fold.2), channel_id=1, source_target_pairs={{0,4},{1,5},{2,6},{3,7},{4,0},{5,1},{6,2},{7,3},{8,12},{9,13},{10,... | collective-permute-start | bytes 442376 | tf_op jit(solution)/shard_map/ppermute | solution.py:360
  28.8 0.0 collective-permute-done.8.refs_1_
  28.8 2.2 %collective-permute-start.9 = (bf16[64,1152]{1,0:T(8,128)(2,1)S(1)}, bf16[64,1152]{1,0:T(8,128)(2,1)S(1)}, u32[]{:S(2)}, u32[]{:S(2)}) collective-permute-start(bf16[64,1152]{1,0:T(8,128)(2,1)S(1)} %fold.3), channel_id=1, source_target_pairs={{0,2},{1,3},{2,0},{3,1},{4,6},{5,7},{6,4},{7,5},{8,10},{9,11},{10,... | collective-permute-start | bytes 442376 | tf_op jit(solution)/shard_map/ppermute | solution.py:360
  31.0 0.9 %collective-permute-done.6.refs_1_ = bf16[64,1152]{1,0:T(8,128)(2,1)S(1)} collective-permute-done((bf16[64,1152]{1,0:T(8,128)(2,1)S(1)}, bf16[64,1152]{1,0:T(8,128)(2,1)S(1)}, u32[]{:S(2)}, u32[]{:S(2)}) %collective-permute-start.6) | collective-permute-done | bytes 147488 | tf_op jit(solution)/shard_map/ppermute | solution.py:360
  31.9 1.7 %collective-permute-done.5.refs_0_ = bf16[64,1152]{1,0:T(8,128)(2,1)S(1)} collective-permute-done((bf16[64,1152]{1,0:T(8,128)(2,1)S(1)}, bf16[64,1152]{1,0:T(8,128)(2,1)S(1)}, u32[]{:S(2)}, u32[]{:S(2)}) %collective-permute-start.5) | collective-permute-done | bytes 147488 | tf_op jit(solution)/shard_map/ppermute | solution.py:360
  33.6 2.3 %collective-permute-done.9.refs_3_ = bf16[64,1152]{1,0:T(8,128)(2,1)S(1)} collective-permute-done((bf16[64,1152]{1,0:T(8,128)(2,1)S(1)}, bf16[64,1152]{1,0:T(8,128)(2,1)S(1)}, u32[]{:S(2)}, u32[]{:S(2)}) %collective-permute-start.9) | collective-permute-done | bytes 147488 | tf_op jit(solution)/shard_map/ppermute | solution.py:360
  35.9 0.3 collect.1
  36.1 0.1 all_to_all.6
  36.2 20.0 %all_to_all.9 = bf16[32,4,1152]{2,1,0:T(4,128)(2,1)S(1)} all-to-all(bf16[32,4,1152]{2,1,0:T(4,128)(2,1)S(1)} %all_to_all.6), channel_id=1, replica_groups=mesh['sens'=32,'hour'=8] {'sens'}, dimensions={0} | all-to-all | bytes 589824 | tf_op jit(solution)/shard_map/all_to_all | solution.py:393
  56.3 0.9 %reshape.20 = f32[128,1152]{1,0:T(8,128)} reshape(bf16[32,4,1152]{2,1,0:T(4,128)(2,1)S(1)} %all_to_all.9) | data formatting | bytes 884736 | tf_op jit(solution)/shard_map/convert_element_type | solution.py:394
  (9 shorter events, 0.1 us)
Async XLA Ops:
  0.0 12.1 %collective-permute-start = (bf16[24,4096]{1,0:T(8,128)(2,1)}, bf16[24,4096]{1,0:T(8,128)(2,1)S(1)}, u32[]{:S(2)}, u32[]{:S(2)}) collective-permute-start(bf16[24,4096]{1,0:T(8,128)(2,1)} %bitcast.8), channel_id=1, source_target_pairs={{0,240},{8,248},{16,0},{24,8},{32,16},{40,24},{48,32},{56,40},{64,... | collective-permute-start | bytes 589832 | tf_op jit(solution)/shard_map/ppermute | solution.py:282
  7.3 6.5 %collective-permute-start.1 = (bf16[24,4096]{1,0:T(8,128)(2,1)}, bf16[24,4096]{1,0:T(8,128)(2,1)S(1)}, u32[]{:S(2)}, u32[]{:S(2)}) collective-permute-start(bf16[24,4096]{1,0:T(8,128)(2,1)} %bitcast.9), channel_id=1, source_target_pairs={{0,8},{8,0},{16,24},{24,16},{32,40},{40,32},{48,56},{56,48},{64,72... | collective-permute-start | bytes 589832 | tf_op jit(solution)/shard_map/ppermute | solution.py:283
  8.3 4.5 %copy-start.2 = (bf16[2,1024,256]{2,1,0:T(8,128)(2,1)S(1)}, bf16[2,1024,256]{2,1,0:T(8,128)(2,1)}, u32[]{:S(2)}) copy-start(bf16[2,1024,256]{2,1,0:T(8,128)(2,1)} %constant.11.clone.common_any.common_ref) | copy-start | bytes 3145732
  8.3 4.5 %copy-start.3 = (f32[2,16,512]{2,1,0:T(8,128)S(1)}, f32[2,16,512]{2,1,0:T(8,128)}, u32[]{:S(2)}) copy-start(f32[2,16,512]{2,1,0:T(8,128)} %constant.10.clone.twiddle_any.twiddle_ref) | copy-start | bytes 196612
  12.1 2.9 %copy-start = (bf16[2048,512]{1,0:T(8,128)(2,1)S(1)}, bf16[2048,512]{1,0:T(8,128)(2,1)}, u32[]{:S(2)}) copy-start(bf16[2048,512]{1,0:T(8,128)(2,1)} %constant.12.clone.cosines_ref) | copy-start | bytes 6291460
  12.1 2.9 %copy-start.1 = (bf16[2048,512]{1,0:T(8,128)(2,1)S(1)}, bf16[2048,512]{1,0:T(8,128)(2,1)}, u32[]{:S(2)}) copy-start(bf16[2048,512]{1,0:T(8,128)(2,1)} %constant.13.clone.sines_ref) | copy-start | bytes 6291460
  12.1 2.9 %copy-start.4 = (bf16[128,128]{1,0:T(8,128)(2,1)S(1)}, bf16[128,128]{1,0:T(8,128)(2,1)}, u32[]{:S(2)}) copy-start(bf16[128,128]{1,0:T(8,128)(2,1)} %constant.14.clone.flip_ref) | copy-start | bytes 98308
  12.2 1.7 %collective-permute-start.2 = (bf16[24,4096]{1,0:T(8,128)(2,1)S(1)}, bf16[24,4096]{1,0:T(8,128)(2,1)S(1)}, u32[]{:S(2)}, u32[]{:S(2)}) collective-permute-start(bf16[24,4096]{1,0:T(8,128)(2,1)S(1)} %collective-permute-done.rows_ref), channel_id=1, source_target_pairs={{0,8},{8,0},{16,24},{24,16},{32,40},{40,32},{48,56},{56,48},{64,72... | collective-permute-start | bytes 589832 | tf_op jit(solution)/shard_map/ppermute | solution.py:318
  18.5 9.4 %collective-permute-start.3 = (bf16[64,1152]{1,0:T(8,128)(2,1)S(1)}, bf16[64,1152]{1,0:T(8,128)(2,1)S(1)}, u32[]{:S(2)}, u32[]{:S(2)}) collective-permute-start(bf16[64,1152]{1,0:T(8,128)(2,1)S(1)} %get-tuple-element.22), channel_id=1, source_target_pairs={{0,3},{1,2},{2,1},{3,0},{4,7},{5,6},{6,5},{7,4},{8,11},{9,10},{10,... | collective-permute-start | bytes 442376 | tf_op jit(solution)/shard_map/ppermute | solution.py:360
  21.3 6.6 %collective-permute-start.4 = (bf16[64,1152]{1,0:T(8,128)(2,1)S(1)}, bf16[64,1152]{1,0:T(8,128)(2,1)S(1)}, u32[]{:S(2)}, u32[]{:S(2)}) collective-permute-start(bf16[64,1152]{1,0:T(8,128)(2,1)S(1)} %get-tuple-element.23), channel_id=1, source_target_pairs={{0,1},{1,0},{2,3},{3,2},{4,5},{5,4},{6,7},{7,6},{8,9},{9,8},{10,11... | collective-permute-start | bytes 442376 | tf_op jit(solution)/shard_map/ppermute | solution.py:360
  21.3 7.4 %collective-permute-start.8 = (bf16[64,1152]{1,0:T(8,128)(2,1)S(1)}, bf16[64,1152]{1,0:T(8,128)(2,1)S(1)}, u32[]{:S(2)}, u32[]{:S(2)}) collective-permute-start(bf16[64,1152]{1,0:T(8,128)(2,1)S(1)} %get-tuple-element.29), channel_id=1, source_target_pairs={{0,4},{1,5},{2,6},{3,7},{4,0},{5,1},{6,2},{7,3},{8,12},{9,13},{10,... | collective-permute-start | bytes 442376 | tf_op jit(solution)/shard_map/ppermute | solution.py:360
  26.3 5.6 %collective-permute-start.6 = (bf16[64,1152]{1,0:T(8,128)(2,1)S(1)}, bf16[64,1152]{1,0:T(8,128)(2,1)S(1)}, u32[]{:S(2)}, u32[]{:S(2)}) collective-permute-start(bf16[64,1152]{1,0:T(8,128)(2,1)S(1)} %get-tuple-element.26), channel_id=1, source_target_pairs={{0,3},{1,2},{2,1},{3,0},{4,7},{5,6},{6,5},{7,4},{8,11},{9,10},{10,... | collective-permute-start | bytes 442376 | tf_op jit(solution)/shard_map/ppermute | solution.py:360
  27.0 4.9 %collective-permute-start.7 = (bf16[64,1152]{1,0:T(8,128)(2,1)S(1)}, bf16[64,1152]{1,0:T(8,128)(2,1)S(1)}, u32[]{:S(2)}, u32[]{:S(2)}) collective-permute-start(bf16[64,1152]{1,0:T(8,128)(2,1)S(1)} %get-tuple-element.27), channel_id=1, source_target_pairs={{0,1},{1,0},{2,3},{3,2},{4,5},{5,4},{6,7},{7,6},{8,9},{9,8},{10,11... | collective-permute-start | bytes 442376 | tf_op jit(solution)/shard_map/ppermute | solution.py:360
  28.0 5.6 %collective-permute-start.5 = (bf16[64,1152]{1,0:T(8,128)(2,1)S(1)}, bf16[64,1152]{1,0:T(8,128)(2,1)S(1)}, u32[]{:S(2)}, u32[]{:S(2)}) collective-permute-start(bf16[64,1152]{1,0:T(8,128)(2,1)S(1)} %fold.2), channel_id=1, source_target_pairs={{0,4},{1,5},{2,6},{3,7},{4,0},{5,1},{6,2},{7,3},{8,12},{9,13},{10,... | collective-permute-start | bytes 442376 | tf_op jit(solution)/shard_map/ppermute | solution.py:360
  28.8 7.1 %collective-permute-start.9 = (bf16[64,1152]{1,0:T(8,128)(2,1)S(1)}, bf16[64,1152]{1,0:T(8,128)(2,1)S(1)}, u32[]{:S(2)}, u32[]{:S(2)}) collective-permute-start(bf16[64,1152]{1,0:T(8,128)(2,1)S(1)} %fold.3), channel_id=1, source_target_pairs={{0,2},{1,3},{2,0},{3,1},{4,6},{5,7},{6,4},{7,5},{8,10},{9,11},{10,... | collective-permute-start | bytes 442376 | tf_op jit(solution)/shard_map/ppermute | solution.py:360

commit v9 on v8

--- a/solution.py
+++ b/solution.py
@@ -180,15 +180,17 @@
     group = 16
 
     def cross(k):
-        for i in range(count):
-            for g in range(0, PAIRS, group):
-                first_at = pl.ds(pl.multiple_of(firsts[i] * PAIRS + g, group), group)
-                second_at = pl.ds(pl.multiple_of(seconds[i] * PAIRS + g, group), group)
-                first = kept_ref[k, first_at, :].astype(jnp.float32)
-                second = second_rows_ref[k, second_at, :].astype(jnp.float32)
-                ar, ai = first[:, :BINS], first[:, BINS:]
-                br, bi = second[:, :BINS], second[:, BINS:]
-                at = pl.ds(g, group)
+        for g in range(0, PAIRS, group):
+            def load(ref, index):
+                at = pl.ds(pl.multiple_of(index * PAIRS + g, group), group)
+                return ref[k, at, :].astype(jnp.float32)
+
+            first_of = {i: load(kept_ref, firsts[i]) for i in (0, 2, 4)}
+            second_of = {i: load(second_rows_ref, seconds[i]) for i in (0, 1, 2)}
+            at = pl.ds(g, group)
+            for i, (f, s) in enumerate(((0, 0), (0, 1), (2, 2), (4, 0), (4, 1))):
+                ar, ai = first_of[f][:, :BINS], first_of[f][:, BINS:]
+                br, bi = second_of[s][:, :BINS], second_of[s][:, BINS:]
                 cross_ref[i, at, pl.ds(k * BINS, BINS)] = (ar * br + ai * bi).astype(jnp.bfloat16)
                 cross_ref[i, at, pl.ds(NB + k * BINS, BINS)] = (ar * bi - ai * br).astype(jnp.bfloat16)
 

time: 57.2 us -> 56.5 us (0.988)
  Pallas kernels: 12.3 us -> 11.5 us
  waiting for transfers between devices: 4.88 us -> 5.62 us
  blocking collectives: 20 us -> 19.3 us
    ppermute x7, waiting for transfers between devices: 4.87 us -> 5.61 us  [exchanged(): lax.ppermute(part, 'hour', [(h, h ^ distance) for h in range(hours)])]
    all_to_all x1, blocking collectives: 20 us -> 19.3 us  [shards(): lax.all_to_all(outgoing, 'sens', split_axis=0, concat_axis=0, tiled=True)]
  transfers between devices with their start and end apart: 10 -> 10, of which waited for: 3 -> 3; matrix products, arithmetic and copies ran while one was open for 0% -> 0% of each run, Pallas kernels for 13% -> 12%
where the time goes in v9:
time: 56.5 us; the launch traced here: 56.3 us
  blocking collectives  19.3 us (34%)
  starting transfers between devices  18.8 us (33%)
  Pallas kernels  11.5 us (20%)
  waiting for transfers between devices  5.62 us (10%)
  local copies, waits for them, and re-layouts  0.96 us (2%)
    all_to_all x1, blocking collectives, shards(): lax.all_to_all(outgoing, 'sens', split_axis=0, concat_axis=0, tiled=True)  19.3 us
    ppermute x7, starting transfers between devices, exchanged(): lax.ppermute(part, 'hour', [(h, h ^ distance) for h in range(hours)])  9.9 us
    ppermute x1, starting transfers between devices, shards(): lax.ppermute(rows, 'sens', [(s, (s - 2) % sens) for s in range(sens)])  7.33 us
    ppermute x7, waiting for transfers between devices, exchanged(): lax.ppermute(part, 'hour', [(h, h ^ distance) for h in range(hours)])  5.61 us
    pallas_call x1, Pallas kernels, shards(): pl.pallas_call(own_kernel, out_shape=(pltpu.VMEM((RES + 1, PICKED + SLAB,...  3.81 us
    pallas_call x1, Pallas kernels, shards(): pl.pallas_call(functools.partial(across_kernel, other), out_shape=(one,)...  3.2 us
    pallas_call x2, Pallas kernels, whitened(): pl.pallas_call(kernel, out_shape=spectra, in_specs=in_specs, out_specs=vm...  2.16 us
    pallas_call x1, Pallas kernels, shards(): pl.pallas_call(functools.partial(along_kernel, same), out_shape=(one,) *...  1.99 us
  transfers between devices with their start and end apart: 10, of which 3 were waited for; matrix products, arithmetic and copies ran while one was open for 0% of the time, Pallas kernels for 12%

profile of v9, /device:TPU:1, one launch (start us, length us, event | category | flops | bytes accessed | tf_op | source)
XLA Modules:
  0.0 56.3 jit_solution(15653848608784404082)
XLA Ops:
  0.0 7.3 %collective-permute-start = (bf16[24,4096]{1,0:T(8,128)(2,1)}, bf16[24,4096]{1,0:T(8,128)(2,1)S(1)}, u32[]{:S(2)}, u32[]{:S(2)}) collective-permute-start(bf16[24,4096]{1,0:T(8,128)(2,1)} %bitcast.8), channel_id=1, source_target_pairs={{0,240},{8,248},{16,0},{24,8},{32,16},{40,24},{48,32},{56,40},{64,... | collective-permute-start | bytes 589832 | tf_op jit(solution)/shard_map/ppermute | solution.py:284
  7.3 1.0 %collective-permute-start.1 = (bf16[24,4096]{1,0:T(8,128)(2,1)}, bf16[24,4096]{1,0:T(8,128)(2,1)S(1)}, u32[]{:S(2)}, u32[]{:S(2)}) collective-permute-start(bf16[24,4096]{1,0:T(8,128)(2,1)} %bitcast.9), channel_id=1, source_target_pairs={{0,8},{8,0},{16,24},{24,16},{32,40},{40,32},{48,56},{56,48},{64,72... | collective-permute-start | bytes 589832 | tf_op jit(solution)/shard_map/ppermute | solution.py:285
  8.3 3.8 %own.1 = (bf16[17,224,256]{2,1,0:T(8,128)(2,1)S(1)}, bf16[128,64]{1,0:T(8,128)(2,1)S(1)}) custom-call(bf16[24,4096]{1,0:T(8,128)(2,1)} %bitcast.10, f32[2,16,512]{2,1,0:T(8,128)} %constant.10.clone.twiddle_any.twiddle_ref, bf16[2,1024,256]{2,1,0:T(8,128)(2,1)} %constant.11.clone.common_any.common_ref, s32[1,64]{1,0:T(1,128)} %bitcast.11, s32[1,64]{1,0:T(1,128)} %bitcast.12, ...), custom_call_target="tpu_custom_call" | custom-call | flops 10000000000 | bytes 1000000 | tf_op jit(solution)/shard_map/own/pallas_call | solution.py:297
  12.1 0.0 collective-permute-done.rows_ref
  12.1 0.0 copy-start
  12.1 0.0 copy-start.1
  12.1 0.0 copy-start.4
  12.2 0.6 %collective-permute-start.2 = (bf16[24,4096]{1,0:T(8,128)(2,1)S(1)}, bf16[24,4096]{1,0:T(8,128)(2,1)S(1)}, u32[]{:S(2)}, u32[]{:S(2)}) collective-permute-start(bf16[24,4096]{1,0:T(8,128)(2,1)S(1)} %collective-permute-done.rows_ref), channel_id=1, source_target_pairs={{0,8},{8,0},{16,24},{24,16},{32,40},{40,32},{48,56},{56,48},{64,72... | collective-permute-start | bytes 589832 | tf_op jit(solution)/shard_map/ppermute | solution.py:320
  12.8 1.1 %farther.1.far_ref = bf16[16,32,256]{2,1,0:T(8,128)(2,1)S(1)} custom-call(bf16[24,4096]{1,0:T(8,128)(2,1)S(1)} %collective-permute-done.rows_ref, f32[2,16,512]{2,1,0:T(8,128)S(1)} %copy-done.3, bf16[2,1024,256]{2,1,0:T(8,128)(2,1)S(1)} %copy-done.2), custom_call_target="tpu_custom_call" | custom-call | flops 700000000 | bytes 1000000 | tf_op jit(solution)/shard_map/farther/pallas_call | solution.py:323
  13.9 0.0 collective-permute-done.2.passed_ref
  13.9 1.1 %nearer.1.near_ref = bf16[16,32,256]{2,1,0:T(8,128)(2,1)S(1)} custom-call(bf16[24,4096]{1,0:T(8,128)(2,1)S(1)} %collective-permute-done.1.sibling_ref, bf16[24,4096]{1,0:T(8,128)(2,1)S(1)} %collective-permute-done.2.passed_ref, f32[2,16,512]{2,1,0:T(8,128)S(1)} %copy-done.3, bf16[2,1024,256]{2,1,0:T(8,128)(2,1)S(1)} %copy-done.2), custom_call_target="tpu_custom_call" | custom-call | flops 700000000 | bytes 1000000 | tf_op jit(solution)/shard_map/nearer/pallas_call | solution.py:323
  15.0 3.2 %across.1 = (bf16[64,1152]{1,0:T(8,128)(2,1)S(1)}, bf16[64,1152]{1,0:T(8,128)(2,1)S(1)}, bf16[64,1152]{1,0:T(8,128)(2,1)S(1)}, bf16[64,1152]{1,0:T(8,128)(2,1)S(1)}, bf16[16,192,256]{2,1,0:T(8,128)(2,1)S(1)}) custom-call(bf16[17,224,256]{2,1,0:T(8,128)(2,1)S(1)} %get-tuple-element.20.kept_ref, bf16[16,32,256]{2,1,0:T(8,128)(2,1)S(1)} %nearer.1.near_ref, ...), custom_call_target="tpu_custom_call" | custom-call | flops 3000000000 | bytes 1000000 | tf_op jit(solution)/shard_map/across/pallas_call | solution.py:341
  18.2 2.8 %collective-permute-start.3 = (bf16[64,1152]{1,0:T(8,128)(2,1)S(1)}, bf16[64,1152]{1,0:T(8,128)(2,1)S(1)}, u32[]{:S(2)}, u32[]{:S(2)}) collective-permute-start(bf16[64,1152]{1,0:T(8,128)(2,1)S(1)} %get-tuple-element.22), channel_id=1, source_target_pairs={{0,3},{1,2},{2,1},{3,0},{4,7},{5,6},{6,5},{7,4},{8,11},{9,10},{10,... | collective-permute-start | bytes 442376 | tf_op jit(solution)/shard_map/ppermute | solution.py:362
  21.0 0.0 collective-permute-start.4
  21.0 2.4 %collective-permute-start.8 = (bf16[64,1152]{1,0:T(8,128)(2,1)S(1)}, bf16[64,1152]{1,0:T(8,128)(2,1)S(1)}, u32[]{:S(2)}, u32[]{:S(2)}) collective-permute-start(bf16[64,1152]{1,0:T(8,128)(2,1)S(1)} %get-tuple-element.29), channel_id=1, source_target_pairs={{0,4},{1,5},{2,6},{3,7},{4,0},{5,1},{6,2},{7,3},{8,12},{9,13},{10,... | collective-permute-start | bytes 442376 | tf_op jit(solution)/shard_map/ppermute | solution.py:362
  23.5 2.0 %along.1 = (bf16[64,1152]{1,0:T(8,128)(2,1)S(1)}, bf16[64,1152]{1,0:T(8,128)(2,1)S(1)}, bf16[64,1152]{1,0:T(8,128)(2,1)S(1)}, bf16[64,1152]{1,0:T(8,128)(2,1)S(1)}) custom-call(bf16[17,224,256]{2,1,0:T(8,128)(2,1)S(1)} %get-tuple-element.20.kept_ref, bf16[16,192,256]{2,1,0:T(8,128)(2,1)S(1)} %get-tuple-element.25.second_rows_ref, ...), custom_call_target="tpu_custom_call" | custom-call | flops 3000000000 | bytes 1000000 | tf_op jit(solution)/shard_map/along/pallas_call | solution.py:351
  25.5 0.7 %collective-permute-start.6 = (bf16[64,1152]{1,0:T(8,128)(2,1)S(1)}, bf16[64,1152]{1,0:T(8,128)(2,1)S(1)}, u32[]{:S(2)}, u32[]{:S(2)}) collective-permute-start(bf16[64,1152]{1,0:T(8,128)(2,1)S(1)} %get-tuple-element.26), channel_id=1, source_target_pairs={{0,3},{1,2},{2,1},{3,0},{4,7},{5,6},{6,5},{7,4},{8,11},{9,10},{10,... | collective-permute-start | bytes 442376 | tf_op jit(solution)/shard_map/ppermute | solution.py:362
  26.2 0.9 %collective-permute-start.7 = (bf16[64,1152]{1,0:T(8,128)(2,1)S(1)}, bf16[64,1152]{1,0:T(8,128)(2,1)S(1)}, u32[]{:S(2)}, u32[]{:S(2)}) collective-permute-start(bf16[64,1152]{1,0:T(8,128)(2,1)S(1)} %get-tuple-element.27), channel_id=1, source_target_pairs={{0,1},{1,0},{2,3},{3,2},{4,5},{5,4},{6,7},{7,6},{8,9},{9,8},{10,11... | collective-permute-start | bytes 442376 | tf_op jit(solution)/shard_map/ppermute | solution.py:362
  27.1 0.0 collective-permute-done.3.refs_0_
  27.1 0.0 collective-permute-done.4.refs_1_
  27.1 0.1 fold.2
  27.2 1.2 %collective-permute-start.5 = (bf16[64,1152]{1,0:T(8,128)(2,1)S(1)}, bf16[64,1152]{1,0:T(8,128)(2,1)S(1)}, u32[]{:S(2)}, u32[]{:S(2)}) collective-permute-start(bf16[64,1152]{1,0:T(8,128)(2,1)S(1)} %fold.2), channel_id=1, source_target_pairs={{0,4},{1,5},{2,6},{3,7},{4,0},{5,1},{6,2},{7,3},{8,12},{9,13},{10,... | collective-permute-start | bytes 442376 | tf_op jit(solution)/shard_map/ppermute | solution.py:362
  28.4 0.0 collective-permute-done.8.refs_1_
  28.5 1.8 %collective-permute-start.9 = (bf16[64,1152]{1,0:T(8,128)(2,1)S(1)}, bf16[64,1152]{1,0:T(8,128)(2,1)S(1)}, u32[]{:S(2)}, u32[]{:S(2)}) collective-permute-start(bf16[64,1152]{1,0:T(8,128)(2,1)S(1)} %fold.3), channel_id=1, source_target_pairs={{0,2},{1,3},{2,0},{3,1},{4,6},{5,7},{6,4},{7,5},{8,10},{9,11},{10,... | collective-permute-start | bytes 442376 | tf_op jit(solution)/shard_map/ppermute | solution.py:362
  30.2 0.9 %collective-permute-done.6.refs_1_ = bf16[64,1152]{1,0:T(8,128)(2,1)S(1)} collective-permute-done((bf16[64,1152]{1,0:T(8,128)(2,1)S(1)}, bf16[64,1152]{1,0:T(8,128)(2,1)S(1)}, u32[]{:S(2)}, u32[]{:S(2)}) %collective-permute-start.6) | collective-permute-done | bytes 147488 | tf_op jit(solution)/shard_map/ppermute | solution.py:362
  31.1 0.0 collective-permute-done.7.refs_2_
  31.1 1.7 %collective-permute-done.5.refs_0_ = bf16[64,1152]{1,0:T(8,128)(2,1)S(1)} collective-permute-done((bf16[64,1152]{1,0:T(8,128)(2,1)S(1)}, bf16[64,1152]{1,0:T(8,128)(2,1)S(1)}, u32[]{:S(2)}, u32[]{:S(2)}) %collective-permute-start.5) | collective-permute-done | bytes 147488 | tf_op jit(solution)/shard_map/ppermute | solution.py:362
  32.8 3.1 %collective-permute-done.9.refs_3_ = bf16[64,1152]{1,0:T(8,128)(2,1)S(1)} collective-permute-done((bf16[64,1152]{1,0:T(8,128)(2,1)S(1)}, bf16[64,1152]{1,0:T(8,128)(2,1)S(1)}, u32[]{:S(2)}, u32[]{:S(2)}) %collective-permute-start.9) | collective-permute-done | bytes 147488 | tf_op jit(solution)/shard_map/ppermute | solution.py:362
  35.8 0.3 collect.1
  36.1 0.1 all_to_all.6
  36.2 19.3 %all_to_all.9 = bf16[32,4,1152]{2,1,0:T(4,128)(2,1)S(1)} all-to-all(bf16[32,4,1152]{2,1,0:T(4,128)(2,1)S(1)} %all_to_all.6), channel_id=1, replica_groups=mesh['sens'=32,'hour'=8] {'sens'}, dimensions={0} | all-to-all | bytes 589824 | tf_op jit(solution)/shard_map/all_to_all | solution.py:395
  55.5 0.9 %reshape.20 = f32[128,1152]{1,0:T(8,128)} reshape(bf16[32,4,1152]{2,1,0:T(4,128)(2,1)S(1)} %all_to_all.9) | data formatting | bytes 884736 | tf_op jit(solution)/shard_map/convert_element_type | solution.py:396
  (9 shorter events, 0.1 us)
Async XLA Ops:
  0.0 12.1 %collective-permute-start = (bf16[24,4096]{1,0:T(8,128)(2,1)}, bf16[24,4096]{1,0:T(8,128)(2,1)S(1)}, u32[]{:S(2)}, u32[]{:S(2)}) collective-permute-start(bf16[24,4096]{1,0:T(8,128)(2,1)} %bitcast.8), channel_id=1, source_target_pairs={{0,240},{8,248},{16,0},{24,8},{32,16},{40,24},{48,32},{56,40},{64,... | collective-permute-start | bytes 589832 | tf_op jit(solution)/shard_map/ppermute | solution.py:284
  7.3 6.5 %collective-permute-start.1 = (bf16[24,4096]{1,0:T(8,128)(2,1)}, bf16[24,4096]{1,0:T(8,128)(2,1)S(1)}, u32[]{:S(2)}, u32[]{:S(2)}) collective-permute-start(bf16[24,4096]{1,0:T(8,128)(2,1)} %bitcast.9), channel_id=1, source_target_pairs={{0,8},{8,0},{16,24},{24,16},{32,40},{40,32},{48,56},{56,48},{64,72... | collective-permute-start | bytes 589832 | tf_op jit(solution)/shard_map/ppermute | solution.py:285
  8.3 4.5 %copy-start.2 = (bf16[2,1024,256]{2,1,0:T(8,128)(2,1)S(1)}, bf16[2,1024,256]{2,1,0:T(8,128)(2,1)}, u32[]{:S(2)}) copy-start(bf16[2,1024,256]{2,1,0:T(8,128)(2,1)} %constant.11.clone.common_any.common_ref) | copy-start | bytes 3145732
  8.3 4.5 %copy-start.3 = (f32[2,16,512]{2,1,0:T(8,128)S(1)}, f32[2,16,512]{2,1,0:T(8,128)}, u32[]{:S(2)}) copy-start(f32[2,16,512]{2,1,0:T(8,128)} %constant.10.clone.twiddle_any.twiddle_ref) | copy-start | bytes 196612
  12.1 2.9 %copy-start = (bf16[2048,512]{1,0:T(8,128)(2,1)S(1)}, bf16[2048,512]{1,0:T(8,128)(2,1)}, u32[]{:S(2)}) copy-start(bf16[2048,512]{1,0:T(8,128)(2,1)} %constant.12.clone.cosines_ref) | copy-start | bytes 6291460
  12.1 2.9 %copy-start.1 = (bf16[2048,512]{1,0:T(8,128)(2,1)S(1)}, bf16[2048,512]{1,0:T(8,128)(2,1)}, u32[]{:S(2)}) copy-start(bf16[2048,512]{1,0:T(8,128)(2,1)} %constant.13.clone.sines_ref) | copy-start | bytes 6291460
  12.1 2.9 %copy-start.4 = (bf16[128,128]{1,0:T(8,128)(2,1)S(1)}, bf16[128,128]{1,0:T(8,128)(2,1)}, u32[]{:S(2)}) copy-start(bf16[128,128]{1,0:T(8,128)(2,1)} %constant.14.clone.flip_ref) | copy-start | bytes 98308
  12.2 1.7 %collective-permute-start.2 = (bf16[24,4096]{1,0:T(8,128)(2,1)S(1)}, bf16[24,4096]{1,0:T(8,128)(2,1)S(1)}, u32[]{:S(2)}, u32[]{:S(2)}) collective-permute-start(bf16[24,4096]{1,0:T(8,128)(2,1)S(1)} %collective-permute-done.rows_ref), channel_id=1, source_target_pairs={{0,8},{8,0},{16,24},{24,16},{32,40},{40,32},{48,56},{56,48},{64,72... | collective-permute-start | bytes 589832 | tf_op jit(solution)/shard_map/ppermute | solution.py:320
  18.2 8.9 %collective-permute-start.3 = (bf16[64,1152]{1,0:T(8,128)(2,1)S(1)}, bf16[64,1152]{1,0:T(8,128)(2,1)S(1)}, u32[]{:S(2)}, u32[]{:S(2)}) collective-permute-start(bf16[64,1152]{1,0:T(8,128)(2,1)S(1)} %get-tuple-element.22), channel_id=1, source_target_pairs={{0,3},{1,2},{2,1},{3,0},{4,7},{5,6},{6,5},{7,4},{8,11},{9,10},{10,... | collective-permute-start | bytes 442376 | tf_op jit(solution)/shard_map/ppermute | solution.py:362
  21.0 6.1 %collective-permute-start.4 = (bf16[64,1152]{1,0:T(8,128)(2,1)S(1)}, bf16[64,1152]{1,0:T(8,128)(2,1)S(1)}, u32[]{:S(2)}, u32[]{:S(2)}) collective-permute-start(bf16[64,1152]{1,0:T(8,128)(2,1)S(1)} %get-tuple-element.23), channel_id=1, source_target_pairs={{0,1},{1,0},{2,3},{3,2},{4,5},{5,4},{6,7},{7,6},{8,9},{9,8},{10,11... | collective-permute-start | bytes 442376 | tf_op jit(solution)/shard_map/ppermute | solution.py:362
  21.0 7.4 %collective-permute-start.8 = (bf16[64,1152]{1,0:T(8,128)(2,1)S(1)}, bf16[64,1152]{1,0:T(8,128)(2,1)S(1)}, u32[]{:S(2)}, u32[]{:S(2)}) collective-permute-start(bf16[64,1152]{1,0:T(8,128)(2,1)S(1)} %get-tuple-element.29), channel_id=1, source_target_pairs={{0,4},{1,5},{2,6},{3,7},{4,0},{5,1},{6,2},{7,3},{8,12},{9,13},{10,... | collective-permute-start | bytes 442376 | tf_op jit(solution)/shard_map/ppermute | solution.py:362
  25.5 5.6 %collective-permute-start.6 = (bf16[64,1152]{1,0:T(8,128)(2,1)S(1)}, bf16[64,1152]{1,0:T(8,128)(2,1)S(1)}, u32[]{:S(2)}, u32[]{:S(2)}) collective-permute-start(bf16[64,1152]{1,0:T(8,128)(2,1)S(1)} %get-tuple-element.26), channel_id=1, source_target_pairs={{0,3},{1,2},{2,1},{3,0},{4,7},{5,6},{6,5},{7,4},{8,11},{9,10},{10,... | collective-permute-start | bytes 442376 | tf_op jit(solution)/shard_map/ppermute | solution.py:362
  26.2 4.9 %collective-permute-start.7 = (bf16[64,1152]{1,0:T(8,128)(2,1)S(1)}, bf16[64,1152]{1,0:T(8,128)(2,1)S(1)}, u32[]{:S(2)}, u32[]{:S(2)}) collective-permute-start(bf16[64,1152]{1,0:T(8,128)(2,1)S(1)} %get-tuple-element.27), channel_id=1, source_target_pairs={{0,1},{1,0},{2,3},{3,2},{4,5},{5,4},{6,7},{7,6},{8,9},{9,8},{10,11... | collective-permute-start | bytes 442376 | tf_op jit(solution)/shard_map/ppermute | solution.py:362
  27.2 5.6 %collective-permute-start.5 = (bf16[64,1152]{1,0:T(8,128)(2,1)S(1)}, bf16[64,1152]{1,0:T(8,128)(2,1)S(1)}, u32[]{:S(2)}, u32[]{:S(2)}) collective-permute-start(bf16[64,1152]{1,0:T(8,128)(2,1)S(1)} %fold.2), channel_id=1, source_target_pairs={{0,4},{1,5},{2,6},{3,7},{4,0},{5,1},{6,2},{7,3},{8,12},{9,13},{10,... | collective-permute-start | bytes 442376 | tf_op jit(solution)/shard_map/ppermute | solution.py:362
  28.5 7.4 %collective-permute-start.9 = (bf16[64,1152]{1,0:T(8,128)(2,1)S(1)}, bf16[64,1152]{1,0:T(8,128)(2,1)S(1)}, u32[]{:S(2)}, u32[]{:S(2)}) collective-permute-start(bf16[64,1152]{1,0:T(8,128)(2,1)S(1)} %fold.3), channel_id=1, source_target_pairs={{0,2},{1,3},{2,0},{3,1},{4,6},{5,7},{6,4},{7,5},{8,10},{9,11},{10,... | collective-permute-start | bytes 442376 | tf_op jit(solution)/shard_map/ppermute | solution.py:362
